TPU v7x, 32 devices: a whole 2x2x4 slice. The times are simulated.
32 devices in a mesh: fsdp: 2 (over core), context: 4 (over y, x), tensor: 4 (over z).
Axes of the slice: x: 2, y: 2, z: 4, core: 2. Of those that a mesh axis runs over, the one named last changes fastest.
Arguments:
- tokens: bfloat16 [8192, 1024], P(('fsdp', 'context')), may hold values from -6 to 6
- encoder: bfloat16 [16384, 1024], P(('fsdp', 'context')), may hold values from -6 to 6
- cotangent: bfloat16 [8192, 1024], P(('fsdp', 'context')), may hold values from -6 to 6
- lengths: int32 [2, 2], P('fsdp'), may hold values from 1024 to 3072, as said below
- order: int32 [2, 4096], P('fsdp'), may hold values from 0 to 4095, as said below
- in_proj: float32 [6, 1024, 1024], P(None, ('fsdp', 'context'), 'tensor'), may hold values from -0.5625 to 0.5625
- out_proj: float32 [2, 1024, 1024], P(None, 'tensor', ('fsdp', 'context')), may hold values from -1.5 to 1.5
- w_up: float32 [1024, 4096], P(('fsdp', 'context'), 'tensor'), may hold values from -0.1875 to 0.1875
- w_down: float32 [4096, 1024], P('tensor', ('fsdp', 'context')), may hold values from -0.09375 to 0.09375
- head_bias: float32 [4, 128, 8], P(None, 'tensor', ('fsdp', 'context')), may hold values from -4 to 4
- up_bias: float32 [512, 8], P('tensor', ('fsdp', 'context')), may hold values from -4 to 4
- vectors: float32 [9, 1024], P(None, ('fsdp', 'context')), may hold values from -2 to 2
- in_first: float32 [6, 1024, 1024], P(None, ('fsdp', 'context'), 'tensor'), may hold values from -256 to 256
- out_first: float32 [2, 1024, 1024], P(None, 'tensor', ('fsdp', 'context')), may hold values from -80 to 80
- up_first: float32 [1024, 4096], P(('fsdp', 'context'), 'tensor'), may hold values from -224 to 224
- down_first: float32 [4096, 1024], P('tensor', ('fsdp', 'context')), may hold values from -256 to 256
- hbias_first: float32 [4, 128, 8], P(None, 'tensor', ('fsdp', 'context')), may hold values from -512 to 512
- ubias_first: float32 [512, 8], P('tensor', ('fsdp', 'context')), may hold values from -224 to 224
- vec_first: float32 [9, 1024], P(None, ('fsdp', 'context')), may hold values from -384 to 384
- in_second: float32 [6, 1024, 1024], P(None, ('fsdp', 'context'), 'tensor'), may hold values from 1024 to 8192
- out_second: float32 [2, 1024, 1024], P(None, 'tensor', ('fsdp', 'context')), may hold values from 92.16 to 737.28
- up_second: float32 [1024, 4096], P(('fsdp', 'context'), 'tensor'), may hold values from 655.36 to 5242.88
- down_second: float32 [4096, 1024], P('tensor', ('fsdp', 'context')), may hold values from 1024 to 8192
- hbias_second: float32 [4, 128, 8], P(None, 'tensor', ('fsdp', 'context')), may hold values from 4096 to 32768
- ubias_second: float32 [512, 8], P('tensor', ('fsdp', 'context')), may hold values from 655.36 to 5242.88
- vec_second: float32 [9, 1024], P(None, ('fsdp', 'context')), may hold values from 2007.04 to 16056.32
Outputs:
- out: float32 [8192, 1024], P(('fsdp', 'context'))
- grad_tokens: float32 [8192, 1024], P(('fsdp', 'context'), 'tensor')
- grad_encoder: float32 [16384, 1024], P(('fsdp', 'context'), 'tensor')
- clip_factors: float32 [16], P('tensor')
- in_proj_new: float32 [6, 1024, 1024], P(None, ('fsdp', 'context'), 'tensor')
- in_first_new: float32 [6, 1024, 1024], P(None, ('fsdp', 'context'), 'tensor')
- in_second_new: float32 [6, 1024, 1024], P(None, ('fsdp', 'context'), 'tensor')
- in_proj_copy: bfloat16 [6, 1024, 1024], P(None, ('fsdp', 'context'), 'tensor')
- out_proj_new: float32 [2, 1024, 1024], P(None, 'tensor', ('fsdp', 'context'))
- out_first_new: float32 [2, 1024, 1024], P(None, 'tensor', ('fsdp', 'context'))
- out_second_new: float32 [2, 1024, 1024], P(None, 'tensor', ('fsdp', 'context'))
- out_proj_copy: bfloat16 [2, 1024, 1024], P(None, 'tensor', ('fsdp', 'context'))
- w_up_new: float32 [1024, 4096], P(('fsdp', 'context'), 'tensor')
- up_first_new: float32 [1024, 4096], P(('fsdp', 'context'), 'tensor')
- up_second_new: float32 [1024, 4096], P(('fsdp', 'context'), 'tensor')
- w_up_copy: bfloat16 [1024, 4096], P(('fsdp', 'context'), 'tensor')
- w_down_new: float32 [4096, 1024], P('tensor', ('fsdp', 'context'))
- down_first_new: float32 [4096, 1024], P('tensor', ('fsdp', 'context'))
- down_second_new: float32 [4096, 1024], P('tensor', ('fsdp', 'context'))
- w_down_copy: bfloat16 [4096, 1024], P('tensor', ('fsdp', 'context'))
- head_bias_new: float32 [4, 128, 8], P(None, 'tensor', ('fsdp', 'context'))
- hbias_first_new: float32 [4, 128, 8], P(None, 'tensor', ('fsdp', 'context'))
- hbias_second_new: float32 [4, 128, 8], P(None, 'tensor', ('fsdp', 'context'))
- head_bias_copy: bfloat16 [4, 128, 8], P(None, 'tensor', ('fsdp', 'context'))
- up_bias_new: float32 [512, 8], P('tensor', ('fsdp', 'context'))
- ubias_first_new: float32 [512, 8], P('tensor', ('fsdp', 'context'))
- ubias_second_new: float32 [512, 8], P('tensor', ('fsdp', 'context'))
- up_bias_copy: bfloat16 [512, 8], P('tensor', ('fsdp', 'context'))
- vectors_new: float32 [9, 1024], P(None, ('fsdp', 'context'))
- vec_first_new: float32 [9, 1024], P(None, ('fsdp', 'context'))
- vec_second_new: float32 [9, 1024], P(None, ('fsdp', 'context'))
- vectors_copy: bfloat16 [9, 1024], P(None, ('fsdp', 'context'))
Inputs may be any that keep to these rules, and one draw needn't show every extreme that they name: Each pack holds 2 sequences, in order, whose lengths sum to 4096. `order`: each row is a permutation of its pack's positions that deals rounds of 4 blocks of 128 positions: dealt row d * 1024 + r * 128 + k holds position (r * 4 + b) * 128 + k, where b runs over all blocks of round r as d runs over 0 to 3.
All inputs are finite; a program needn't handle non-finite values.
Results may differ from a plain program's by a relative error of at most 0.029.
Values may be sent and summed in bfloat16 or wider, within the bound.
No kernel may reach another device: no remote copies, remote signals or barrier semaphores. Data moves between devices by JAX's collectives and lax.ppermute only.
A program may use at most 256 MiB of HBM per device.

v0:
```python
from functools import partial, reduce

import jax
import jax.numpy as jnp
from jax import lax
from jax.experimental import pallas as pl
from jax.experimental.pallas import tpu as pltpu
from jax.sharding import PartitionSpec as P

HEAD = 64
ENC = 4096
STEP = 10
BLK = 128

NEGATIVE = -1e30
NORM_EPS = 1e-05
ADAM_EPS = 1e-08
BETA = 0.5
CLIP_LIMIT = 10.0
RATES = (0.05, 0.3, 0.05, 0.03, 0.3, 0.3, 0.3)
DECAYS = (0.1, 0.1, 0.1, 0.1, 0.0, 0.0, 0.0)
SCALE = HEAD ** (-0.5)
VMEM_BYTES = 56 * 1024 * 1024
F, C, T = "fsdp", "context", "tensor"
SHARD = (F, C)
NO_COST = pl.CostEstimate(flops=0, bytes_accessed=0, transcendentals=0)


def product(left_side, right_side):
    return jnp.dot(left_side, right_side, preferred_element_type=jnp.float32)


def contract_rows(left_side, right_side):
    return lax.dot_general(
        left_side, right_side, (((0,), (0,)), ((), ())), preferred_element_type=jnp.float32
    )


def contract_cols(left_side, right_side):
    return lax.dot_general(
        left_side, right_side, (((1,), (1,)), ((), ())), preferred_element_type=jnp.float32
    )


def stack_heads(block, heads):
    lanes = lax.broadcasted_iota(jnp.int32, block.shape, 1) // HEAD
    zero = jnp.zeros_like(block)
    return jnp.concatenate([jnp.where(lanes == h, block, zero) for h in range(heads)], axis=0)


def merge_heads(stacked, heads):
    rows = stacked.shape[0] // heads
    lanes = lax.broadcasted_iota(jnp.int32, (rows, stacked.shape[1]), 1) // HEAD
    merged = stacked[:rows]
    for h in range(1, heads):
        merged = jnp.where(lanes == h, stacked[h * rows : (h + 1) * rows], merged)
    return merged


def col_to_row(column):
    return jnp.transpose(jnp.broadcast_to(column, (column.shape[0], 128)))[0:1]


def fold_lanes(tile, combine):
    return reduce(combine, [tile[:, j : j + 128] for j in range(0, tile.shape[1], 128)])


def whole(shape):
    return pl.BlockSpec(shape, lambda i, s: (0,) * len(shape), pipeline_mode=pl.Buffered(1))


def fetch_kv(sources, places, sems):
    copies = [
        pltpu.make_async_copy(source, place, sems.at[i])
        for i, (source, place) in enumerate(zip(sources, places))
    ]

    @pl.when(pl.program_id(0) == 0)
    def _():
        for copy in copies:
            copy.start()
        for copy in copies:
            copy.wait()


def piece_bounds(pieces):
    full, half = pieces[0].shape[0], pieces[3].shape[0]
    return [(0, 0, full), (1, 0, full), (2, 0, full), (3, 0, half), (3, half, half)]


def member_rows(order_ref, row, bounds, full):
    return [
        pl.ds(pl.multiple_of(order_ref[row, j] * full + start, size), size)
        for j, start, size in bounds
    ]


def gate_body(*refs):
    pass


def after(values, others):
    count, every = len(values), [*values, *others]
    return pl.pallas_call(
        gate_body,
        in_specs=[pl.BlockSpec(memory_space=pl.ANY)] * len(every),
        out_specs=[pl.BlockSpec(memory_space=pl.ANY)] * count,
        out_shape=[jax.ShapeDtypeStruct(value.shape, value.dtype) for value in values],
        input_output_aliases={i: i for i in range(count)},
        cost_estimate=NO_COST,
        name="gate",
    )(*every)


def cross_fwd_body(heads, bounds, seg_ref, q_ref, *refs):
    sources, (o_ref, lse_ref, kv_ref, s_ref, sems) = refs[: len(bounds)], refs[len(bounds) :]
    places = member_rows(seg_ref, 3, bounds, sources[0].shape[0])
    fetch_kv(sources, [kv_ref.at[place] for place in places], sems)
    block = pl.program_id(0)
    low, high, cut = seg_ref[0, block], seg_ref[1, block], seg_ref[2, block]
    queries = stack_heads(q_ref[...] * jnp.bfloat16(SCALE), heads)
    rows, width = queries.shape
    tiles, _, step = s_ref.shape

    def attend(sequence):
        def scores(t, highest):
            at = pl.ds(pl.multiple_of(sequence * ENC + t * step, step), step)
            tile = contract_cols(queries, kv_ref[at, :width])
            s_ref[t] = tile
            return jnp.maximum(highest, fold_lanes(tile, jnp.maximum))

        highest = lax.fori_loop(0, tiles, scores, jnp.full((rows, 128), NEGATIVE, jnp.float32))
        peak = jnp.max(highest, axis=1, keepdims=True)

        def weigh(t, running):
            total, summed = running
            at = pl.ds(pl.multiple_of(sequence * ENC + t * step, step), step)
            weights = jnp.exp(s_ref[t] - peak)
            summed = summed + product(weights.astype(jnp.bfloat16), kv_ref[at, width:])
            return total + fold_lanes(weights, jnp.add), summed

        total, summed = lax.fori_loop(
            0,
            tiles,
            weigh,
            (jnp.zeros((rows, 128), jnp.float32), jnp.zeros((rows, width), jnp.float32)),
        )
        total = jnp.sum(total, axis=1, keepdims=True)
        merged = merge_heads(summed / total, heads)
        lse = col_to_row(peak + jnp.log(total))
        place = lax.broadcasted_iota(jnp.int32, merged.shape, 0)
        own = jnp.where(place >= cut, 1, 0) == sequence
        o_ref[...] = jnp.where(own, merged, o_ref[...].astype(jnp.float32)).astype(o_ref.dtype)
        place = lax.broadcasted_iota(jnp.int32, lse.shape, 1) % BLK
        own = jnp.where(place >= cut, 1, 0) == sequence
        lse_ref[0] = jnp.where(own, lse, lse_ref[0])

    o_ref[...] = jnp.zeros_like(o_ref)
    lse_ref[...] = jnp.zeros_like(lse_ref)
    pl.loop(low, high + 1)(attend)


def cross_fwd(queries, enc_kv, seg):
    count, width = queries.shape
    heads, blocks, step = width // HEAD, count // BLK, 1024
    rows, bounds = heads * BLK, piece_bounds(enc_kv)
    enc_all = sum(piece.shape[0] for piece in enc_kv)
    return pl.pallas_call(
        partial(cross_fwd_body, heads, bounds),
        grid_spec=pltpu.PrefetchScalarGridSpec(
            num_scalar_prefetch=1,
            grid=(blocks,),
            in_specs=[pl.BlockSpec((BLK, width), lambda i, s: (i, 0))]
            + [pl.BlockSpec(memory_space=pl.ANY)] * len(bounds),
            out_specs=[
                pl.BlockSpec((BLK, width), lambda i, s: (i, 0)),
                pl.BlockSpec((1, 1, rows), lambda i, s: (i, 0, 0)),
            ],
            scratch_shapes=[
                pltpu.VMEM((enc_all, 2 * width), jnp.bfloat16),
                pltpu.VMEM((ENC // step, rows, step), jnp.float32),
                pltpu.SemaphoreType.DMA((len(bounds),)),
            ],
        ),
        out_shape=[
            jax.ShapeDtypeStruct((count, width), jnp.bfloat16),
            jax.ShapeDtypeStruct((blocks, 1, rows), jnp.float32),
        ],
        compiler_params=pltpu.CompilerParams(vmem_limit_bytes=VMEM_BYTES),
        cost_estimate=NO_COST,
        name="cross_fwd",
    )(seg, queries, *enc_kv)


def cross_bwd_body(heads, bounds, waits, step, seg_ref, q_ref, g_ref, o_ref, lse_ref, *refs):
    count = len(bounds)
    sources, (dq_ref, *outs) = refs[:count], refs[count + waits : 2 * count + waits + 1]
    kv_ref, acc_ref, sems = refs[2 * count + waits + 1 :]
    places = member_rows(seg_ref, 3, bounds, sources[0].shape[0])
    fetch_kv(sources, [kv_ref.at[place] for place in places], sems)
    block = pl.program_id(0)

    @pl.when(block == 0)
    def _():
        acc_ref[...] = jnp.zeros_like(acc_ref)

    low, high, cut = seg_ref[0, block], seg_ref[1, block], seg_ref[2, block]
    queries = stack_heads(q_ref[...] * jnp.bfloat16(SCALE), heads)
    rows, width = queries.shape
    grads = stack_heads(g_ref[...], heads)
    dots = g_ref[...].astype(jnp.float32) * o_ref[...].astype(jnp.float32)
    dot_row = col_to_row(jnp.sum(stack_heads(dots, heads), axis=1, keepdims=True))
    all_lse = lse_ref[0]
    place = lax.broadcasted_iota(jnp.int32, all_lse.shape, 1) % BLK
    own_seq = jnp.where(place >= cut, 1, 0)

    def sequence_terms(sequence, q_grad):
        lse = jnp.where(own_seq == sequence, all_lse, -NEGATIVE)

        def tile_terms(t, q_grad):
            at = pl.ds(pl.multiple_of(sequence * ENC + t * step, step), step)
            keys, values = kv_ref[at, :width], kv_ref[at, width:]
            probs = jnp.exp(contract_cols(keys, queries) - lse)
            s_grad = (probs * (contract_cols(values, grads) - dot_row)).astype(jnp.bfloat16)
            acc_ref[at, width:] += product(probs.astype(jnp.bfloat16), grads)
            acc_ref[at, :width] += product(s_grad, queries)
            return q_grad + contract_rows(s_grad, keys)

        return lax.fori_loop(0, ENC // step, tile_terms, q_grad)

    q_grad = lax.fori_loop(low, high + 1, sequence_terms, jnp.zeros((rows, width), jnp.float32))
    dq_ref[...] = (merge_heads(q_grad, heads) * SCALE).astype(dq_ref.dtype)

    @pl.when(block == pl.num_programs(0) - 1)
    def _():
        for out, place in zip(outs, places):
            out[...] = acc_ref[place, :].astype(out.dtype)


def cross_bwd(queries, enc_kv, seg, grads, context, lse, others):
    count, width = queries.shape
    heads, blocks, step = width // HEAD, count // BLK, 512
    rows, bounds = heads * BLK, piece_bounds(enc_kv)
    enc_all = sum(piece.shape[0] for piece in enc_kv)
    row = pl.BlockSpec((BLK, width), lambda i, s: (i, 0))
    return pl.pallas_call(
        partial(cross_bwd_body, heads, bounds, len(others), step),
        grid_spec=pltpu.PrefetchScalarGridSpec(
            num_scalar_prefetch=1,
            grid=(blocks,),
            in_specs=[row, row, row, pl.BlockSpec((1, 1, rows), lambda i, s: (i, 0, 0))]
            + [pl.BlockSpec(memory_space=pl.ANY)] * (len(bounds) + len(others)),
            out_specs=[row] + [whole(piece.shape) for piece in enc_kv],
            scratch_shapes=[
                pltpu.VMEM((enc_all, 2 * width), jnp.bfloat16),
                pltpu.VMEM((enc_all, 2 * width), jnp.float32),
                pltpu.SemaphoreType.DMA((len(bounds),)),
            ],
        ),
        out_shape=[jax.ShapeDtypeStruct((count, width), jnp.bfloat16)]
        + [jax.ShapeDtypeStruct(piece.shape, jnp.bfloat16) for piece in enc_kv],
        compiler_params=pltpu.CompilerParams(vmem_limit_bytes=VMEM_BYTES),
        cost_estimate=NO_COST,
        name="cross_bwd",
    )(seg, queries, grads, context, lse, *enc_kv, *others)


def gather_tile(kv_ref, t, columns):
    at = pl.ds(pl.multiple_of(t * BLK, BLK), BLK)
    return jnp.concatenate([kv_ref[j, at, columns] for j in range(kv_ref.shape[0])], axis=0)


def self_fwd_body(heads, bounds, meta_ref, q_ref, *refs):
    sources, (o_ref, lse_ref, top_ref, kv_refs, sems) = refs[: len(bounds)], refs[len(bounds) :]
    fetch_kv(sources, [kv_refs.at[j, pl.ds(at, size)] for j, at, size in bounds], sems)
    groups = kv_refs.shape[0]
    block = pl.program_id(0)
    base, first, last = [meta_ref[groups + k, block] for k in range(3)]
    cut = meta_ref[groups + 3, 0]
    queries = stack_heads(q_ref[...] * jnp.bfloat16(SCALE), heads)
    rows, width = queries.shape
    q_pos = base + lax.broadcasted_iota(jnp.int32, (rows, BLK), 0) % BLK
    q_start = jnp.where(q_pos >= cut, cut, 0)
    lane = lax.broadcasted_iota(jnp.int32, (rows, BLK), 1)

    def visit(t, running):
        peak, total, summed = running
        raw = contract_cols(queries, gather_tile(kv_refs, t, slice(0, width)))
        parts = []
        for d in range(groups):
            k_pos = lane + meta_ref[d, t]
            seen = (k_pos <= q_pos) & (k_pos >= q_start)
            parts.append(jnp.where(seen, raw[:, d * BLK : (d + 1) * BLK], NEGATIVE))
        new_peak = jnp.maximum(peak, jnp.max(reduce(jnp.maximum, parts), axis=1, keepdims=True))
        weights = [jnp.exp(part - new_peak) for part in parts]
        shrink = jnp.exp(peak - new_peak)
        total = total * shrink + jnp.sum(reduce(jnp.add, weights), axis=1, keepdims=True)
        low_weights = jnp.concatenate(weights, axis=1).astype(jnp.bfloat16)
        values = gather_tile(kv_refs, t, slice(width, 2 * width))
        return new_peak, total, summed * shrink + product(low_weights, values)

    peak, total, summed = lax.fori_loop(
        first,
        last + 1,
        visit,
        (
            jnp.full((rows, 1), NEGATIVE, jnp.float32),
            jnp.zeros((rows, 1), jnp.float32),
            jnp.zeros((rows, width), jnp.float32),
        ),
    )
    o_ref[...] = merge_heads(summed / total, heads).astype(o_ref.dtype)
    lse_ref[0] = col_to_row(peak + jnp.log(total))
    top_ref[0] = col_to_row(peak)


def self_fwd(queries, kv, meta):
    count, width = queries.shape
    heads, blocks, bounds = width // HEAD, count // BLK, piece_bounds(kv)
    rows, kept = heads * BLK, (bounds[-1][0] + 1,) + kv[0].shape
    row = pl.BlockSpec((BLK, width), lambda i, s: (i, 0))
    stat = pl.BlockSpec((1, 1, rows), lambda i, s: (i, 0, 0))
    return pl.pallas_call(
        partial(self_fwd_body, heads, bounds),
        grid_spec=pltpu.PrefetchScalarGridSpec(
            num_scalar_prefetch=1,
            grid=(blocks,),
            in_specs=[row] + [pl.BlockSpec(memory_space=pl.ANY)] * len(bounds),
            out_specs=[row, stat, stat],
            scratch_shapes=[
                pltpu.VMEM(kept, jnp.bfloat16),
                pltpu.SemaphoreType.DMA((len(bounds),)),
            ],
        ),
        out_shape=[jax.ShapeDtypeStruct((count, width), jnp.bfloat16)]
        + [jax.ShapeDtypeStruct((blocks, 1, rows), jnp.float32)] * 2,
        compiler_params=pltpu.CompilerParams(vmem_limit_bytes=VMEM_BYTES),
        cost_estimate=NO_COST,
        name="self_fwd",
    )(meta, queries, *kv)


def self_bwd_body(heads, bounds, waits, meta_ref, q_ref, g_ref, o_ref, lse_ref, *refs):
    count = len(bounds)
    sources, (dq_ref, *outs) = refs[:count], refs[count + waits : 2 * count + waits + 1]
    kv_refs, acc_ref, sems = refs[2 * count + waits + 1 :]
    fetch_kv(sources, [kv_refs.at[j, pl.ds(at, size)] for j, at, size in bounds], sems)
    groups = kv_refs.shape[0]
    block = pl.program_id(0)

    @pl.when(block == 0)
    def _():
        acc_ref[...] = jnp.zeros_like(acc_ref)

    base, first, last = [meta_ref[groups + k, block] for k in range(3)]
    cut = meta_ref[groups + 3, 0]
    queries = stack_heads(q_ref[...] * jnp.bfloat16(SCALE), heads)
    rows, width = queries.shape
    grads = stack_heads(g_ref[...], heads)
    dots = g_ref[...].astype(jnp.float32) * o_ref[...].astype(jnp.float32)
    dot_row = col_to_row(jnp.sum(stack_heads(dots, heads), axis=1, keepdims=True))
    lse = lse_ref[0]
    q_pos = base + lax.broadcasted_iota(jnp.int32, lse.shape, 1) % BLK
    q_start = jnp.where(q_pos >= cut, cut, 0)
    sub = lax.broadcasted_iota(jnp.int32, (BLK, rows), 0)

    def tile_terms(t, q_grad):
        at = pl.ds(pl.multiple_of(t * BLK, BLK), BLK)
        keys = gather_tile(kv_refs, t, slice(0, width))
        values = gather_tile(kv_refs, t, slice(width, 2 * width))
        raw = contract_cols(keys, queries)
        parts = []
        for d in range(groups):
            k_base = meta_ref[d, t]
            seen = (sub <= q_pos - k_base) & (sub >= q_start - k_base)
            parts.append(jnp.where(seen, jnp.exp(raw[d * BLK : (d + 1) * BLK] - lse), 0.0))
        probs = jnp.concatenate(parts, axis=0)
        s_grad = (probs * (contract_cols(values, grads) - dot_row)).astype(jnp.bfloat16)
        acc_ref[:, at, width:] += product(probs.astype(jnp.bfloat16), grads).reshape(
            groups, BLK, width
        )
        acc_ref[:, at, :width] += product(s_grad, queries).reshape(groups, BLK, width)
        return q_grad + contract_rows(s_grad, keys)

    q_grad = lax.fori_loop(first, last + 1, tile_terms, jnp.zeros((rows, width), jnp.float32))
    dq_ref[...] = (merge_heads(q_grad, heads) * SCALE).astype(dq_ref.dtype)

    @pl.when(block == pl.num_programs(0) - 1)
    def _():
        for out, (j, at, size) in zip(outs, bounds):
            out[...] = acc_ref[j, at : at + size].astype(out.dtype)


def self_bwd(queries, kv, meta, grads, context, lse, others):
    count, width = queries.shape
    heads, blocks, bounds = width // HEAD, count // BLK, piece_bounds(kv)
    rows, kept = heads * BLK, (bounds[-1][0] + 1,) + kv[0].shape
    row = pl.BlockSpec((BLK, width), lambda i, s: (i, 0))
    stat = pl.BlockSpec((1, 1, rows), lambda i, s: (i, 0, 0))
    return pl.pallas_call(
        partial(self_bwd_body, heads, bounds, len(others)),
        grid_spec=pltpu.PrefetchScalarGridSpec(
            num_scalar_prefetch=1,
            grid=(blocks,),
            in_specs=[row, row, row, stat]
            + [pl.BlockSpec(memory_space=pl.ANY)] * (len(bounds) + len(others)),
            out_specs=[row] + [whole(piece.shape) for piece in kv],
            scratch_shapes=[
                pltpu.VMEM(kept, jnp.bfloat16),
                pltpu.VMEM(kept, jnp.float32),
                pltpu.SemaphoreType.DMA((len(bounds),)),
            ],
        ),
        out_shape=[jax.ShapeDtypeStruct((count, width), jnp.bfloat16)]
        + [jax.ShapeDtypeStruct(piece.shape, jnp.bfloat16) for piece in kv],
        compiler_params=pltpu.CompilerParams(vmem_limit_bytes=VMEM_BYTES),
        cost_estimate=NO_COST,
        name="self_bwd",
    )(meta, queries, grads, context, lse, *kv, *others)


def move_body(index_ref, in_ref, out_ref):
    out_ref[...] = in_ref[...].astype(out_ref.dtype)


def put_blocks(rows, index, dtype):
    count, width = rows.shape
    return pl.pallas_call(
        move_body,
        grid_spec=pltpu.PrefetchScalarGridSpec(
            num_scalar_prefetch=1,
            grid=(count // BLK,),
            in_specs=[pl.BlockSpec((BLK, width), lambda i, s: (i, 0))],
            out_specs=pl.BlockSpec((BLK, width), lambda i, s: (s[i], 0)),
        ),
        out_shape=jax.ShapeDtypeStruct((count, width), dtype),
        cost_estimate=NO_COST,
        name="put_blocks",
    )(index, rows)


def normalize(hidden, gain_row, shift_row):
    centred = hidden - jnp.mean(hidden, axis=-1, keepdims=True)
    factor = lax.rsqrt(jnp.mean(centred * centred, axis=-1, keepdims=True) + NORM_EPS)
    unit_rows = centred * factor
    return (unit_rows * gain_row + shift_row, unit_rows, factor)


def normalize_back(incoming, unit_rows, factor, gain_row):
    scaled = incoming * gain_row
    centred_grad = (
        scaled
        - jnp.mean(scaled, axis=-1, keepdims=True)
        - unit_rows * jnp.mean(scaled * unit_rows, axis=-1, keepdims=True)
    )
    return (factor * centred_grad, jnp.sum(incoming * unit_rows, axis=0), jnp.sum(incoming, axis=0))


def adamw_step(master, gradient, first_moment, second_moment, step_rate, weight_decay):
    first_moment = BETA * first_moment + (1.0 - BETA) * gradient
    second_moment = BETA * second_moment + (1.0 - BETA) * gradient * gradient
    correction = 1.0 - BETA**STEP
    update = first_moment / correction / (jnp.sqrt(second_moment / correction) + ADAM_EPS)
    return (master - step_rate * (update + weight_decay * master), first_moment, second_moment)
def swap(value, axis, j):
    return lax.ppermute(value, axis, [(i, i ^ j) for i in range(lax.axis_size(axis))])


def spread(blocks, axis):
    return [blocks[0]] + [swap(blocks[j], axis, j) for j in range(1, len(blocks))]


def total(blocks):
    return reduce(jnp.add, [block.astype(jnp.float32) for block in blocks])


def column_blocks(array, count):
    size = array.shape[1] // count
    return [array[:, j * size : (j + 1) * size] for j in range(count)]


def row_blocks(array, count):
    size = array.shape[0] // count
    return [array[j * size : (j + 1) * size] for j in range(count)]


def pick_rows(array, index, size):
    return lax.dynamic_slice_in_dim(array, index * size, size, 0)


def by_shard(flat, shard_rows):
    shards, used = flat.shape
    return jnp.pad(flat, ((0, 0), (0, shard_rows * 128 - used))).reshape(-1, 128)


def relay_gather(block, others=()):
    near, far = swap(block, C, 1), swap(block, C, 2)
    if others:
        near, far = after([near, far], others)
    half = block.shape[0] // 2
    return [block, near, far, swap(far[:half], C, 1), swap(near[half:], C, 2)]


def relay_start(terms):
    return swap(terms[3], C, 1), swap(terms[4], C, 2)


def relay_join(terms, passed):
    own, near, far = terms[:3]
    half, low = own.shape[0] // 2, own.dtype
    near = jnp.concatenate([near[:half], (total([near[half:], passed[1]])).astype(low)])
    far = jnp.concatenate([(total([far[:half], passed[0]])).astype(low), far[half:]])
    return own, near, far


def relay_finish(joined):
    own, near, far = joined
    return [own, swap(near, C, 1), swap(far, C, 2)]


def per_device(tokens, encoder, cotangent, lengths, order, *params):
    masters, firsts, seconds = params[:7], params[7:14], params[14:]
    in_proj, out_proj, w_up, w_down, head_bias, up_bias, vectors = masters
    low, wide = jnp.bfloat16, jnp.float32
    groups, member = lax.axis_size(C), lax.axis_index(C)
    depth, plane = lax.axis_size(T), lax.axis_index(T)
    shards, shard_index = lax.axis_size(SHARD), lax.axis_index(SHARD)
    row_count, model_width = tokens.shape
    head_width, hidden_width = in_proj.shape[2], w_up.shape[1]
    heads = head_width // HEAD
    shard_rows = in_proj.shape[1]
    rounds = row_count // BLK
    rows = row_count // depth
    per_slice, per_member = rows // BLK, rounds // groups
    all_heads, all_hidden = depth * head_width, depth * hidden_width

    n_vec, n_head, n_up = vectors.size, head_bias.size, up_bias.size
    small = jnp.concatenate([vectors.reshape(-1), head_bias.reshape(-1)])
    first_part = jnp.concatenate(
        [in_proj[0], in_proj[1], in_proj[2], by_shard(small[None], shard_rows)], axis=1
    )
    first_part = lax.all_gather(first_part.astype(low), SHARD, axis=0, tiled=True)
    biases = jnp.concatenate([head_bias[2].reshape(-1), up_bias.reshape(-1)])
    proj_pack = jnp.concatenate(
        [out_proj[0].T, out_proj[1].T, in_proj[3], by_shard(biases[None], shard_rows)], axis=1
    ).astype(low)
    ffn_pack = jnp.concatenate([w_up, w_down.T], axis=1).astype(low)

    def from_planes(array):
        return [array] + [swap(array, T, j) for j in range(1, depth)]

    proj_packs = from_planes(proj_pack)
    w_enc = jnp.concatenate([in_proj[4], in_proj[5]], axis=1).astype(low)
    (w_enc,) = after([w_enc], proj_packs[1:])
    w_enc = lax.all_gather(w_enc, SHARD, axis=0, tiled=True)
    w_self = first_part[:, : 3 * head_width]
    used = -(-(n_vec + n_head) // 128)
    small = first_part.reshape(shards, shard_rows, -1)[:, :used, 3 * head_width :]
    small = small.reshape(shards, -1)
    vec_all = small[:, :n_vec].reshape(shards, 9, -1).transpose(1, 0, 2).reshape(9, -1)
    vec_all = vec_all.astype(wide)

    def by_columns(flat, count):
        return flat.reshape(shards, count, -1).transpose(1, 2, 0).reshape(count, -1).astype(wide)

    bias_heads = by_columns(small[:, n_vec : n_vec + n_head], 4)

    bases = order[0].reshape(groups, rounds, BLK)[:, :, 0]
    cut = lengths[0, 0]
    near = member ^ jnp.arange(groups)
    spot = jnp.arange(rounds)
    q_rounds = (plane ^ (spot // per_slice)) * per_slice + spot % per_slice
    q_bases = jnp.take(lax.dynamic_index_in_dim(bases, member, 0, keepdims=False), q_rounds)
    seg = jnp.stack(
        [
            (q_bases >= cut).astype(jnp.int32),
            (q_bases + BLK - 1 >= cut).astype(jnp.int32),
            jnp.clip(cut - q_bases, 0, BLK),
            jnp.pad(near, (0, rounds - groups)),
        ]
    ).astype(jnp.int32)
    near_bases = jnp.take(bases, near, axis=0)
    meta = jnp.concatenate(
        [
            near_bases,
            q_bases[None],
            jnp.where(q_bases >= cut, cut // (groups * BLK), 0)[None],
            q_rounds[None],
            jnp.full((1, rounds), cut),
        ],
        axis=0,
    ).astype(jnp.int32)
    places = (
        lax.dynamic_slice_in_dim(near_bases, member * per_member, per_member, 1) // BLK
        - member * rounds
    ).reshape(-1)

    qkv = product(tokens, w_self)
    queries = (qkv[:, :head_width] + bias_heads[0]).astype(low)
    queries = jnp.concatenate([pick_rows(queries, plane ^ j, rows) for j in range(depth)])
    no_bias = jnp.zeros((head_width,), wide)
    kv = (qkv[:, head_width:] + jnp.concatenate([no_bias, bias_heads[1]])).astype(low)
    kv = relay_gather(kv)
    ffn_packs = from_planes(after([ffn_pack], kv[:1])[0])
    (w_enc,) = after([w_enc], kv[:1])
    enc_kv = product(encoder, w_enc) + jnp.concatenate([no_bias, bias_heads[3]])
    enc_kv = enc_kv.astype(low)

    def side_by_side(packs, bounds):
        return jnp.concatenate([pack[:, a:b] for a, b in bounds for pack in packs], axis=1)

    proj_bounds = [(i * head_width, (i + 1) * head_width) for i in range(3)]
    proj_bounds.append((3 * head_width, proj_pack.shape[1]))
    w_proj = side_by_side(proj_packs, proj_bounds)
    w_proj = lax.all_gather(w_proj, SHARD, axis=0, tiled=True)
    (enc_kv,) = after([enc_kv], kv[3:])
    ffn_packs = after(ffn_packs, kv[3:])
    w_one = side_by_side(ffn_packs, [(0, hidden_width)])
    w_one = lax.all_gather(w_one, SHARD, axis=0, tiled=True)
    w_two = side_by_side(ffn_packs, [(hidden_width, 2 * hidden_width)])
    w_two = lax.all_gather(w_two, SHARD, axis=0, tiled=True)
    w_out = w_proj[:, :all_heads], w_proj[:, all_heads : 2 * all_heads]
    w_cross = w_proj[:, 2 * all_heads : 3 * all_heads]
    used = -(-(n_head // 4 + n_up) // 128)
    biases = w_proj.reshape(shards, shard_rows, -1)[:, :used, 3 * all_heads :]
    biases = biases.reshape(shards, used, depth, 128).transpose(0, 2, 1, 3)
    biases = biases.reshape(shards, depth, -1)[:, :, : n_head // 4 + n_up]
    biases = biases.transpose(1, 2, 0).astype(wide)
    bias_cross = biases[:, : n_head // 4].reshape(-1)
    bias_up = biases[:, n_head // 4 :].reshape(-1)

    def heads_to_rows(array):
        return jnp.concatenate(spread(row_blocks(array, depth), T), axis=1)

    def rows_to_heads(array):
        return jnp.concatenate(spread(column_blocks(array, depth), T), axis=0)

    def owned(gradient):
        return lax.psum_scatter(gradient.astype(low), SHARD, scatter_dimension=0, tiled=True)

    def updated(index, gradient, scale=None):
        old = masters[index], gradient, firsts[index], seconds[index]
        master, first, second = adamw_step(*old, RATES[index], DECAYS[index])
        if scale is not None:
            master = master * scale
        return master, first, second, master.astype(low)

    def plane_parts(parts):
        pieces = [column_blocks(part, depth) for part in parts]
        return [jnp.concatenate([p[j] for p in pieces], axis=1) for j in range(depth)]

    self_context, self_lse, peaks = self_fwd(queries, kv, meta)
    self_all = heads_to_rows(self_context)
    enc_kv = relay_gather(enc_kv, [self_all])
    own_tokens = pick_rows(tokens, plane, rows).astype(wide)
    hidden_one = own_tokens + contract_cols(self_all, w_out[0]) + vec_all[0]
    normed_one, unit_one, factor_one = normalize(hidden_one, vec_all[3], vec_all[4])
    low_one = normed_one.astype(low)
    cross_queries = rows_to_heads((product(low_one, w_cross) + bias_cross).astype(low))
    holder = plane * groups // depth
    outgoing = []
    for j in range(groups):
        wanted = lax.dynamic_slice_in_dim(near_bases[j], plane * per_slice, per_slice)
        wanted = jnp.clip(wanted // BLK - member * rounds, 0, rounds - 1)
        picked = [pick_rows(cotangent, wanted[i], BLK) for i in range(per_slice)]
        outgoing.append(jnp.concatenate(picked))
    outgoing = after(outgoing, enc_kv[3:])
    incoming = jnp.where(member == holder, outgoing[0], jnp.zeros_like(outgoing[0]))
    for j in range(1, groups):
        pairs = []
        for level in range(depth):
            source = level * groups // depth
            pairs.append((source * depth + level, (source ^ j) * depth + level))
        incoming = incoming + lax.ppermute(outgoing[j], (C, T), pairs)
    cot_rows = incoming.astype(wide)

    cross_context, cross_lse = cross_fwd(cross_queries, enc_kv, seg)
    cross_all = heads_to_rows(cross_context)
    hidden_two = normed_one + contract_cols(cross_all, w_out[1]) + vec_all[1]
    normed_two, unit_two, factor_two = normalize(hidden_two, vec_all[5], vec_all[6])
    low_two = normed_two.astype(low)
    upward = product(low_two, w_one) + bias_up
    below = 0.5 * (1.0 + lax.erf(upward * 0.5**0.5))
    activated = (upward * below).astype(low)
    slope = below + upward * jnp.exp(-0.5 * upward * upward) * (0.5 / jnp.pi) ** 0.5
    hidden_three = normed_two + contract_cols(activated, w_two) + vec_all[2]
    normed_three, unit_three, factor_three = normalize(hidden_three, vec_all[7], vec_all[8])

    out_rows = from_planes(normed_three.astype(low))

    grad_three, gain_three, shift_three = normalize_back(
        cot_rows, unit_three, factor_three, vec_all[7]
    )
    mlp_grad = grad_three.astype(low)
    grad_w_two = contract_rows(mlp_grad, activated).astype(low)
    act_grad = product(mlp_grad, w_two).astype(low)
    up_grad = (act_grad.astype(wide) * slope).astype(low)
    grad_w_one = contract_rows(low_two, up_grad).astype(low)
    grad_up_bias = jnp.sum(up_grad.astype(wide), axis=0)
    grad_two, gain_two, shift_two = normalize_back(
        grad_three + contract_cols(up_grad, w_one), unit_two, factor_two, vec_all[5]
    )
    low_grad_two = grad_two.astype(low)
    cross_grads = rows_to_heads(product(low_grad_two, w_out[1]).astype(low))
    grad_out_cross = contract_rows(low_grad_two, cross_all).astype(low)
    own_down, own_up = owned(grad_w_two), owned(grad_w_one)
    out_rows = after(out_rows, [cross_grads])
    out_rows = jnp.stack(out_rows)[plane ^ jnp.arange(depth)].reshape(row_count, model_width)
    portion = row_count // groups
    returned = [pick_rows(out_rows, near[j], portion) for j in range(groups)]
    cross_q_grad, *enc_terms = cross_bwd(
        cross_queries,
        enc_kv,
        seg,
        cross_grads,
        cross_context,
        cross_lse,
        [grad_w_two, grad_w_one, grad_out_cross, *returned],
    )
    returned = spread(returned, C)
    enc_passed = relay_start(enc_terms)
    cross_q_all, *returned = after([heads_to_rows(cross_q_grad), *returned], [own_down])
    grad_one, gain_one, shift_one = normalize_back(
        grad_two + contract_cols(cross_q_all, w_cross), unit_one, factor_one, vec_all[3]
    )
    low_grad_one = grad_one.astype(low)
    self_grads = product(low_grad_one, w_out[0]).astype(low)
    enc_passed = after(enc_passed, [self_grads])
    cross_q_late, low_grad_late = after([cross_q_all, low_grad_one], [self_grads])
    self_grads = rows_to_heads(self_grads)
    enc_terms = relay_finish(relay_join(enc_terms, enc_passed))
    grad_in_cross = contract_rows(low_one, cross_q_late).astype(low)
    grad_out_self = contract_rows(low_grad_late, self_all).astype(low)
    grad_vectors = jnp.stack(
        [
            jnp.sum(grad_one, axis=0),
            jnp.sum(grad_two, axis=0),
            jnp.sum(grad_three, axis=0),
            gain_one,
            shift_one,
            gain_two,
            shift_two,
            gain_three,
            shift_three,
        ]
    )
    vec_part = grad_vectors.reshape(9, shards, -1).transpose(1, 0, 2).reshape(shards, -1)
    up_part = grad_up_bias.reshape(depth, -1, shards).transpose(2, 0, 1)
    small_part = jnp.concatenate(
        [
            by_shard(jnp.concatenate([vec_part, up_part[:, j]], axis=1), shard_rows)
            for j in range(depth)
        ],
        axis=1,
    ).astype(low)
    grad_proj = jnp.concatenate([grad_out_self, grad_out_cross, grad_in_cross, small_part], axis=1)
    down_parts = spread(plane_parts(after([own_down], [self_grads])), T)
    q_grad, *kv_terms = self_bwd(
        queries,
        kv,
        meta,
        self_grads,
        self_context,
        self_lse,
        [grad_proj],
    )
    kv_passed = relay_start(kv_terms)

    kv_joined = relay_join(kv_terms, kv_passed)
    (grad_proj,) = after([grad_proj], [own_up, q_grad])
    own_proj = owned(grad_proj)
    up_parts = spread(plane_parts(after([own_up], [q_grad])), T)
    enc_terms = after(enc_terms, kv_joined[1:])
    enc_grad = total(enc_terms).astype(low)
    width_part = model_width // depth
    enc_parts = [
        contract_cols(enc_grad, pick_rows(w_enc, plane ^ j, width_part)).astype(low)
        for j in range(depth)
    ]
    enc_sent = spread(enc_parts, T)
    grad_w_enc = contract_rows(encoder, enc_grad).astype(low)
    result = put_blocks(jnp.concatenate(returned), places, wide)
    top_all = jnp.max(peaks.reshape(-1, heads, BLK), axis=(0, 2))
    for axis in (C, F):
        step = 1
        while step < lax.axis_size(axis):
            top_all = jnp.maximum(top_all, swap(top_all, axis, step))
            step *= 2

    kv_terms = after(relay_finish(kv_joined), [*enc_parts, grad_w_enc, result])
    kv_grad = total(kv_terms).astype(low)
    q_natural = jnp.concatenate([pick_rows(q_grad, plane ^ j, rows) for j in range(depth)])
    qkv_grad = jnp.concatenate([q_natural, kv_grad], axis=1)
    token_terms = []
    for j in range(depth):
        term = contract_cols(qkv_grad, pick_rows(w_self, plane ^ j, width_part))
        piece = lax.dynamic_slice_in_dim(grad_one, (plane ^ j) * width_part, width_part, 1)
        piece = piece + pick_rows(term, plane, rows)
        token_terms.append(
            lax.dynamic_update_slice_in_dim(term, piece, plane * rows, 0).astype(low)
        )
    token_sent = spread(token_terms, T)
    grad_w_self = contract_rows(tokens, qkv_grad)
    grad_head_bias = jnp.stack(
        [
            jnp.sum(q_grad.astype(wide), axis=0),
            jnp.sum(kv_grad[:, head_width:].astype(wide), axis=0),
            jnp.sum(cross_q_grad.astype(wide), axis=0),
            jnp.sum(enc_grad[:, head_width:].astype(wide), axis=0),
        ]
    )
    head_part = grad_head_bias.reshape(4, -1, shards).transpose(2, 0, 1).reshape(shards, -1)
    grad_first = jnp.concatenate([grad_w_self, by_shard(head_part, shard_rows)], axis=1).astype(low)
    own_first = owned(grad_first).astype(wide)
    own_enc = owned(after([grad_w_enc], [grad_first])[0]).astype(wide)
    down_parts = after(down_parts, [grad_first, *token_terms])
    ffn_new = updated(2, total(up_parts)) + updated(3, total(down_parts).T)
    proj_parts = [own_proj[:, i * all_heads : (i + 1) * all_heads] for i in range(3)]
    proj_parts = plane_parts(proj_parts + [own_proj[:, 3 * all_heads :]])
    proj = total(spread(after(proj_parts, [grad_first, *token_terms]), T))
    grad_encoder = total(enc_sent)
    grad_tokens = total(token_sent)

    out_self, out_cross, in_cross = [
        proj[:, i * head_width : (i + 1) * head_width] for i in range(3)
    ]
    small_part = proj[:, 3 * head_width :].reshape(-1)
    gradients = {
        0: jnp.stack(
            column_blocks(own_first[:, : 3 * head_width], 3)
            + [in_cross]
            + column_blocks(own_enc, 2)
        ),
        1: jnp.stack([out_self.T, out_cross.T]),
        4: own_first[:, 3 * head_width :].reshape(-1)[:n_head].reshape(head_bias.shape),
        5: small_part[n_vec : n_vec + n_up].reshape(up_bias.shape),
        6: small_part[:n_vec].reshape(vectors.shape),
    }
    clip_factor = CLIP_LIMIT / jnp.maximum(top_all, CLIP_LIMIT)
    root_factor = jnp.sqrt(clip_factor)
    column_roots = jnp.repeat(root_factor, HEAD)
    in_scale = jnp.concatenate(
        [column_roots[None], column_roots[None], jnp.ones((4, head_width), wide)], axis=0
    )[:, None, :]
    slot_heads = (jnp.arange(head_bias.shape[1]) * shards + shard_index) // HEAD
    picked = jnp.sum(
        jnp.where(slot_heads[:, None] == jnp.arange(heads)[None, :], root_factor[None, :], 0.0),
        axis=1,
    )
    bias_scale = jnp.concatenate([picked[None], jnp.ones((3, picked.shape[0]), wide)], axis=0)
    scales = {0: in_scale, 4: bias_scale[:, :, None]}
    results = [result, grad_tokens, grad_encoder, clip_factor]
    for index in range(7):
        if index in gradients:
            results += updated(index, gradients[index], scales.get(index))
        else:
            results += ffn_new[4 * (index - 2) : 4 * (index - 1)]
    return tuple(results)


def solution(mesh):
    rows, table = P(SHARD, None), P(F, None)
    weights = (
        P(None, SHARD, T),
        P(None, T, SHARD),
        P(SHARD, T),
        P(T, SHARD),
        P(None, T, SHARD),
        P(T, SHARD),
        P(None, SHARD),
    )
    by_columns = P(SHARD, T)
    updates = tuple(spec for spec in weights for _ in range(4))
    return jax.shard_map(
        per_device,
        mesh=mesh,
        in_specs=(rows, rows, rows, table, table) + weights * 3,
        out_specs=(rows, by_columns, by_columns, P(T)) + updates,
        check_vma=False,
    )
```

profile of v0, /device:TPU:0, one launch (start us, length us, event | category | flops | bytes accessed | tf_op | source)
XLA Modules:
  0.0 896.4 jit_solution(15599036182300141717)
XLA Ops:
  17.7 6.5 collective-permute-done.7.refs_1_
  24.2 9.5 %collective-permute-done.8.refs_2_ = bf16[128,896]{1,0:T(8,128)(2,1)S(1)} collective-permute-done((bf16[128,896]{1,0:T(8,128)(2,1)S(1)}, bf16[128,896]{1,0:T(8,128)(2,1)S(1)}, u32[]{:S(2)}, u32[]{:S(2)}) %collective-permute-start.8) | collective-permute-done | bytes 229408 | tf_op jit(solution)/shard_map/ppermute | solution.py:466
  62.5 14.8 %collective-permute-done.1.refs_2_ = bf16[1024,512]{1,0:T(8,128)(2,1)S(1)} collective-permute-done((bf16[1024,512]{1,0:T(8,128)(2,1)S(1)}, bf16[1024,512]{1,0:T(8,128)(2,1)S(1)}, u32[]{:S(2)}, u32[]{:S(2)}) %collective-permute-start.1) | collective-permute-done | bytes 1048608 | tf_op jit(solution)/shard_map/ppermute | solution.py:466
  82.8 15.7 %collective-permute-done.21.refs_2_ = bf16[128,2048]{1,0:T(8,128)(2,1)S(1)} collective-permute-done((bf16[128,2048]{1,0:T(8,128)(2,1)}, bf16[128,2048]{1,0:T(8,128)(2,1)S(1)}, u32[]{:S(2)}, u32[]{:S(2)}) %collective-permute-start.21) | collective-permute-done | bytes 524320 | tf_op jit(solution)/shard_map/ppermute | solution.py:466
  110.6 6.2 fusion.7.refs_0_
  131.7 34.8 %self_fwd.1 = (bf16[1024,256]{1,0:T(8,128)(2,1)}, f32[8,1,512]{2,1,0:T(1,128)}, f32[8,1,512]{2,1,0:T(1,128)}) custom-call(s32[8,8]{1,0:T(8,128)} %concatenate.143.meta_ref, bf16[1024,256]{1,0:T(8,128)(2,1)} %pad_maximum_fusion.10.q_ref, bf16[1024,512]{1,0:T(8,128)(2,1)} %copy-done, bf16[1024,512]{1,0:T(8,128)(2,1)} %collective-permute-done.refs_1_, ...), custom_call_target="tpu_custom_call" | custom-call | tf_op jit(solution)/shard_map/self_fwd/pallas_call | solution.py:323
  168.9 8.4 collective-permute-start.5
  177.5 5.6 collective-permute-done.5
  206.7 4.6 collective-permute-done.11
  212.1 21.3 %collective-permute-done.15.refs_3_.refs_4_ = bf16[1024,512]{1,0:T(8,128)(2,1)S(1)} collective-permute-done((bf16[1024,512]{1,0:T(8,128)(2,1)}, bf16[1024,512]{1,0:T(8,128)(2,1)S(1)}, u32[]{:S(2)}, u32[]{:S(2)}) %collective-permute-start.15) | collective-permute-done | bytes 1048608 | tf_op jit(solution)/shard_map/ppermute | solution.py:466
  235.3 42.4 %cross_fwd.1 = (bf16[1024,256]{1,0:T(8,128)(2,1)}, f32[8,1,512]{2,1,0:T(1,128)}) custom-call(s32[4,8]{1,0:T(4,128)} %pad_add_fusion.seg_ref, bf16[1024,256]{1,0:T(8,128)(2,1)} %pad_maximum_fusion.12.q_ref, bf16[2048,512]{1,0:T(8,128)(2,1)} %gate.21.refs_0_, bf16[2048,512]{1,0:T(8,128)(2,1)} %get-tuple-element.87.refs_1_, ...), custom_call_target="tpu_custom_call" | custom-call | tf_op jit(solution)/shard_map/cross_fwd/pallas_call | solution.py:168
  290.8 4.6 collective-permute-start.23
  298.4 8.6 multiply_convert_fusion
  307.0 6.6 fusion.164
  318.4 5.7 convolution_convert_fusion.1.refs_5_
  332.3 8.8 fusion.165
  341.2 6.8 multiply_reduce_fusion
  352.8 5.9 convolution_convert_fusion.refs_6_
  359.3 5.9 collective-permute-done.28
  365.2 18.9 %collective-permute-start.26 = (bf16[256,256]{1,0:T(8,128)(2,1)S(1)}, bf16[256,256]{1,0:T(8,128)(2,1)S(1)}, u32[]{:S(2)}, u32[]{:S(2)}) collective-permute-start(bf16[256,256]{1,0:T(8,128)(2,1)S(1)} %get-tuple-element.408), channel_id=1, source_target_pairs={{0,1},{1,0},{2,3},{3,2},{4,5},{5,4},{6,7},{7,6},{8,9},{9,8},{10,11... | collective-permute-start | bytes 393224 | tf_op jit(solution)/shard_map/ppermute | solution.py:466
  400.4 72.7 %cross_bwd.1 = (bf16[1024,256]{1,0:T(8,128)(2,1)}, bf16[2048,512]{1,0:T(8,128)(2,1)}, bf16[2048,512]{1,0:T(8,128)(2,1)}, bf16[2048,512]{1,0:T(8,128)(2,1)}, bf16...) custom-call(s32[4,8]{1,0:T(4,128)} %pad_add_fusion.seg_ref, bf16[1024,256]{1,0:T(8,128)(2,1)} %pad_maximum_fusion.12.q_ref, ...), custom_call_target="tpu_custom_call" | custom-call | tf_op jit(solution)/shard_map/cross_bwd/pallas_call | solution.py:246
  477.7 4.9 collective-permute-done.34
  492.2 6.5 collective-permute-start.45
  547.6 38.3 %self_bwd.1 = (bf16[1024,256]{1,0:T(8,128)(2,1)}, bf16[1024,512]{1,0:T(8,128)(2,1)}, bf16[1024,512]{1,0:T(8,128)(2,1)}, bf16[1024,512]{1,0:T(8,128)(2,1)}, bf16[...) custom-call(s32[8,8]{1,0:T(8,128)} %concatenate.143.meta_ref, bf16[1024,256]{1,0:T(8,128)(2,1)} %pad_maximum_fusion.10.q_ref, ...), custom_call_target="tpu_custom_call" | custom-call | tf_op jit(solution)/shard_map/self_bwd/pallas_call | solution.py:400
  589.8 6.6 put_blocks.1.refs_8_
  670.5 8.2 collective-permute-start.50
  678.7 16.7 %collective-permute-done.62 = bf16[128,1024]{1,0:T(8,128)(2,1)} collective-permute-done((bf16[128,1024]{1,0:T(8,128)(2,1)}, bf16[128,1024]{1,0:T(8,128)(2,1)}, u32[]{:S(2)}, u32[]{:S(2)}) %collective-permute-start.62) | collective-permute-done | bytes 262176 | tf_op jit(solution)/shard_map/ppermute | solution.py:466
  699.0 19.5 %collective-permute-start.52 = (bf16[2048,256]{1,0:T(8,128)(2,1)}, bf16[2048,256]{1,0:T(8,128)(2,1)}, u32[]{:S(2)}, u32[]{:S(2)}) collective-permute-start(bf16[2048,256]{1,0:T(8,128)(2,1)} %convolution_convert_fusion.5.refs_4_), channel_id=1, source_target_pairs={{0,1},{1,0},{2,3},{3,2},{4,5},{5,4},{6,7},{7,6},{8,9},{9,8},{10,11... | collective-permute-start | bytes 3145736 | tf_op jit(solution)/shard_map/ppermute | solution.py:466
  721.8 52.2 %collective-permute-done.50 = bf16[1024,256]{1,0:T(8,128)(2,1)S(1)} collective-permute-done((bf16[1024,256]{1,0:T(8,128)(2,1)S(1)}, bf16[1024,256]{1,0:T(8,128)(2,1)S(1)}, u32[]{:S(2)}, u32[]{:S(2)}) %collective-permute-start.50) | collective-permute-done | bytes 524320 | tf_op jit(solution)/shard_map/ppermute | solution.py:466
  777.6 58.2 %collective-permute-done.65.refs_2_ = bf16[128,1024]{1,0:T(8,128)(2,1)S(1)} collective-permute-done((bf16[128,1024]{1,0:T(8,128)(2,1)S(1)}, bf16[128,1024]{1,0:T(8,128)(2,1)S(1)}, u32[]{:S(2)}, u32[]{:S(2)}) %collective-permute-start.65) | collective-permute-done | bytes 262176 | tf_op jit(solution)/shard_map/ppermute | solution.py:466
  857.5 6.0 collective-permute-start.59
  865.3 14.5 %collective-permute-done.59 = bf16[128,896]{1,0:T(8,128)(2,1)S(1)} collective-permute-done((bf16[128,896]{1,0:T(8,128)(2,1)}, bf16[128,896]{1,0:T(8,128)(2,1)S(1)}, u32[]{:S(2)}, u32[]{:S(2)}) %collective-permute-start.59) | collective-permute-done | bytes 229408 | tf_op jit(solution)/shard_map/ppermute | solution.py:466
  (713 shorter events, 325.9 us)
Async XLA Ops:
  7.2 38.9 %all-gather.6.cloned.1.call-start = ((), (), s32[]{:S(2)}) async-start(), calls=%async_computation.5 | async-start | bytes 2064384 | tf_op jit(solution)/shard_map/all_gather | solution.py:542
  10.8 99.7 %all-gather.10.cloned.1.call-start = ((), (), s32[]{:S(2)}) async-start(), calls=%async_computation.7 | async-start | bytes 1179648 | tf_op jit(solution)/shard_map/all_gather | solution.py:555
  37.6 154.0 %all-gather.8.cloned.1.call-start = ((), (), s32[]{:S(2)}) async-start(), calls=%async_computation.6 | async-start | bytes 8257536 | tf_op jit(solution)/shard_map/all_gather | solution.py:615
  46.1 252.3 %all-gather.12.cloned.1.call-start = ((), (), s32[]{:S(2)}) async-start(), calls=%async_computation.8 | async-start | bytes 9437184 | tf_op jit(solution)/shard_map/all_gather | solution.py:619
  60.0 38.4 %collective-permute-start.21 = (bf16[128,2048]{1,0:T(8,128)(2,1)}, bf16[128,2048]{1,0:T(8,128)(2,1)S(1)}, u32[]{:S(2)}, u32[]{:S(2)}) collective-permute-start(bf16[128,2048]{1,0:T(8,128)(2,1)} %gate.23.refs_0_), channel_id=1, source_target_pairs={{0,2},{1,3},{2,0},{3,1},{4,6},{5,7},{6,4},{7,5},{8,10},{9,11},{10,... | collective-permute-start | bytes 1572872 | tf_op jit(solution)/shard_map/ppermute | solution.py:466
  61.1 37.4 %collective-permute-start.22 = (bf16[128,2048]{1,0:T(8,128)(2,1)}, bf16[128,2048]{1,0:T(8,128)(2,1)S(1)}, u32[]{:S(2)}, u32[]{:S(2)}) collective-permute-start(bf16[128,2048]{1,0:T(8,128)(2,1)} %gate.23.refs_0_), channel_id=1, source_target_pairs={{0,3},{1,2},{2,1},{3,0},{4,7},{5,6},{6,5},{7,4},{8,11},{9,10},{10,... | collective-permute-start | bytes 1572872 | tf_op jit(solution)/shard_map/ppermute | solution.py:466
  104.1 202.9 %all-gather.14.cloned.1.call-start = ((), (), s32[]{:S(2)}) async-start(), calls=%async_computation.9 | async-start | bytes 9437184 | tf_op jit(solution)/shard_map/all_gather | solution.py:621
  105.3 395.9 %reduce-scatter.6.cloned.1.call-start = ((), (), s32[]{:S(2)}) async-start(), calls=%async_computation.10 | async-start | bytes 9437184 | tf_op jit(solution)/shard_map/reduce_scatter | solution.py:639
  116.7 68.1 %collective-permute-start.13 = (bf16[2048,512]{1,0:T(8,128)(2,1)}, bf16[2048,512]{1,0:T(8,128)(2,1)S(1)}, u32[]{:S(2)}, u32[]{:S(2)}) collective-permute-start(bf16[2048,512]{1,0:T(8,128)(2,1)} %gate.21.refs_0_), channel_id=1, source_target_pairs={{0,4},{4,0},{8,12},{12,8},{1,5},{5,1},{9,13},{13,9},{2,6},{6,2},{1... | collective-permute-start | bytes 6291464 | tf_op jit(solution)/shard_map/ppermute | solution.py:466
  118.2 66.7 %collective-permute-start.14 = (bf16[2048,512]{1,0:T(8,128)(2,1)}, bf16[2048,512]{1,0:T(8,128)(2,1)}, u32[]{:S(2)}, u32[]{:S(2)}) collective-permute-start(bf16[2048,512]{1,0:T(8,128)(2,1)} %gate.21.refs_0_), channel_id=1, source_target_pairs={{0,8},{4,12},{8,0},{12,4},{1,9},{5,13},{9,1},{13,5},{2,10},{6,14},... | collective-permute-start | bytes 6291464 | tf_op jit(solution)/shard_map/ppermute | solution.py:466
  188.9 44.5 %collective-permute-start.15 = (bf16[1024,512]{1,0:T(8,128)(2,1)}, bf16[1024,512]{1,0:T(8,128)(2,1)S(1)}, u32[]{:S(2)}, u32[]{:S(2)}) collective-permute-start(bf16[1024,512]{1,0:T(8,128)(2,1)} %slice.561), channel_id=1, source_target_pairs={{0,4},{4,0},{8,12},{12,8},{1,5},{5,1},{9,13},{13,9},{2,6},{6,2},{1... | collective-permute-start | bytes 3145736 | tf_op jit(solution)/shard_map/ppermute | solution.py:466
  189.9 43.4 %collective-permute-start.16 = (bf16[1024,512]{1,0:T(8,128)(2,1)}, bf16[1024,512]{1,0:T(8,128)(2,1)S(1)}, u32[]{:S(2)}, u32[]{:S(2)}) collective-permute-start(bf16[1024,512]{1,0:T(8,128)(2,1)} %slice.562), channel_id=1, source_target_pairs={{0,8},{4,12},{8,0},{12,4},{1,9},{5,13},{9,1},{13,5},{2,10},{6,14},... | collective-permute-start | bytes 3145736 | tf_op jit(solution)/shard_map/ppermute | solution.py:466
  324.1 314.8 %reduce-scatter.10.cloned.1.call-start = ((), (), s32[]{:S(2)}) async-start(), calls=%async_computation.12 | async-start | bytes 9437184 | tf_op jit(solution)/shard_map/reduce_scatter | solution.py:639
  327.8 60.9 %collective-permute-start.29 = (bf16[256,1024]{1,0:T(8,128)(2,1)S(1)}, bf16[256,1024]{1,0:T(8,128)(2,1)S(1)}, u32[]{:S(2)}, u32[]{:S(2)}) collective-permute-start(bf16[256,1024]{1,0:T(8,128)(2,1)S(1)} %get-tuple-element.365.refs_0_), channel_id=1, source_target_pairs={{0,1},{1,0},{2,3},{3,2},{4,5},{5,4},{6,7},{7,6},{8,9},{9,8},{10,11... | collective-permute-start | bytes 1572872 | tf_op jit(solution)/shard_map/ppermute | solution.py:466
  327.9 60.9 %collective-permute-start.30 = (bf16[256,1024]{1,0:T(8,128)(2,1)S(1)}, bf16[256,1024]{1,0:T(8,128)(2,1)}, u32[]{:S(2)}, u32[]{:S(2)}) collective-permute-start(bf16[256,1024]{1,0:T(8,128)(2,1)S(1)} %get-tuple-element.365.refs_0_), channel_id=1, source_target_pairs={{0,2},{1,3},{2,0},{3,1},{4,6},{5,7},{6,4},{7,5},{8,10},{9,11},{10,... | collective-permute-start | bytes 1572872 | tf_op jit(solution)/shard_map/ppermute | solution.py:466
  328.5 60.3 %collective-permute-start.31 = (bf16[256,1024]{1,0:T(8,128)(2,1)S(1)}, bf16[256,1024]{1,0:T(8,128)(2,1)}, u32[]{:S(2)}, u32[]{:S(2)}) collective-permute-start(bf16[256,1024]{1,0:T(8,128)(2,1)S(1)} %get-tuple-element.365.refs_0_), channel_id=1, source_target_pairs={{0,3},{1,2},{2,1},{3,0},{4,7},{5,6},{6,5},{7,4},{8,11},{9,10},{10,... | collective-permute-start | bytes 1572872 | tf_op jit(solution)/shard_map/ppermute | solution.py:466
  359.2 489.5 %reduce-scatter.14.cloned.1.call-start = ((), (), s32[]{:S(2)}) async-start(), calls=%async_computation.14 | async-start | bytes 1179648 | tf_op jit(solution)/shard_map/reduce_scatter | solution.py:639
  396.5 104.7 %collective-permute-start.35 = (bf16[256,1024]{1,0:T(8,128)(2,1)}, bf16[256,1024]{1,0:T(8,128)(2,1)}, u32[]{:S(2)}, u32[]{:S(2)}) collective-permute-start(bf16[256,1024]{1,0:T(8,128)(2,1)} %get-tuple-element.355.refs_9_), channel_id=1, source_target_pairs={{0,4},{4,0},{8,12},{12,8},{1,5},{5,1},{9,13},{13,9},{2,6},{6,2},{1... | collective-permute-start | bytes 1572872 | tf_op jit(solution)/shard_map/ppermute | solution.py:466
  398.9 102.3 %collective-permute-start.36 = (bf16[256,1024]{1,0:T(8,128)(2,1)}, bf16[256,1024]{1,0:T(8,128)(2,1)}, u32[]{:S(2)}, u32[]{:S(2)}) collective-permute-start(bf16[256,1024]{1,0:T(8,128)(2,1)} %get-tuple-element.354.refs_10_), channel_id=1, source_target_pairs={{0,8},{4,12},{8,0},{12,4},{1,9},{5,13},{9,1},{13,5},{2,10},{6,14},... | collective-permute-start | bytes 1572872 | tf_op jit(solution)/shard_map/ppermute | solution.py:466
  398.9 102.3 %collective-permute-start.37 = (bf16[256,1024]{1,0:T(8,128)(2,1)}, bf16[256,1024]{1,0:T(8,128)(2,1)}, u32[]{:S(2)}, u32[]{:S(2)}) collective-permute-start(bf16[256,1024]{1,0:T(8,128)(2,1)} %get-tuple-element.353.refs_11_), channel_id=1, source_target_pairs={{0,12},{4,8},{8,4},{12,0},{1,13},{5,9},{9,5},{13,1},{2,14},{6,10},... | collective-permute-start | bytes 1572872 | tf_op jit(solution)/shard_map/ppermute | solution.py:466
  530.8 81.7 %collective-permute-start.47 = (bf16[2048,512]{1,0:T(8,128)(2,1)}, bf16[2048,512]{1,0:T(8,128)(2,1)}, u32[]{:S(2)}, u32[]{:S(2)}) collective-permute-start(bf16[2048,512]{1,0:T(8,128)(2,1)} %pad_maximum_fusion.2), channel_id=1, source_target_pairs={{0,4},{4,0},{8,12},{12,8},{1,5},{5,1},{9,13},{13,9},{2,6},{6,2},{1... | collective-permute-start | bytes 6291464 | tf_op jit(solution)/shard_map/ppermute | solution.py:466
  533.9 78.6 %collective-permute-start.48 = (bf16[2048,512]{1,0:T(8,128)(2,1)}, bf16[2048,512]{1,0:T(8,128)(2,1)}, u32[]{:S(2)}, u32[]{:S(2)}) collective-permute-start(bf16[2048,512]{1,0:T(8,128)(2,1)} %pad_maximum_fusion.3), channel_id=1, source_target_pairs={{0,8},{4,12},{8,0},{12,4},{1,9},{5,13},{9,1},{13,5},{2,10},{6,14},... | collective-permute-start | bytes 6291464 | tf_op jit(solution)/shard_map/ppermute | solution.py:466
  637.9 211.8 %reduce-scatter.8.cloned.1.call-start = ((), (), s32[]{:S(2)}) async-start(), calls=%async_computation.11 | async-start | bytes 2064384 | tf_op jit(solution)/shard_map/reduce_scatter | solution.py:639
  638.6 212.9 %reduce-scatter.12.cloned.1.call-start = ((), (), s32[]{:S(2)}) async-start(), calls=%async_computation.13 | async-start | bytes 8257536 | tf_op jit(solution)/shard_map/reduce_scatter | solution.py:639
  658.0 37.4 %collective-permute-start.62 = (bf16[128,1024]{1,0:T(8,128)(2,1)}, bf16[128,1024]{1,0:T(8,128)(2,1)}, u32[]{:S(2)}, u32[]{:S(2)}) collective-permute-start(bf16[128,1024]{1,0:T(8,128)(2,1)} %get-tuple-element.372), channel_id=1, source_target_pairs={{0,2},{1,3},{2,0},{3,1},{4,6},{5,7},{6,4},{7,5},{8,10},{9,11},{10,... | collective-permute-start | bytes 786440 | tf_op jit(solution)/shard_map/ppermute | solution.py:466
  670.5 103.5 %collective-permute-start.50 = (bf16[1024,256]{1,0:T(8,128)(2,1)S(1)}, bf16[1024,256]{1,0:T(8,128)(2,1)S(1)}, u32[]{:S(2)}, u32[]{:S(2)}) collective-permute-start(bf16[1024,256]{1,0:T(8,128)(2,1)S(1)} %convert_element_type.390.refs_7_), channel_id=1, source_target_pairs={{0,2},{1,3},{2,0},{3,1},{4,6},{5,7},{6,4},{7,5},{8,10},{9,11},{10,... | collective-permute-start | bytes 1572872 | tf_op jit(solution)/shard_map/ppermute | solution.py:466
  695.4 78.6 %collective-permute-start.49 = (bf16[1024,256]{1,0:T(8,128)(2,1)S(1)}, bf16[1024,256]{1,0:T(8,128)(2,1)S(1)}, u32[]{:S(2)}, u32[]{:S(2)}) collective-permute-start(bf16[1024,256]{1,0:T(8,128)(2,1)S(1)} %convert_element_type.388.refs_6_), channel_id=1, source_target_pairs={{0,1},{1,0},{2,3},{3,2},{4,5},{5,4},{6,7},{7,6},{8,9},{9,8},{10,11... | collective-permute-start | bytes 1572872 | tf_op jit(solution)/shard_map/ppermute | solution.py:466
  695.5 149.6 %collective-permute-start.54 = (bf16[2048,256]{1,0:T(8,128)(2,1)}, bf16[2048,256]{1,0:T(8,128)(2,1)}, u32[]{:S(2)}, u32[]{:S(2)}) collective-permute-start(bf16[2048,256]{1,0:T(8,128)(2,1)} %convolution_convert_fusion.3.refs_6_), channel_id=1, source_target_pairs={{0,3},{1,2},{2,1},{3,0},{4,7},{5,6},{6,5},{7,4},{8,11},{9,10},{10,... | collective-permute-start | bytes 3145736 | tf_op jit(solution)/shard_map/ppermute | solution.py:466
  696.6 148.5 %collective-permute-start.53 = (bf16[2048,256]{1,0:T(8,128)(2,1)}, bf16[2048,256]{1,0:T(8,128)(2,1)}, u32[]{:S(2)}, u32[]{:S(2)}) collective-permute-start(bf16[2048,256]{1,0:T(8,128)(2,1)} %convolution_convert_fusion.4.refs_5_), channel_id=1, source_target_pairs={{0,2},{1,3},{2,0},{3,1},{4,6},{5,7},{6,4},{7,5},{8,10},{9,11},{10,... | collective-permute-start | bytes 3145736 | tf_op jit(solution)/shard_map/ppermute | solution.py:466
  699.0 146.1 %collective-permute-start.52 = (bf16[2048,256]{1,0:T(8,128)(2,1)}, bf16[2048,256]{1,0:T(8,128)(2,1)}, u32[]{:S(2)}, u32[]{:S(2)}) collective-permute-start(bf16[2048,256]{1,0:T(8,128)(2,1)} %convolution_convert_fusion.5.refs_4_), channel_id=1, source_target_pairs={{0,1},{1,0},{2,3},{3,2},{4,5},{5,4},{6,7},{7,6},{8,9},{9,8},{10,11... | collective-permute-start | bytes 3145736 | tf_op jit(solution)/shard_map/ppermute | solution.py:466
  774.0 61.8 %collective-permute-start.65 = (bf16[128,1024]{1,0:T(8,128)(2,1)S(1)}, bf16[128,1024]{1,0:T(8,128)(2,1)S(1)}, u32[]{:S(2)}, u32[]{:S(2)}) collective-permute-start(bf16[128,1024]{1,0:T(8,128)(2,1)S(1)} %copy-done.83), channel_id=1, source_target_pairs={{0,2},{1,3},{2,0},{3,1},{4,6},{5,7},{6,4},{7,5},{8,10},{9,11},{10,... | collective-permute-start | bytes 786440 | tf_op jit(solution)/shard_map/ppermute | solution.py:466
  774.0 61.8 %collective-permute-start.66 = (bf16[128,1024]{1,0:T(8,128)(2,1)S(1)}, bf16[128,1024]{1,0:T(8,128)(2,1)S(1)}, u32[]{:S(2)}, u32[]{:S(2)}) collective-permute-start(bf16[128,1024]{1,0:T(8,128)(2,1)S(1)} %copy-done.82), channel_id=1, source_target_pairs={{0,3},{1,2},{2,1},{3,0},{4,7},{5,6},{6,5},{7,4},{8,11},{9,10},{10,... | collective-permute-start | bytes 786440 | tf_op jit(solution)/shard_map/ppermute | solution.py:466
  (178 other events, 2501.9 us)
Sparse Core Ops, SparseCore 0:
  11.0 29.4 all-gather.5
  42.9 27.7 all-gather.9
  72.6 70.9 all-gather.7
  145.4 88.1 all-gather.11
  235.3 54.5 all-gather.13
  324.2 72.0 reduce-scatter.5
  400.1 73.7 reduce-scatter.9
  638.0 33.0 reduce-scatter.13
  674.5 39.6 reduce-scatter.7
  717.4 66.9 reduce-scatter.11
where the time goes:
time: 901 us; the launch traced here: 896 us
  waiting for transfers between devices  251 us (28%)
  Pallas kernels  195 us (22%)
  starting transfers between devices  150 us (17%)
  local copies, waits for them, and re-layouts  101 us (11%)
  matrix products  94.9 us (11%)
  other arithmetic  80 us (9%)
  between operations  24.6 us (3%)
    ppermute x64, waiting for transfers between devices, swap(): lax.ppermute(value, axis, [(i, i ^ j) for i in range(lax.axis_size(axis))])  250 us
    ppermute x64, starting transfers between devices, swap(): lax.ppermute(value, axis, [(i, i ^ j) for i in range(lax.axis_size(axis))])  138 us
    pallas_call x1, Pallas kernels, cross_bwd(): pl.pallas_call(partial(cross_bwd_body, heads, bounds, len(others), step),...  72.7 us
    unnamed x314, local copies, waits for them, and re-layouts  44.3 us
    pallas_call x1, Pallas kernels, cross_fwd(): pl.pallas_call(partial(cross_fwd_body, heads, bounds), grid_spec=pltpu.Pr...  42.4 us
    pallas_call x1, Pallas kernels, self_bwd(): pl.pallas_call(partial(self_bwd_body, heads, bounds, len(others)), grid_s...  38.3 us
    dot_general x7, matrix products, product(): return jnp.dot(left_side, right_side, preferred_element_type=jnp.float32)  36.2 us
    pallas_call x1, Pallas kernels, self_fwd(): pl.pallas_call(partial(self_fwd_body, heads, bounds), grid_spec=pltpu.Pre...  34.8 us
  transfers between devices with their start and end apart: 77, of which 24 were waited for; matrix products, arithmetic and copies ran while one was open for 26% of the time, Pallas kernels for 22%

commit v1 on v0

--- a/solution.py
+++ b/solution.py
@@ -24,6 +24,7 @@
 F, C, T = "fsdp", "context", "tensor"
 SHARD = (F, C)
 NO_COST = pl.CostEstimate(flops=0, bytes_accessed=0, transcendentals=0)
+SOME_COST = pl.CostEstimate(flops=2 * 10**10, bytes_accessed=2**25, transcendentals=0)
 
 
 def product(left_side, right_side):
@@ -192,33 +193,39 @@
     )(seg, queries, *enc_kv)
 
 
-def cross_bwd_body(heads, bounds, waits, step, seg_ref, q_ref, g_ref, o_ref, lse_ref, *refs):
-    count = len(bounds)
-    sources, (dq_ref, *outs) = refs[:count], refs[count + waits : 2 * count + waits + 1]
-    kv_ref, acc_ref, sems = refs[2 * count + waits + 1 :]
-    places = member_rows(seg_ref, 3, bounds, sources[0].shape[0])
+def cross_bwd_body(heads, bounds, kind, step, seg_ref, q_ref, g_ref, o_ref, lse_ref, *refs):
+    count, outs = len(bounds), refs[-len(bounds) - 4 : -3]
+    sources, prior, (dq_ref, *outs) = refs[:count], refs[count], outs
+    kv_ref, acc_ref, sems = refs[-3:]
+    block = pl.program_id(0)
+    sequence, full = seg_ref[4, kind], ENC // 2
+    places = [
+        pl.ds(pl.multiple_of(seg_ref[3, j] * full + at - sequence * ENC, size), size)
+        for j, at, size in bounds
+    ]
     fetch_kv(sources, [kv_ref.at[place] for place in places], sems)
-    block = pl.program_id(0)
 
     @pl.when(block == 0)
     def _():
         acc_ref[...] = jnp.zeros_like(acc_ref)
 
-    low, high, cut = seg_ref[0, block], seg_ref[1, block], seg_ref[2, block]
-    queries = stack_heads(q_ref[...] * jnp.bfloat16(SCALE), heads)
-    rows, width = queries.shape
-    grads = stack_heads(g_ref[...], heads)
-    dots = g_ref[...].astype(jnp.float32) * o_ref[...].astype(jnp.float32)
-    dot_row = col_to_row(jnp.sum(stack_heads(dots, heads), axis=1, keepdims=True))
-    all_lse = lse_ref[0]
-    place = lax.broadcasted_iota(jnp.int32, all_lse.shape, 1) % BLK
-    own_seq = jnp.where(place >= cut, 1, 0)
-
-    def sequence_terms(sequence, q_grad):
-        lse = jnp.where(own_seq == sequence, all_lse, -NEGATIVE)
+    seen = (seg_ref[0, block] <= sequence) & (seg_ref[1, block] >= sequence)
+    start = prior[...] if kind == 0 else jnp.zeros_like(dq_ref)
+    dq_ref[...] = start
+
+    @pl.when(seen)
+    def _():
+        queries = stack_heads(q_ref[...] * jnp.bfloat16(SCALE), heads)
+        rows, width = queries.shape
+        grads = stack_heads(g_ref[...], heads)
+        dots = g_ref[...].astype(jnp.float32) * o_ref[...].astype(jnp.float32)
+        dot_row = col_to_row(jnp.sum(stack_heads(dots, heads), axis=1, keepdims=True))
+        place = lax.broadcasted_iota(jnp.int32, lse_ref[0].shape, 1) % BLK
+        own_seq = jnp.where(place >= seg_ref[2, block], 1, 0)
+        lse = jnp.where(own_seq == sequence, lse_ref[0], -NEGATIVE)
 
         def tile_terms(t, q_grad):
-            at = pl.ds(pl.multiple_of(sequence * ENC + t * step, step), step)
+            at = pl.ds(pl.multiple_of(t * step, step), step)
             keys, values = kv_ref[at, :width], kv_ref[at, width:]
             probs = jnp.exp(contract_cols(keys, queries) - lse)
             s_grad = (probs * (contract_cols(values, grads) - dot_row)).astype(jnp.bfloat16)
@@ -226,10 +233,11 @@
             acc_ref[at, :width] += product(s_grad, queries)
             return q_grad + contract_rows(s_grad, keys)
 
-        return lax.fori_loop(0, ENC // step, tile_terms, q_grad)
-
-    q_grad = lax.fori_loop(low, high + 1, sequence_terms, jnp.zeros((rows, width), jnp.float32))
-    dq_ref[...] = (merge_heads(q_grad, heads) * SCALE).astype(dq_ref.dtype)
+        q_grad = lax.fori_loop(
+            0, ENC // step, tile_terms, jnp.zeros((rows, width), jnp.float32)
+        )
+        q_grad = merge_heads(q_grad, heads) * SCALE + start.astype(jnp.float32)
+        dq_ref[...] = q_grad.astype(dq_ref.dtype)
 
     @pl.when(block == pl.num_programs(0) - 1)
     def _():
@@ -237,32 +245,35 @@
             out[...] = acc_ref[place, :].astype(out.dtype)
 
 
-def cross_bwd(queries, enc_kv, seg, grads, context, lse, others):
+def cross_bwd(kind, queries, enc_kv, seg, grads, context, lse, prior, others):
     count, width = queries.shape
     heads, blocks, step = width // HEAD, count // BLK, 512
-    rows, bounds = heads * BLK, piece_bounds(enc_kv)
-    enc_all = sum(piece.shape[0] for piece in enc_kv)
+    bounds = piece_bounds(enc_kv)
+    picked = [(0, 1), (2, 3, 4)][kind]
+    pieces, bounds = [enc_kv[i] for i in picked], [bounds[i] for i in picked]
     row = pl.BlockSpec((BLK, width), lambda i, s: (i, 0))
     return pl.pallas_call(
-        partial(cross_bwd_body, heads, bounds, len(others), step),
+        partial(cross_bwd_body, heads, bounds, kind, step),
         grid_spec=pltpu.PrefetchScalarGridSpec(
             num_scalar_prefetch=1,
             grid=(blocks,),
-            in_specs=[row, row, row, pl.BlockSpec((1, 1, rows), lambda i, s: (i, 0, 0))]
-            + [pl.BlockSpec(memory_space=pl.ANY)] * (len(bounds) + len(others)),
-            out_specs=[row] + [whole(piece.shape) for piece in enc_kv],
+            in_specs=[row, row, row, pl.BlockSpec((1, 1, heads * BLK), lambda i, s: (i, 0, 0))]
+            + [pl.BlockSpec(memory_space=pl.ANY)] * len(bounds)
+            + [row]
+            + [pl.BlockSpec(memory_space=pl.ANY)] * len(others),
+            out_specs=[row] + [whole(piece.shape) for piece in pieces],
             scratch_shapes=[
-                pltpu.VMEM((enc_all, 2 * width), jnp.bfloat16),
-                pltpu.VMEM((enc_all, 2 * width), jnp.float32),
+                pltpu.VMEM((ENC, 2 * width), jnp.bfloat16),
+                pltpu.VMEM((ENC, 2 * width), jnp.float32),
                 pltpu.SemaphoreType.DMA((len(bounds),)),
             ],
         ),
         out_shape=[jax.ShapeDtypeStruct((count, width), jnp.bfloat16)]
-        + [jax.ShapeDtypeStruct(piece.shape, jnp.bfloat16) for piece in enc_kv],
+        + [jax.ShapeDtypeStruct(piece.shape, jnp.bfloat16) for piece in pieces],
         compiler_params=pltpu.CompilerParams(vmem_limit_bytes=VMEM_BYTES),
         cost_estimate=NO_COST,
         name="cross_bwd",
-    )(seg, queries, grads, context, lse, *enc_kv, *others)
+    )(seg, queries, grads, context, lse, *pieces, prior, *others)
 
 
 def gather_tile(kv_ref, t, columns):
@@ -434,9 +445,215 @@
             out_specs=pl.BlockSpec((BLK, width), lambda i, s: (s[i], 0)),
         ),
         out_shape=jax.ShapeDtypeStruct((count, width), dtype),
-        cost_estimate=NO_COST,
+        cost_estimate=SOME_COST,
         name="put_blocks",
     )(index, rows)
+
+
+def join_body(whole_ref, passed_ref, *refs):
+    total = whole_ref[...].astype(jnp.float32) + passed_ref[...].astype(jnp.float32)
+    refs[-1][...] = total.astype(refs[-1].dtype)
+
+
+def add_half(whole_rows, passed, lower, others):
+    half, width = passed.shape
+    size = min(half, 256)
+    first = half // size if lower else 0
+    part = pl.BlockSpec((size, width), lambda i: (first + i, 0))
+    return pl.pallas_call(
+        join_body,
+        grid=(half // size,),
+        in_specs=[part, pl.BlockSpec((size, width), lambda i: (i, 0))]
+        + [pl.BlockSpec(memory_space=pl.ANY)] * len(others),
+        out_specs=part,
+        out_shape=jax.ShapeDtypeStruct(whole_rows.shape, whole_rows.dtype),
+        input_output_aliases={0: 0},
+        cost_estimate=NO_COST,
+        name="add_half",
+    )(whole_rows, passed, *others)
+
+
+def grad_body(count, *refs):
+    out_ref, start = refs[-1], 0
+    for k in range(count):
+        terms = contract_rows(refs[2 * k][...], refs[2 * k + 1][...])
+        out_ref[:, start : start + terms.shape[1]] = terms.astype(out_ref.dtype)
+        start += terms.shape[1]
+    for ref in refs[2 * count : -1]:
+        out_ref[:, start : start + ref.shape[1]] = ref[...]
+        start += ref.shape[1]
+
+
+def grad_columns(pairs, others, tiles=1):
+    flat = [array for pair in pairs for array in pair]
+    width = pairs[0][0].shape[1]
+    columns = sum(right.shape[1] for _, right in pairs) + sum(array.shape[1] for array in others)
+    size = pairs[0][1].shape[0]
+    if tiles == 1:
+        specs = [pl.BlockSpec(array.shape, lambda i: (0, 0)) for array in flat + others]
+    else:
+        specs = [
+            pl.BlockSpec((size, width), lambda i: (0, 0)),
+            pl.BlockSpec((size, columns // tiles), lambda i: (0, i)),
+        ]
+    return pl.pallas_call(
+        partial(grad_body, len(pairs)),
+        grid=(tiles,),
+        in_specs=specs,
+        out_specs=pl.BlockSpec((width, columns // tiles), lambda i: (0, i)),
+        out_shape=jax.ShapeDtypeStruct((width, columns), jnp.bfloat16),
+        compiler_params=pltpu.CompilerParams(vmem_limit_bytes=VMEM_BYTES),
+        cost_estimate=NO_COST,
+        name="grad_columns",
+    )(*flat, *others)
+
+
+def plane_body(plane_ref, *refs):
+    start = 0
+    for ref in refs[:-1]:
+        refs[-1][:, start : start + ref.shape[1]] = ref[...]
+        start += ref.shape[1]
+
+
+def by_plane_order(arrays, plane, depth):
+    size = arrays[0].shape[0]
+    widths = [array.shape[1] // depth for array in arrays]
+    return pl.pallas_call(
+        plane_body,
+        grid_spec=pltpu.PrefetchScalarGridSpec(
+            num_scalar_prefetch=1,
+            grid=(depth,),
+            in_specs=[pl.BlockSpec((size, width), lambda p, s: (0, s[0] ^ p)) for width in widths],
+            out_specs=pl.BlockSpec((size, sum(widths)), lambda p, s: (0, p)),
+        ),
+        out_shape=jax.ShapeDtypeStruct((size, depth * sum(widths)), arrays[0].dtype),
+        cost_estimate=NO_COST,
+        name="by_plane_order",
+    )(plane.reshape(1).astype(jnp.int32), *arrays)
+
+
+ANYWHERE = pl.BlockSpec(memory_space=pl.ANY)
+
+
+def sum_body(count, *refs):
+    out_ref, column_ref = refs[-2:]
+    added = reduce(jnp.add, [ref[...].astype(jnp.float32) for ref in refs[:count]])
+    rounded = added.astype(out_ref.dtype)
+    out_ref[...] = rounded
+
+    @pl.when(pl.program_id(0) == 0)
+    def _():
+        column_ref[...] = jnp.zeros_like(column_ref)
+
+    column_ref[...] += jnp.sum(rounded.astype(jnp.float32), axis=0, keepdims=True)
+
+
+def sum_terms(terms, others, cost=SOME_COST):
+    count, width = terms[0].shape
+    size = 256
+    tile = pl.BlockSpec((size, width), lambda i: (i, 0))
+    return pl.pallas_call(
+        partial(sum_body, len(terms)),
+        grid=(count // size,),
+        in_specs=[tile] * len(terms) + [ANYWHERE] * len(others),
+        out_specs=[tile, pl.BlockSpec((1, width), lambda i: (0, 0))],
+        out_shape=[
+            jax.ShapeDtypeStruct((count, width), jnp.bfloat16),
+            jax.ShapeDtypeStruct((1, width), jnp.float32),
+        ],
+        cost_estimate=cost,
+        name="sum_terms",
+    )(*terms, *others)
+
+
+def share_body(depth, parts, extra, plane_ref, *refs):
+    rows = [ref[...] for ref in refs[:parts]]
+    merged = rows[0] if parts == 1 else jnp.concatenate(rows, axis=1)
+    own = pl.program_id(0) == plane_ref[0]
+    for j in range(depth):
+        term = contract_cols(merged, refs[parts + j][...])
+        if extra:
+            term = term + jnp.where(own, refs[parts + depth + j][...], 0.0)
+        refs[len(refs) - depth + j][...] = term.astype(jnp.bfloat16)
+
+
+def plane_shares(arrays, weight, plane, depth, extra, others, cost=SOME_COST):
+    count, size = arrays[-1].shape[0], 256 if extra is None else extra.shape[0]
+    part = weight.shape[0] // depth
+    last = pl.BlockSpec((size, arrays[-1].shape[1]), lambda i, s: (i, 0))
+    specs = [last]
+    if len(arrays) == 2:
+        specs = [pl.BlockSpec((size, arrays[0].shape[1]), lambda i, s: (s[0] ^ i, 0)), last]
+    for j in range(depth):
+        specs.append(
+            pl.BlockSpec((part, weight.shape[1]), partial(lambda j, i, s: (s[0] ^ j, 0), j))
+        )
+    inputs = [*arrays, *[weight] * depth]
+    if extra is not None:
+        for j in range(depth):
+            specs.append(pl.BlockSpec((size, part), partial(lambda j, i, s: (0, s[0] ^ j), j)))
+        inputs += [extra] * depth
+    return pl.pallas_call(
+        partial(share_body, depth, len(arrays), extra is not None),
+        grid_spec=pltpu.PrefetchScalarGridSpec(
+            num_scalar_prefetch=1,
+            grid=(count // size,),
+            in_specs=specs + [ANYWHERE] * len(others),
+            out_specs=[pl.BlockSpec((size, part), lambda i, s: (i, 0))] * depth,
+        ),
+        out_shape=[jax.ShapeDtypeStruct((count, part), jnp.bfloat16)] * depth,
+        compiler_params=pltpu.CompilerParams(vmem_limit_bytes=VMEM_BYTES),
+        cost_estimate=cost,
+        name="plane_shares",
+    )(plane.reshape(1).astype(jnp.int32), *inputs, *others)
+
+
+def gather_grad_body(parts, adds, plane_ref, left_ref, *refs):
+    out_ref, acc_ref = refs[-2:]
+    step = pl.program_id(0)
+
+    @pl.when(step == 0)
+    def _():
+        acc_ref[...] = jnp.zeros_like(acc_ref)
+
+    start = 0
+    for ref in refs[:parts]:
+        stop = start + ref.shape[1]
+        acc_ref[:, start:stop] += contract_rows(left_ref[...], ref[...])
+        start = stop
+
+    @pl.when(step == pl.num_programs(0) - 1)
+    def _():
+        out_ref[:, :start] = acc_ref[...].astype(out_ref.dtype)
+        at = start
+        for ref in refs[parts : parts + adds]:
+            out_ref[:, at : at + ref.shape[1]] = ref[...]
+            at += ref.shape[1]
+
+
+def weight_grad(left, arrays, adds, plane, size, others, cost=SOME_COST):
+    count, width = left.shape
+    last = pl.BlockSpec((size, arrays[-1].shape[1]), lambda i, s: (i, 0))
+    specs = [pl.BlockSpec((size, width), lambda i, s: (i, 0)), last]
+    if len(arrays) == 2:
+        specs.insert(1, pl.BlockSpec((size, arrays[0].shape[1]), lambda i, s: (s[0] ^ i, 0)))
+    made = sum(array.shape[1] for array in arrays)
+    columns = made + sum(array.shape[1] for array in adds)
+    specs += [whole(array.shape) for array in adds] + [ANYWHERE] * len(others)
+    return pl.pallas_call(
+        partial(gather_grad_body, len(arrays), len(adds)),
+        grid_spec=pltpu.PrefetchScalarGridSpec(
+            num_scalar_prefetch=1,
+            grid=(count // size,),
+            in_specs=specs,
+            out_specs=pl.BlockSpec((width, columns), lambda i, s: (0, 0)),
+            scratch_shapes=[pltpu.VMEM((width, made), jnp.float32)],
+        ),
+        out_shape=jax.ShapeDtypeStruct((width, columns), jnp.bfloat16),
+        compiler_params=pltpu.CompilerParams(vmem_limit_bytes=VMEM_BYTES),
+        cost_estimate=cost,
+        name="weight_grad",
+    )(plane.reshape(1).astype(jnp.int32), left, *arrays, *adds, *others)
 
 
 def normalize(hidden, gain_row, shift_row):
@@ -490,7 +707,8 @@
 
 def by_shard(flat, shard_rows):
     shards, used = flat.shape
-    return jnp.pad(flat, ((0, 0), (0, shard_rows * 128 - used))).reshape(-1, 128)
+    flat = jnp.pad(flat, ((0, 0), (0, -used % 128))).reshape(shards, -1, 128)
+    return jnp.pad(flat, ((0, 0), (0, shard_rows - flat.shape[1]), (0, 0))).reshape(-1, 128)
 
 
 def relay_gather(block, others=()):
@@ -501,16 +719,13 @@
     return [block, near, far, swap(far[:half], C, 1), swap(near[half:], C, 2)]
 
 
-def relay_start(terms):
-    return swap(terms[3], C, 1), swap(terms[4], C, 2)
-
-
-def relay_join(terms, passed):
+def relay_start(upper, lower):
+    return swap(upper, C, 1), swap(lower, C, 2)
+
+
+def relay_join(terms, passed, others=()):
     own, near, far = terms[:3]
-    half, low = own.shape[0] // 2, own.dtype
-    near = jnp.concatenate([near[:half], (total([near[half:], passed[1]])).astype(low)])
-    far = jnp.concatenate([(total([far[:half], passed[0]])).astype(low), far[half:]])
-    return own, near, far
+    return own, add_half(near, passed[1], True, others), add_half(far, passed[0], False, others)
 
 
 def relay_finish(joined):
@@ -577,6 +792,7 @@
             (q_bases + BLK - 1 >= cut).astype(jnp.int32),
             jnp.clip(cut - q_bases, 0, BLK),
             jnp.pad(near, (0, rounds - groups)),
+            (member * encoder.shape[0] // ENC) ^ jnp.minimum(spot, 1),
         ]
     ).astype(jnp.int32)
     near_bases = jnp.take(bases, near, axis=0)
@@ -605,6 +821,7 @@
     (w_enc,) = after([w_enc], kv[:1])
     enc_kv = product(encoder, w_enc) + jnp.concatenate([no_bias, bias_heads[3]])
     enc_kv = enc_kv.astype(low)
+    *kv[3:], w_kept = after([*kv[3:], w_self], [enc_kv])
 
     def side_by_side(packs, bounds):
         return jnp.concatenate([pack[:, a:b] for a, b in bounds for pack in packs], axis=1)
@@ -632,8 +849,11 @@
     def heads_to_rows(array):
         return jnp.concatenate(spread(row_blocks(array, depth), T), axis=1)
 
+    def to_heads(array):
+        return spread(column_blocks(array, depth), T)
+
     def rows_to_heads(array):
-        return jnp.concatenate(spread(column_blocks(array, depth), T), axis=0)
+        return jnp.concatenate(to_heads(array), axis=0)
 
     def owned(gradient):
         return lax.psum_scatter(gradient.astype(low), SHARD, scatter_dimension=0, tiled=True)
@@ -644,10 +864,6 @@
         if scale is not None:
             master = master * scale
         return master, first, second, master.astype(low)
-
-    def plane_parts(parts):
-        pieces = [column_blocks(part, depth) for part in parts]
-        return [jnp.concatenate([p[j] for p in pieces], axis=1) for j in range(depth)]
 
     self_context, self_lse, peaks = self_fwd(queries, kv, meta)
     self_all = heads_to_rows(self_context)
@@ -664,6 +880,14 @@
         wanted = jnp.clip(wanted // BLK - member * rounds, 0, rounds - 1)
         picked = [pick_rows(cotangent, wanted[i], BLK) for i in range(per_slice)]
         outgoing.append(jnp.concatenate(picked))
+    (peaks,) = after([peaks], [cross_queries])
+    top_all = jnp.max(peaks.reshape(-1, heads, BLK), axis=(0, 2))
+    for axis in (C, F):
+        step = 1
+        while step < lax.axis_size(axis):
+            top_all = jnp.maximum(top_all, swap(top_all, axis, step))
+            step *= 2
+    enc_kv[3:] = after(enc_kv[3:], [cross_queries, top_all])
     outgoing = after(outgoing, enc_kv[3:])
     incoming = jnp.where(member == holder, outgoing[0], jnp.zeros_like(outgoing[0]))
     for j in range(1, groups):
@@ -672,8 +896,6 @@
             source = level * groups // depth
             pairs.append((source * depth + level, (source ^ j) * depth + level))
         incoming = incoming + lax.ppermute(outgoing[j], (C, T), pairs)
-    cot_rows = incoming.astype(wide)
-
     cross_context, cross_lse = cross_fwd(cross_queries, enc_kv, seg)
     cross_all = heads_to_rows(cross_context)
     hidden_two = normed_one + contract_cols(cross_all, w_out[1]) + vec_all[1]
@@ -686,51 +908,37 @@
     hidden_three = normed_two + contract_cols(activated, w_two) + vec_all[2]
     normed_three, unit_three, factor_three = normalize(hidden_three, vec_all[7], vec_all[8])
 
-    out_rows = from_planes(normed_three.astype(low))
-
     grad_three, gain_three, shift_three = normalize_back(
-        cot_rows, unit_three, factor_three, vec_all[7]
+        incoming.astype(wide), unit_three, factor_three, vec_all[7]
     )
     mlp_grad = grad_three.astype(low)
     grad_w_two = contract_rows(mlp_grad, activated).astype(low)
-    act_grad = product(mlp_grad, w_two).astype(low)
+    act_grad = product(after([mlp_grad], [grad_w_two])[0], w_two).astype(low)
     up_grad = (act_grad.astype(wide) * slope).astype(low)
-    grad_w_one = contract_rows(low_two, up_grad).astype(low)
     grad_up_bias = jnp.sum(up_grad.astype(wide), axis=0)
     grad_two, gain_two, shift_two = normalize_back(
         grad_three + contract_cols(up_grad, w_one), unit_two, factor_two, vec_all[5]
     )
     low_grad_two = grad_two.astype(low)
-    cross_grads = rows_to_heads(product(low_grad_two, w_out[1]).astype(low))
-    grad_out_cross = contract_rows(low_grad_two, cross_all).astype(low)
+    cross_grads = product(low_grad_two, w_out[1]).astype(low)
+    (up_late,) = after([up_grad], [cross_grads])
+    grad_w_one = grad_columns([(low_two, up_late)], [], depth)
+    cross_grads = rows_to_heads(cross_grads)
     own_down, own_up = owned(grad_w_two), owned(grad_w_one)
-    out_rows = after(out_rows, [cross_grads])
-    out_rows = jnp.stack(out_rows)[plane ^ jnp.arange(depth)].reshape(row_count, model_width)
-    portion = row_count // groups
-    returned = [pick_rows(out_rows, near[j], portion) for j in range(groups)]
-    cross_q_grad, *enc_terms = cross_bwd(
-        cross_queries,
-        enc_kv,
-        seg,
-        cross_grads,
-        cross_context,
-        cross_lse,
-        [grad_w_two, grad_w_one, grad_out_cross, *returned],
-    )
-    returned = spread(returned, C)
-    enc_passed = relay_start(enc_terms)
-    cross_q_all, *returned = after([heads_to_rows(cross_q_grad), *returned], [own_down])
+    out_rows = from_planes(after([normed_three.astype(low)], [cross_grads])[0])
+    saved = seg, cross_grads, cross_context, cross_lse
+    cross_q_grad, far, *halves = cross_bwd(
+        1, cross_queries, enc_kv, *saved, cross_queries, [grad_w_two, grad_w_one]
+    )
+    enc_passed = relay_start(*halves)
+    cross_q_grad, *enc_terms = cross_bwd(0, cross_queries, enc_kv, *saved, cross_q_grad, [])
+    (cross_q_grad,) = after([cross_q_grad], [*out_rows[1:], *enc_passed, own_down])
+    (cross_q_all,) = after([heads_to_rows(cross_q_grad)], [own_up])
     grad_one, gain_one, shift_one = normalize_back(
         grad_two + contract_cols(cross_q_all, w_cross), unit_one, factor_one, vec_all[3]
     )
     low_grad_one = grad_one.astype(low)
     self_grads = product(low_grad_one, w_out[0]).astype(low)
-    enc_passed = after(enc_passed, [self_grads])
-    cross_q_late, low_grad_late = after([cross_q_all, low_grad_one], [self_grads])
-    self_grads = rows_to_heads(self_grads)
-    enc_terms = relay_finish(relay_join(enc_terms, enc_passed))
-    grad_in_cross = contract_rows(low_one, cross_q_late).astype(low)
-    grad_out_self = contract_rows(low_grad_late, self_all).astype(low)
     grad_vectors = jnp.stack(
         [
             jnp.sum(grad_one, axis=0),
@@ -746,82 +954,71 @@
     )
     vec_part = grad_vectors.reshape(9, shards, -1).transpose(1, 0, 2).reshape(shards, -1)
     up_part = grad_up_bias.reshape(depth, -1, shards).transpose(2, 0, 1)
-    small_part = jnp.concatenate(
-        [
-            by_shard(jnp.concatenate([vec_part, up_part[:, j]], axis=1), shard_rows)
-            for j in range(depth)
-        ],
-        axis=1,
-    ).astype(low)
-    grad_proj = jnp.concatenate([grad_out_self, grad_out_cross, grad_in_cross, small_part], axis=1)
-    down_parts = spread(plane_parts(after([own_down], [self_grads])), T)
+    small_part = [jnp.concatenate([vec_part, up_part[:, j]], axis=1) for j in range(depth)]
+    small_part = jnp.concatenate([by_shard(part, shard_rows) for part in small_part], axis=1)
+    self_grads = rows_to_heads(self_grads)
+    own_down, own_up = after([own_down, own_up], [self_grads])
+    by_plane = by_plane_order([own_up, own_down], plane, depth)
+    ffn = lax.psum_scatter(by_plane, T, scatter_dimension=1, tiled=True)
+    enc_joined = relay_join([*enc_terms, far], enc_passed, [cross_q_all])
+    enc_terms = relay_finish(enc_joined)
     q_grad, *kv_terms = self_bwd(
-        queries,
-        kv,
-        meta,
-        self_grads,
-        self_context,
-        self_lse,
-        [grad_proj],
-    )
-    kv_passed = relay_start(kv_terms)
-
-    kv_joined = relay_join(kv_terms, kv_passed)
-    (grad_proj,) = after([grad_proj], [own_up, q_grad])
+        queries, kv, meta, self_grads, self_context, self_lse, [*enc_joined[1:], by_plane]
+    )
+    kv_passed = relay_start(*kv_terms[3:])
+    (cross_late,) = after([cross_q_all], [q_grad])
+    grad_proj = grad_columns(
+        [(low_grad_two, cross_all), (low_grad_one, self_all), (low_one, cross_late)],
+        [small_part.astype(low)],
+    )
     own_proj = owned(grad_proj)
-    up_parts = spread(plane_parts(after([own_up], [q_grad])), T)
-    enc_terms = after(enc_terms, kv_joined[1:])
-    enc_grad = total(enc_terms).astype(low)
-    width_part = model_width // depth
-    enc_parts = [
-        contract_cols(enc_grad, pick_rows(w_enc, plane ^ j, width_part)).astype(low)
-        for j in range(depth)
-    ]
+    enc_grad, enc_columns = sum_terms(enc_terms, [q_grad])
+
+    enc_parts = plane_shares([enc_grad], w_enc, plane, depth, None, [])
     enc_sent = spread(enc_parts, T)
-    grad_w_enc = contract_rows(encoder, enc_grad).astype(low)
-    result = put_blocks(jnp.concatenate(returned), places, wide)
-    top_all = jnp.max(peaks.reshape(-1, heads, BLK), axis=(0, 2))
-    for axis in (C, F):
-        step = 1
-        while step < lax.axis_size(axis):
-            top_all = jnp.maximum(top_all, swap(top_all, axis, step))
-            step *= 2
-
-    kv_terms = after(relay_finish(kv_joined), [*enc_parts, grad_w_enc, result])
-    kv_grad = total(kv_terms).astype(low)
-    q_natural = jnp.concatenate([pick_rows(q_grad, plane ^ j, rows) for j in range(depth)])
-    qkv_grad = jnp.concatenate([q_natural, kv_grad], axis=1)
-    token_terms = []
-    for j in range(depth):
-        term = contract_cols(qkv_grad, pick_rows(w_self, plane ^ j, width_part))
-        piece = lax.dynamic_slice_in_dim(grad_one, (plane ^ j) * width_part, width_part, 1)
-        piece = piece + pick_rows(term, plane, rows)
-        token_terms.append(
-            lax.dynamic_update_slice_in_dim(term, piece, plane * rows, 0).astype(low)
-        )
-    token_sent = spread(token_terms, T)
-    grad_w_self = contract_rows(tokens, qkv_grad)
+    grad_w_enc = weight_grad(encoder, [enc_grad], [], plane, 512, enc_parts)
+    kv_joined = relay_join(kv_terms, kv_passed, [ffn, grad_w_enc])
+
+    out_rows = after(out_rows, kv_joined[1:])
+    out_rows = jnp.stack(out_rows)[plane ^ jnp.arange(depth)].reshape(row_count, model_width)
+    portion = row_count // groups
+    returned = [pick_rows(out_rows, near[j], portion) for j in range(groups)]
+    ffn = after([ffn], kv_joined[1:])[0].astype(wide)
+    ffn_new = updated(2, ffn[:, :hidden_width]) + updated(3, ffn[:, hidden_width:].T)
+
+    kv_grad, kv_columns = sum_terms(relay_finish(kv_joined), [grad_w_enc, *enc_sent[1:3], *ffn_new, *returned], SOME_COST)
+    returned = spread(after(returned, [kv_grad]), C)
     grad_head_bias = jnp.stack(
         [
             jnp.sum(q_grad.astype(wide), axis=0),
-            jnp.sum(kv_grad[:, head_width:].astype(wide), axis=0),
+            kv_columns[0, head_width:],
             jnp.sum(cross_q_grad.astype(wide), axis=0),
-            jnp.sum(enc_grad[:, head_width:].astype(wide), axis=0),
+            enc_columns[0, head_width:],
         ]
     )
     head_part = grad_head_bias.reshape(4, -1, shards).transpose(2, 0, 1).reshape(shards, -1)
-    grad_first = jnp.concatenate([grad_w_self, by_shard(head_part, shard_rows)], axis=1).astype(low)
-    own_first = owned(grad_first).astype(wide)
-    own_enc = owned(after([grad_w_enc], [grad_first])[0]).astype(wide)
-    down_parts = after(down_parts, [grad_first, *token_terms])
-    ffn_new = updated(2, total(up_parts)) + updated(3, total(down_parts).T)
-    proj_parts = [own_proj[:, i * all_heads : (i + 1) * all_heads] for i in range(3)]
-    proj_parts = plane_parts(proj_parts + [own_proj[:, 3 * all_heads :]])
-    proj = total(spread(after(proj_parts, [grad_first, *token_terms]), T))
-    grad_encoder = total(enc_sent)
+    head_part = by_shard(head_part, shard_rows).astype(low)
+    adds = [head_part, grad_w_enc]
+    grad_first = weight_grad(tokens, [q_grad, kv_grad], adds, plane, rows, [], SOME_COST)
+    (grad_first,) = after([grad_first], [own_proj])
+    token_terms = plane_shares(
+        [q_grad, kv_grad], w_kept, plane, depth, grad_one, [grad_first, *enc_sent[3:]], SOME_COST
+    )
+    token_sent = spread(token_terms, T)
+    own_first = owned(grad_first)
+    cuts = [0, all_heads, 2 * all_heads, 3 * all_heads, own_proj.shape[1]]
+    own_proj = [own_proj[:, a:b] for a, b in zip(cuts, cuts[1:])]
+    proj_parts = [column_blocks(part, depth) for part in own_proj]
+    proj_parts = [jnp.concatenate([p[j] for p in proj_parts], axis=1) for j in range(depth)]
+    own_first, *proj_parts = after([own_first, *proj_parts], token_sent[1:])
+    own_first = own_first.astype(wide)
+    proj = total(spread(proj_parts, T))
+    result = put_blocks(jnp.concatenate(returned), places, wide)
+    (token_sent[0],) = after(token_sent[:1], [result])
     grad_tokens = total(token_sent)
-
-    out_self, out_cross, in_cross = [
+    grad_encoder = total(after(enc_sent, [result]))
+
+    out_cross, out_self, in_cross = [
         proj[:, i * head_width : (i + 1) * head_width] for i in range(3)
     ]
     small_part = proj[:, 3 * head_width :].reshape(-1)
@@ -829,10 +1026,10 @@
         0: jnp.stack(
             column_blocks(own_first[:, : 3 * head_width], 3)
             + [in_cross]
-            + column_blocks(own_enc, 2)
+            + column_blocks(own_first[:, 3 * head_width + 128 :], 2)
         ),
         1: jnp.stack([out_self.T, out_cross.T]),
-        4: own_first[:, 3 * head_width :].reshape(-1)[:n_head].reshape(head_bias.shape),
+        4: own_first[:, 3 * head_width : 3 * head_width + 128].reshape(-1)[:n_head].reshape(head_bias.shape),
         5: small_part[n_vec : n_vec + n_up].reshape(up_bias.shape),
         6: small_part[:n_vec].reshape(vectors.shape),
     }

time: 901 us -> 802 us (0.89)
  Pallas kernels: 195 us -> 267 us
  starting transfers between devices: 150 us -> 96.1 us
  waiting for transfers between devices: 251 us -> 212 us
  matrix products: 94.9 us -> 64.2 us
  local copies, waits for them, and re-layouts: 101 us -> 71.7 us
  other arithmetic: 80 us -> 55.5 us
    pallas_call x1 -> x15, Pallas kernels: 72.7 us -> 148 us  [the longest x2 80.3 us: cross_bwd(): pl.pallas_call(partial(cross_bwd_body, heads, bounds, kind, step), grid_s...]
    ppermute x64 -> x58, starting transfers between devices: 138 us -> 84.5 us  [swap(): lax.ppermute(value, axis, [(i, i ^ j) for i in range(lax.axis_size(axis))])]
    ppermute x64 -> x58, waiting for transfers between devices: 250 us -> 203 us  [swap(): lax.ppermute(value, axis, [(i, i ^ j) for i in range(lax.axis_size(axis))])]
    dot_general x7 -> x1, matrix products: 25 us -> 5.78 us  [contract_rows(): lax.dot_general(left_side, right_side, (((0,), (0,)), ((), ())), preferre...]
    convert_element_type x12 -> x7, other arithmetic: 14.2 us -> 1.85 us  [the longest x1 1.1 us: per_device(): own_first = own_first.astype(wide)]
    unnamed x314 -> x257, local copies, waits for them, and re-layouts: 44.3 us -> 32 us
    dot_general x13 -> x5, matrix products: 33.7 us -> 24.4 us  [contract_cols(): lax.dot_general(left_side, right_side, (((1,), (1,)), ((), ())), preferre...]
  transfers between devices with their start and end apart: 77 -> 71, of which waited for: 24 -> 34; matrix products, arithmetic and copies ran while one was open for 26% -> 18% of each run, Pallas kernels for 22% -> 33%
where the time goes in v1:
time: 802 us; the launch traced here: 790 us
  Pallas kernels  267 us (33%)
  waiting for transfers between devices  212 us (26%)
  starting transfers between devices  96.1 us (12%)
  local copies, waits for them, and re-layouts  71.7 us (9%)
  matrix products  64.2 us (8%)
  other arithmetic  55.5 us (7%)
  between operations  24.1 us (3%)
    ppermute x58, waiting for transfers between devices, swap(): lax.ppermute(value, axis, [(i, i ^ j) for i in range(lax.axis_size(axis))])  203 us
    ppermute x58, starting transfers between devices, swap(): lax.ppermute(value, axis, [(i, i ^ j) for i in range(lax.axis_size(axis))])  84.5 us
    pallas_call x2, Pallas kernels, cross_bwd(): pl.pallas_call(partial(cross_bwd_body, heads, bounds, kind, step), grid_s...  80.3 us
    pallas_call x1, Pallas kernels, cross_fwd(): pl.pallas_call(partial(cross_fwd_body, heads, bounds), grid_spec=pltpu.Pr...  43.5 us
    pallas_call x1, Pallas kernels, self_bwd(): pl.pallas_call(partial(self_bwd_body, heads, bounds, len(others)), grid_s...  35.9 us
    dot_general x7, matrix products, product(): return jnp.dot(left_side, right_side, preferred_element_type=jnp.float32)  34 us
    pallas_call x1, Pallas kernels, self_fwd(): pl.pallas_call(partial(self_fwd_body, heads, bounds), grid_spec=pltpu.Pre...  32.7 us
    unnamed x257, local copies, waits for them, and re-layouts  32 us
  transfers between devices with their start and end apart: 71, of which 34 were waited for; matrix products, arithmetic and copies ran while one was open for 18% of the time, Pallas kernels for 33%

profile of v1, /device:TPU:0, one launch (start us, length us, event | category | flops | bytes accessed | tf_op | source)
XLA Modules:
  0.0 790.3 jit_solution(7012711892982309667)
XLA Ops:
  17.6 6.5 collective-permute-done.4.refs_1_
  24.1 9.5 %collective-permute-done.5.refs_2_ = bf16[128,896]{1,0:T(8,128)(2,1)S(1)} collective-permute-done((bf16[128,896]{1,0:T(8,128)(2,1)S(1)}, bf16[128,896]{1,0:T(8,128)(2,1)S(1)}, u32[]{:S(2)}, u32[]{:S(2)}) %collective-permute-start.5) | collective-permute-done | bytes 229408 | tf_op jit(solution)/shard_map/ppermute | solution.py:683
  70.1 8.4 %collective-permute-done.1.refs_2_ = bf16[1024,512]{1,0:T(8,128)(2,1)S(1)} collective-permute-done((bf16[1024,512]{1,0:T(8,128)(2,1)S(1)}, bf16[1024,512]{1,0:T(8,128)(2,1)S(1)}, u32[]{:S(2)}, u32[]{:S(2)}) %collective-permute-start.1) | collective-permute-done | bytes 1048608 | tf_op jit(solution)/shard_map/ppermute | solution.py:683
  82.8 5.9 fusion.7.refs_3_.refs_0_
  88.7 11.9 %collective-permute-done.2.refs_0_ = bf16[512,512]{1,0:T(8,128)(2,1)S(1)} collective-permute-done((bf16[512,512]{1,0:T(8,128)(2,1)S(1)}, bf16[512,512]{1,0:T(8,128)(2,1)S(1)}, u32[]{:S(2)}, u32[]{:S(2)}) %collective-permute-start.2) | collective-permute-done | bytes 524320 | tf_op jit(solution)/shard_map/ppermute | solution.py:683
  126.2 32.7 %self_fwd.1 = (bf16[1024,256]{1,0:T(8,128)(2,1)}, f32[8,1,512]{2,1,0:T(1,128)}, f32[8,1,512]{2,1,0:T(1,128)}) custom-call(s32[8,8]{1,0:T(8,128)} %concatenate.119.meta_ref, bf16[1024,256]{1,0:T(8,128)(2,1)} %pad_maximum_fusion.5.q_ref, bf16[1024,512]{1,0:T(8,128)(2,1)} %copy-done, bf16[1024,512]{1,0:T(8,128)(2,1)} %collective-permute-done.refs_1_, ...), custom_call_target="tpu_custom_call" | custom-call | tf_op jit(solution)/shard_map/self_fwd/pallas_call | solution.py:334
  167.1 7.7 collective-permute-done.8
  175.6 8.2 %collective-permute-done.13.refs_0_ = bf16[2048,512]{1,0:T(8,128)(2,1)S(1)} collective-permute-done((bf16[2048,512]{1,0:T(8,128)(2,1)}, bf16[2048,512]{1,0:T(8,128)(2,1)S(1)}, u32[]{:S(2)}, u32[]{:S(2)}) %collective-permute-start.13) | collective-permute-done | bytes 2097184 | tf_op jit(solution)/shard_map/ppermute | solution.py:683
  216.6 17.8 %collective-permute-done.17 = f32[4]{0:T(128)S(1)} collective-permute-done((f32[4]{0:T(128)S(1)}, f32[4]{0:T(128)S(1)}, u32[]{:S(2)}, u32[]{:S(2)}) %collective-permute-start.17) | collective-permute-done | bytes 48 | tf_op jit(solution)/shard_map/ppermute | solution.py:683
  240.9 43.5 %cross_fwd.1 = (bf16[1024,256]{1,0:T(8,128)(2,1)}, f32[8,1,512]{2,1,0:T(1,128)}) custom-call(s32[5,8]{1,0:T(8,128)} %stack.99.seg_ref, bf16[1024,256]{1,0:T(8,128)(2,1)} %pad_maximum_fusion.7.refs_1_.refs_2_.q_ref.refs_3_, bf16[2048,512]{1,0:T(8,128)(2,1)} %gate.27.refs_0_, bf16[2048,512]{1,0:T(8,128)(2,1)} %get-tuple-element.99.refs_1_, ...), custom_call_target="tpu_custom_call" | custom-call | tf_op jit(solution)/shard_map/cross_fwd/pallas_call | solution.py:169
  305.4 8.4 %multiply_convert_fusion = (bf16[256,4096]{1,0:T(8,128)(2,1)}, f32[256,4096]{1,0:T(8,128)}) fusion(f32[4096]{0:T(1024)S(1)} %add.655, bf16[256,1024]{1,0:T(8,128)(2,1)S(1)} %fusion.58.refs_0_, bf16[1024,4096]{1,0:T(8,128)(2,1)} %all-gather.12.cloned.1.call-done), kind=kOutput, calls=%fused_computation.14 | convolution fusion | flops 2153775104 | bytes 15220736 | tf_op jit(solution)/shard_map/dot_general | solution.py:31
  313.8 6.6 fusion.132
  331.1 7.3 fusion.133
  338.4 9.0 %multiply_reduce_fusion = (bf16[1024]{0:T(1024)(128)(2,1)}, f32[256]{0:T(256)S(1)}, f32[256]{0:T(256)S(1)}, bf16[1024]{0:T(1024)(128)(2,1)}, f32[256,1024]{1,0:T(8,128)S(1)}) fusion(f32[256,1024]{1,0:T(8,128)S(1)} %get-tuple-element.456, f32[256]{0:T(256)S(1)} %add_rsqrt_fusion.1, f32[256]{0:T(256)S(1)} %broadcast_multiply_fusion.7, ...), kind=kOutput, calls=%fused_computation.66 | convolution fusion | flops 2150102528 | bytes 13643776 | tf_op jit(solution)/shard_map/dot_general | solution.py:41
  352.8 7.0 grad_columns.2.refs_5_
  374.6 54.6 %cross_bwd.2 = (bf16[1024,256]{1,0:T(8,128)(2,1)}, bf16[2048,512]{1,0:T(8,128)(2,1)}, bf16[1024,512]{1,0:T(8,128)(2,1)}, bf16[1024,512]{1,0:T(8,128)(2,1)}) custom-call(s32[5,8]{1,0:T(8,128)} %stack.99.seg_ref, bf16[1024,256]{1,0:T(8,128)(2,1)} %pad_maximum_fusion.7.refs_1_.refs_2_.q_ref.refs_3_, bf16[1024,256]{1,0:T(8,128)(2,1)} %pad_maximum_fusion.14.refs_1_.g_ref, ...), custom_call_target="tpu_custom_call" | custom-call | tf_op jit(solution)/shard_map/cross_bwd/pallas_call | solution.py:255
  434.5 25.7 %cross_bwd.3 = (bf16[1024,256]{1,0:T(8,128)(2,1)}, bf16[2048,512]{1,0:T(8,128)(2,1)}, bf16[2048,512]{1,0:T(8,128)(2,1)}) custom-call(s32[5,8]{1,0:T(8,128)} %stack.99.seg_ref, bf16[1024,256]{1,0:T(8,128)(2,1)} %pad_maximum_fusion.7.refs_1_.refs_2_.q_ref.refs_3_, bf16[1024,256]{1,0:T(8,128)(2,1)} %pad_maximum_fusion.14.refs_1_.g_ref, ...), custom_call_target="tpu_custom_call" | custom-call | tf_op jit(solution)/shard_map/cross_bwd/pallas_call | solution.py:255
  460.3 8.3 %collective-permute-done.33.refs_2_ = bf16[256,1024]{1,0:T(8,128)(2,1)S(1)} collective-permute-done((bf16[256,1024]{1,0:T(8,128)(2,1)}, bf16[256,1024]{1,0:T(8,128)(2,1)S(1)}, u32[]{:S(2)}, u32[]{:S(2)}) %collective-permute-start.33) | collective-permute-done | bytes 524320 | tf_op jit(solution)/shard_map/ppermute | solution.py:683
  468.6 6.6 collective-permute-done.35.refs_4_.passed_ref
  511.5 6.3 collective-permute-done.41
  547.6 35.9 %self_bwd.1 = (bf16[1024,256]{1,0:T(8,128)(2,1)}, bf16[1024,512]{1,0:T(8,128)(2,1)}, bf16[1024,512]{1,0:T(8,128)(2,1)}, bf16[1024,512]{1,0:T(8,128)(2,1)}, bf16[...) custom-call(s32[8,8]{1,0:T(8,128)} %concatenate.119.meta_ref, bf16[1024,256]{1,0:T(8,128)(2,1)} %pad_maximum_fusion.5.q_ref, ...), custom_call_target="tpu_custom_call" | custom-call | tf_op jit(solution)/shard_map/self_bwd/pallas_call | solution.py:411
  583.5 7.1 grad_columns.3
  594.8 7.1 sum_terms.2
  602.0 7.9 %plane_shares.2 = (bf16[2048,256]{1,0:T(8,128)(2,1)}, bf16[2048,256]{1,0:T(8,128)(2,1)}, bf16[2048,256]{1,0:T(8,128)(2,1)}, bf16[2048,256]{1,0:T(8,128)(2,1)}) custom-call(s32[1]{0:T(128)} %bitcast.63.plane_ref, bf16[2048,512]{1,0:T(8,128)(2,1)} %get-tuple-element.127.refs_0_, bf16[1024,512]{1,0:T(8,128)(2,1)} %gate.25.refs_1_.refs_2_.refs_3_.refs_4_, ...), custom_call_target="tpu_custom_call" | custom-call | flops 20000000000 | bytes 33554432 | tf_op jit(solution)/shard_map/plane_shares/pallas_call | solution.py:596
  614.3 6.5 weight_grad.2.refs_1_.refs_3_
  646.5 8.0 %collective-permute-done.49.refs_4_.refs_1_ = bf16[2048,256]{1,0:T(8,128)(2,1)} collective-permute-done((bf16[2048,256]{1,0:T(8,128)(2,1)}, bf16[2048,256]{1,0:T(8,128)(2,1)}, u32[]{:S(2)}, u32[]{:S(2)}) %collective-permute-start.49) | collective-permute-done | bytes 1048608 | tf_op jit(solution)/shard_map/ppermute | solution.py:683
  654.5 27.7 %collective-permute-done.50.refs_5_.refs_2_ = bf16[2048,256]{1,0:T(8,128)(2,1)} collective-permute-done((bf16[2048,256]{1,0:T(8,128)(2,1)}, bf16[2048,256]{1,0:T(8,128)(2,1)}, u32[]{:S(2)}, u32[]{:S(2)}) %collective-permute-start.50) | collective-permute-done | bytes 1048608 | tf_op jit(solution)/shard_map/ppermute | solution.py:683
  690.7 6.9 weight_grad.3.refs_0_
  704.2 6.8 put_blocks.1.refs_1_.refs_4_
  710.9 5.9 plane_shares.3
  729.2 16.8 %collective-permute-done.56.refs_6_ = bf16[1024,256]{1,0:T(8,128)(2,1)S(1)} collective-permute-done((bf16[1024,256]{1,0:T(8,128)(2,1)}, bf16[1024,256]{1,0:T(8,128)(2,1)S(1)}, u32[]{:S(2)}, u32[]{:S(2)}) %collective-permute-start.56) | collective-permute-done | bytes 524320 | tf_op jit(solution)/shard_map/ppermute | solution.py:683
  759.8 12.6 %collective-permute-done.59 = bf16[128,896]{1,0:T(8,128)(2,1)S(1)} collective-permute-done((bf16[128,896]{1,0:T(8,128)(2,1)}, bf16[128,896]{1,0:T(8,128)(2,1)S(1)}, u32[]{:S(2)}, u32[]{:S(2)}) %collective-permute-start.59) | collective-permute-done | bytes 229408 | tf_op jit(solution)/shard_map/ppermute | solution.py:683
  (630 shorter events, 325.1 us)
Async XLA Ops:
  7.2 38.8 %all-gather.6.cloned.1.call-start = ((), (), s32[]{:S(2)}) async-start(), calls=%async_computation.5 | async-start | bytes 2064384 | tf_op jit(solution)/shard_map/all_gather | solution.py:757
  10.8 59.3 %all-gather.8.cloned.1.call-start = ((), (), s32[]{:S(2)}) async-start(), calls=%async_computation.6 | async-start | bytes 1179648 | tf_op jit(solution)/shard_map/all_gather | solution.py:770
  37.5 153.1 %all-gather.10.cloned.1.call-start = ((), (), s32[]{:S(2)}) async-start(), calls=%async_computation.7 | async-start | bytes 8257536 | tf_op jit(solution)/shard_map/all_gather | solution.py:832
  46.0 259.4 %all-gather.12.cloned.1.call-start = ((), (), s32[]{:S(2)}) async-start(), calls=%async_computation.8 | async-start | bytes 9437184 | tf_op jit(solution)/shard_map/all_gather | solution.py:836
  56.6 46.2 %collective-permute-start.23 = (bf16[128,2048]{1,0:T(8,128)(2,1)}, bf16[128,2048]{1,0:T(8,128)(2,1)S(1)}, u32[]{:S(2)}, u32[]{:S(2)}) collective-permute-start(bf16[128,2048]{1,0:T(8,128)(2,1)} %gate.31.refs_0_), channel_id=1, source_target_pairs={{0,1},{1,0},{2,3},{3,2},{4,5},{5,4},{6,7},{7,6},{8,9},{9,8},{10,11... | collective-permute-start | bytes 1572872 | tf_op jit(solution)/shard_map/ppermute | solution.py:683
  60.0 42.7 %collective-permute-start.24 = (bf16[128,2048]{1,0:T(8,128)(2,1)}, bf16[128,2048]{1,0:T(8,128)(2,1)}, u32[]{:S(2)}, u32[]{:S(2)}) collective-permute-start(bf16[128,2048]{1,0:T(8,128)(2,1)} %gate.31.refs_0_), channel_id=1, source_target_pairs={{0,2},{1,3},{2,0},{3,1},{4,6},{5,7},{6,4},{7,5},{8,10},{9,11},{10,... | collective-permute-start | bytes 1572872 | tf_op jit(solution)/shard_map/ppermute | solution.py:683
  61.1 41.7 %collective-permute-start.25 = (bf16[128,2048]{1,0:T(8,128)(2,1)}, bf16[128,2048]{1,0:T(8,128)(2,1)}, u32[]{:S(2)}, u32[]{:S(2)}) collective-permute-start(bf16[128,2048]{1,0:T(8,128)(2,1)} %gate.31.refs_0_), channel_id=1, source_target_pairs={{0,3},{1,2},{2,1},{3,0},{4,7},{5,6},{6,5},{7,4},{8,11},{9,10},{10,... | collective-permute-start | bytes 1572872 | tf_op jit(solution)/shard_map/ppermute | solution.py:683
  106.3 207.5 %all-gather.14.cloned.1.call-start = ((), (), s32[]{:S(2)}) async-start(), calls=%async_computation.9 | async-start | bytes 9437184 | tf_op jit(solution)/shard_map/all_gather | solution.py:838
  107.4 370.1 %reduce-scatter.6.cloned.1.call-start = ((), (), s32[]{:S(2)}) async-start(), calls=%async_computation.10 | async-start | bytes 9437184 | tf_op jit(solution)/shard_map/reduce_scatter | solution.py:859
  111.7 72.1 %collective-permute-start.13 = (bf16[2048,512]{1,0:T(8,128)(2,1)}, bf16[2048,512]{1,0:T(8,128)(2,1)S(1)}, u32[]{:S(2)}, u32[]{:S(2)}) collective-permute-start(bf16[2048,512]{1,0:T(8,128)(2,1)} %gate.27.refs_0_), channel_id=1, source_target_pairs={{0,4},{4,0},{8,12},{12,8},{1,5},{5,1},{9,13},{13,9},{2,6},{6,2},{1... | collective-permute-start | bytes 6291464 | tf_op jit(solution)/shard_map/ppermute | solution.py:683
  112.3 71.6 %collective-permute-start.14 = (bf16[2048,512]{1,0:T(8,128)(2,1)}, bf16[2048,512]{1,0:T(8,128)(2,1)}, u32[]{:S(2)}, u32[]{:S(2)}) collective-permute-start(bf16[2048,512]{1,0:T(8,128)(2,1)} %gate.27.refs_0_), channel_id=1, source_target_pairs={{0,8},{4,12},{8,0},{12,4},{1,9},{5,13},{9,1},{13,5},{2,10},{6,14},... | collective-permute-start | bytes 6291464 | tf_op jit(solution)/shard_map/ppermute | solution.py:683
  187.6 52.0 %collective-permute-start.15 = (bf16[1024,512]{1,0:T(8,128)(2,1)}, bf16[1024,512]{1,0:T(8,128)(2,1)S(1)}, u32[]{:S(2)}, u32[]{:S(2)}) collective-permute-start(bf16[1024,512]{1,0:T(8,128)(2,1)} %slice.524), channel_id=1, source_target_pairs={{0,4},{4,0},{8,12},{12,8},{1,5},{5,1},{9,13},{13,9},{2,6},{6,2},{1... | collective-permute-start | bytes 3145736 | tf_op jit(solution)/shard_map/ppermute | solution.py:683
  189.0 50.6 %collective-permute-start.16 = (bf16[1024,512]{1,0:T(8,128)(2,1)}, bf16[1024,512]{1,0:T(8,128)(2,1)S(1)}, u32[]{:S(2)}, u32[]{:S(2)}) collective-permute-start(bf16[1024,512]{1,0:T(8,128)(2,1)} %slice.525), channel_id=1, source_target_pairs={{0,8},{4,12},{8,0},{12,4},{1,9},{5,13},{9,1},{13,5},{2,10},{6,14},... | collective-permute-start | bytes 3145736 | tf_op jit(solution)/shard_map/ppermute | solution.py:683
  292.6 28.1 %collective-permute-start.28 = (bf16[256,1024]{1,0:T(8,128)(2,1)}, bf16[256,1024]{1,0:T(8,128)(2,1)S(1)}, u32[]{:S(2)}, u32[]{:S(2)}) collective-permute-start(bf16[256,1024]{1,0:T(8,128)(2,1)} %get-tuple-element.112), channel_id=1, source_target_pairs={{0,12},{5,9},{10,6},{15,3},{16,28},{21,25},{26,22},{31,19}} | collective-permute-start | bytes 1572872 | tf_op jit(solution)/shard_map/ppermute | solution.py:898
  330.8 165.0 %reduce-scatter.8.cloned.1.call-start = ((), (), s32[]{:S(2)}) async-start(), calls=%async_computation.11 | async-start | bytes 9437184 | tf_op jit(solution)/shard_map/reduce_scatter | solution.py:859
  359.8 261.0 %reduce-scatter.10.cloned.1.call-start = ((), (), s32[]{:S(2)}) async-start(), calls=%async_computation.12 | async-start | bytes 2621440 | tf_op jit(solution)/shard_map/reduce_scatter | solution.py:962
  429.2 46.0 %collective-permute-start.35 = (bf16[1024,512]{1,0:T(8,128)(2,1)}, bf16[1024,512]{1,0:T(8,128)(2,1)}, u32[]{:S(2)}, u32[]{:S(2)}) collective-permute-start(bf16[1024,512]{1,0:T(8,128)(2,1)} %get-tuple-element.116), channel_id=1, source_target_pairs={{0,4},{4,0},{8,12},{12,8},{1,5},{5,1},{9,13},{13,9},{2,6},{6,2},{1... | collective-permute-start | bytes 3145736 | tf_op jit(solution)/shard_map/ppermute | solution.py:683
  430.1 47.4 %collective-permute-start.36 = (bf16[1024,512]{1,0:T(8,128)(2,1)}, bf16[1024,512]{1,0:T(8,128)(2,1)}, u32[]{:S(2)}, u32[]{:S(2)}) collective-permute-start(bf16[1024,512]{1,0:T(8,128)(2,1)} %get-tuple-element.117), channel_id=1, source_target_pairs={{0,8},{4,12},{8,0},{12,4},{1,9},{5,13},{9,1},{13,5},{2,10},{6,14},... | collective-permute-start | bytes 3145736 | tf_op jit(solution)/shard_map/ppermute | solution.py:683
  430.1 30.1 %collective-permute-start.32 = (bf16[256,1024]{1,0:T(8,128)(2,1)}, bf16[256,1024]{1,0:T(8,128)(2,1)S(1)}, u32[]{:S(2)}, u32[]{:S(2)}) collective-permute-start(bf16[256,1024]{1,0:T(8,128)(2,1)} %gate.35.refs_0_), channel_id=1, source_target_pairs={{0,1},{1,0},{2,3},{3,2},{4,5},{5,4},{6,7},{7,6},{8,9},{9,8},{10,11... | collective-permute-start | bytes 1572872 | tf_op jit(solution)/shard_map/ppermute | solution.py:683
  430.1 38.4 %collective-permute-start.33 = (bf16[256,1024]{1,0:T(8,128)(2,1)}, bf16[256,1024]{1,0:T(8,128)(2,1)S(1)}, u32[]{:S(2)}, u32[]{:S(2)}) collective-permute-start(bf16[256,1024]{1,0:T(8,128)(2,1)} %gate.35.refs_0_), channel_id=1, source_target_pairs={{0,2},{1,3},{2,0},{3,1},{4,6},{5,7},{6,4},{7,5},{8,10},{9,11},{10,... | collective-permute-start | bytes 1572872 | tf_op jit(solution)/shard_map/ppermute | solution.py:683
  431.0 37.5 %collective-permute-start.34 = (bf16[256,1024]{1,0:T(8,128)(2,1)}, bf16[256,1024]{1,0:T(8,128)(2,1)S(1)}, u32[]{:S(2)}, u32[]{:S(2)}) collective-permute-start(bf16[256,1024]{1,0:T(8,128)(2,1)} %gate.35.refs_0_), channel_id=1, source_target_pairs={{0,3},{1,2},{2,1},{3,0},{4,7},{5,6},{6,5},{7,4},{8,11},{9,10},{10,... | collective-permute-start | bytes 1572872 | tf_op jit(solution)/shard_map/ppermute | solution.py:683
  522.5 181.7 %reduce-scatter.12.cloned.1.call-start = ((), (), s32[]{:S(2)}) async-start(), calls=%async_computation.13 | async-start | bytes 8257536 | tf_op jit(solution)/shard_map/reduce_scatter | solution.py:859
  536.6 58.2 %collective-permute-start.44 = (bf16[2048,512]{1,0:T(8,128)(2,1)}, bf16[2048,512]{1,0:T(8,128)(2,1)}, u32[]{:S(2)}, u32[]{:S(2)}) collective-permute-start(bf16[2048,512]{1,0:T(8,128)(2,1)} %add_half.4.refs_5_), channel_id=1, source_target_pairs={{0,4},{4,0},{8,12},{12,8},{1,5},{5,1},{9,13},{13,9},{2,6},{6,2},{1... | collective-permute-start | bytes 6291464 | tf_op jit(solution)/shard_map/ppermute | solution.py:683
  541.7 53.1 %collective-permute-start.45 = (bf16[2048,512]{1,0:T(8,128)(2,1)}, bf16[2048,512]{1,0:T(8,128)(2,1)}, u32[]{:S(2)}, u32[]{:S(2)}) collective-permute-start(bf16[2048,512]{1,0:T(8,128)(2,1)} %add_half.5.refs_6_), channel_id=1, source_target_pairs={{0,8},{4,12},{8,0},{12,4},{1,9},{5,13},{9,1},{13,5},{2,10},{6,14},... | collective-permute-start | bytes 6291464 | tf_op jit(solution)/shard_map/ppermute | solution.py:683
  590.6 157.3 %reduce-scatter.14.cloned.1.call-start = ((), (), s32[]{:S(2)}) async-start(), calls=%async_computation.14 | async-start | bytes 3244032 | tf_op jit(solution)/shard_map/reduce_scatter | solution.py:859
  592.3 28.5 %collective-permute-start.43 = (bf16[512,512]{1,0:T(8,128)(2,1)S(1)}, bf16[512,512]{1,0:T(8,128)(2,1)S(1)}, u32[]{:S(2)}, u32[]{:S(2)}) collective-permute-start(bf16[512,512]{1,0:T(8,128)(2,1)S(1)} %copy-done.103), channel_id=1, source_target_pairs={{0,8},{4,12},{8,0},{12,4},{1,9},{5,13},{9,1},{13,5},{2,10},{6,14},... | collective-permute-start | bytes 1572872 | tf_op jit(solution)/shard_map/ppermute | solution.py:683
  594.6 30.9 %collective-permute-start.46 = (bf16[512,512]{1,0:T(8,128)(2,1)S(1)}, bf16[512,512]{1,0:T(8,128)(2,1)S(1)}, u32[]{:S(2)}, u32[]{:S(2)}) collective-permute-start(bf16[512,512]{1,0:T(8,128)(2,1)S(1)} %copy-done.102), channel_id=1, source_target_pairs={{0,4},{4,0},{8,12},{12,8},{1,5},{5,1},{9,13},{13,9},{2,6},{6,2},{1... | collective-permute-start | bytes 1572872 | tf_op jit(solution)/shard_map/ppermute | solution.py:683
  609.9 44.6 %collective-permute-start.49 = (bf16[2048,256]{1,0:T(8,128)(2,1)}, bf16[2048,256]{1,0:T(8,128)(2,1)}, u32[]{:S(2)}, u32[]{:S(2)}) collective-permute-start(bf16[2048,256]{1,0:T(8,128)(2,1)} %get-tuple-element.129.refs_2_), channel_id=1, source_target_pairs={{0,1},{1,0},{2,3},{3,2},{4,5},{5,4},{6,7},{7,6},{8,9},{9,8},{10,11... | collective-permute-start | bytes 3145736 | tf_op jit(solution)/shard_map/ppermute | solution.py:683
  609.9 72.3 %collective-permute-start.50 = (bf16[2048,256]{1,0:T(8,128)(2,1)}, bf16[2048,256]{1,0:T(8,128)(2,1)}, u32[]{:S(2)}, u32[]{:S(2)}) collective-permute-start(bf16[2048,256]{1,0:T(8,128)(2,1)} %get-tuple-element.130.refs_3_), channel_id=1, source_target_pairs={{0,2},{1,3},{2,0},{3,1},{4,6},{5,7},{6,4},{7,5},{8,10},{9,11},{10,... | collective-permute-start | bytes 3145736 | tf_op jit(solution)/shard_map/ppermute | solution.py:683
  611.8 99.1 %collective-permute-start.54 = (bf16[2048,256]{1,0:T(8,128)(2,1)}, bf16[2048,256]{1,0:T(8,128)(2,1)}, u32[]{:S(2)}, u32[]{:S(2)}) collective-permute-start(bf16[2048,256]{1,0:T(8,128)(2,1)} %get-tuple-element.131.refs_4_), channel_id=1, source_target_pairs={{0,3},{1,2},{2,1},{3,0},{4,7},{5,6},{6,5},{7,4},{8,11},{9,10},{10,... | collective-permute-start | bytes 3145736 | tf_op jit(solution)/shard_map/ppermute | solution.py:683
  623.5 58.7 %collective-permute-start.47 = (bf16[1024,512]{1,0:T(8,128)(2,1)}, bf16[1024,512]{1,0:T(8,128)(2,1)}, u32[]{:S(2)}, u32[]{:S(2)}) collective-permute-start(bf16[1024,512]{1,0:T(8,128)(2,1)} %add_half.6.refs_4_.refs_1_), channel_id=1, source_target_pairs={{0,4},{4,0},{8,12},{12,8},{1,5},{5,1},{9,13},{13,9},{2,6},{6,2},{1... | collective-permute-start | bytes 3145736 | tf_op jit(solution)/shard_map/ppermute | solution.py:683
  628.3 54.0 %collective-permute-start.48 = (bf16[1024,512]{1,0:T(8,128)(2,1)}, bf16[1024,512]{1,0:T(8,128)(2,1)}, u32[]{:S(2)}, u32[]{:S(2)}) collective-permute-start(bf16[1024,512]{1,0:T(8,128)(2,1)} %add_half.7.refs_5_.refs_2_), channel_id=1, source_target_pairs={{0,8},{4,12},{8,0},{12,4},{1,9},{5,13},{9,1},{13,5},{2,10},{6,14},... | collective-permute-start | bytes 3145736 | tf_op jit(solution)/shard_map/ppermute | solution.py:683
  (145 other events, 1320.6 us)
Sparse Core Ops, SparseCore 0:
  10.9 29.4 all-gather.5
  42.9 27.1 all-gather.7
  72.0 72.0 all-gather.9
  145.8 89.6 all-gather.11
  237.2 53.7 all-gather.13
  331.0 71.4 reduce-scatter.5
  406.3 89.4 reduce-scatter.7
  522.6 45.5 reduce-scatter.9
  590.7 86.0 reduce-scatter.11
  704.3 43.5 reduce-scatter.13

commit v2 on v1

--- a/solution.py
+++ b/solution.py
@@ -247,7 +247,7 @@
 
 def cross_bwd(kind, queries, enc_kv, seg, grads, context, lse, prior, others):
     count, width = queries.shape
-    heads, blocks, step = width // HEAD, count // BLK, 512
+    heads, blocks, step = width // HEAD, count // BLK, 2048
     bounds = piece_bounds(enc_kv)
     picked = [(0, 1), (2, 3, 4)][kind]
     pieces, bounds = [enc_kv[i] for i in picked], [bounds[i] for i in picked]
@@ -986,7 +986,7 @@
     ffn = after([ffn], kv_joined[1:])[0].astype(wide)
     ffn_new = updated(2, ffn[:, :hidden_width]) + updated(3, ffn[:, hidden_width:].T)
 
-    kv_grad, kv_columns = sum_terms(relay_finish(kv_joined), [grad_w_enc, *enc_sent[1:3], *ffn_new, *returned], SOME_COST)
+    kv_grad, kv_columns = sum_terms(relay_finish(kv_joined), [grad_w_enc, enc_sent[1], *ffn_new, *returned], SOME_COST)
     returned = spread(after(returned, [kv_grad]), C)
     grad_head_bias = jnp.stack(
         [
@@ -1002,7 +1002,7 @@
     grad_first = weight_grad(tokens, [q_grad, kv_grad], adds, plane, rows, [], SOME_COST)
     (grad_first,) = after([grad_first], [own_proj])
     token_terms = plane_shares(
-        [q_grad, kv_grad], w_kept, plane, depth, grad_one, [grad_first, *enc_sent[3:]], SOME_COST
+        [q_grad, kv_grad], w_kept, plane, depth, grad_one, [grad_first, *enc_sent[2:]], SOME_COST
     )
     token_sent = spread(token_terms, T)
     own_first = owned(grad_first)

time: 802 us -> 800 us (level)
  starting transfers between devices: 96.1 us -> 119 us
  waiting for transfers between devices: 212 us -> 190 us
    ppermute x58, waiting for transfers between devices: 203 us -> 184 us  [swap(): lax.ppermute(value, axis, [(i, i ^ j) for i in range(lax.axis_size(axis))])]
    ppermute x58, starting transfers between devices: 84.5 us -> 99.5 us  [swap(): lax.ppermute(value, axis, [(i, i ^ j) for i in range(lax.axis_size(axis))])]
    reduce_scatter x4, starting transfers between devices: 1.54 us -> 12.9 us  [owned(): lax.psum_scatter(gradient.astype(low), SHARD, scatter_dimension=0, tiled=...]
  transfers between devices with their start and end apart: 71 -> 71, of which waited for: 34 -> 31; matrix products, arithmetic and copies ran while one was open for 18% -> 18% of each run, Pallas kernels for 33% -> 33%
where the time goes in v2:
time: 800 us; the launch traced here: 795 us
  Pallas kernels  270 us (34%)
  waiting for transfers between devices  190 us (24%)
  starting transfers between devices  119 us (15%)
  local copies, waits for them, and re-layouts  72.9 us (9%)
  matrix products  64.2 us (8%)
  other arithmetic  55.6 us (7%)
  between operations  24.2 us (3%)
    ppermute x58, waiting for transfers between devices, swap(): lax.ppermute(value, axis, [(i, i ^ j) for i in range(lax.axis_size(axis))])  184 us
    ppermute x58, starting transfers between devices, swap(): lax.ppermute(value, axis, [(i, i ^ j) for i in range(lax.axis_size(axis))])  99.5 us
    pallas_call x2, Pallas kernels, cross_bwd(): pl.pallas_call(partial(cross_bwd_body, heads, bounds, kind, step), grid_s...  74.5 us
    pallas_call x1, Pallas kernels, cross_fwd(): pl.pallas_call(partial(cross_fwd_body, heads, bounds), grid_spec=pltpu.Pr...  48.1 us
    pallas_call x1, Pallas kernels, self_bwd(): pl.pallas_call(partial(self_bwd_body, heads, bounds, len(others)), grid_s...  38 us
    pallas_call x1, Pallas kernels, self_fwd(): pl.pallas_call(partial(self_fwd_body, heads, bounds), grid_spec=pltpu.Pre...  34.8 us
    dot_general x7, matrix products, product(): return jnp.dot(left_side, right_side, preferred_element_type=jnp.float32)  34 us
    unnamed x257, local copies, waits for them, and re-layouts  33.1 us
  transfers between devices with their start and end apart: 71, of which 31 were waited for; matrix products, arithmetic and copies ran while one was open for 18% of the time, Pallas kernels for 33%

profile of v2, /device:TPU:0, one launch (start us, length us, event | category | flops | bytes accessed | tf_op | source)
XLA Modules:
  0.0 795.1 jit_solution(13621333712166528434)
XLA Ops:
  17.6 6.5 collective-permute-done.4.refs_1_
  24.1 9.5 %collective-permute-done.5.refs_2_ = bf16[128,896]{1,0:T(8,128)(2,1)S(1)} collective-permute-done((bf16[128,896]{1,0:T(8,128)(2,1)S(1)}, bf16[128,896]{1,0:T(8,128)(2,1)S(1)}, u32[]{:S(2)}, u32[]{:S(2)}) %collective-permute-start.5) | collective-permute-done | bytes 229408 | tf_op jit(solution)/shard_map/ppermute | solution.py:683
  70.1 8.4 %collective-permute-done.1.refs_2_ = bf16[1024,512]{1,0:T(8,128)(2,1)S(1)} collective-permute-done((bf16[1024,512]{1,0:T(8,128)(2,1)S(1)}, bf16[1024,512]{1,0:T(8,128)(2,1)S(1)}, u32[]{:S(2)}, u32[]{:S(2)}) %collective-permute-start.1) | collective-permute-done | bytes 1048608 | tf_op jit(solution)/shard_map/ppermute | solution.py:683
  82.8 5.9 fusion.7.refs_3_.refs_0_
  88.7 11.9 %collective-permute-done.2.refs_0_ = bf16[512,512]{1,0:T(8,128)(2,1)S(1)} collective-permute-done((bf16[512,512]{1,0:T(8,128)(2,1)S(1)}, bf16[512,512]{1,0:T(8,128)(2,1)S(1)}, u32[]{:S(2)}, u32[]{:S(2)}) %collective-permute-start.2) | collective-permute-done | bytes 524320 | tf_op jit(solution)/shard_map/ppermute | solution.py:683
  126.1 34.8 %self_fwd.1 = (bf16[1024,256]{1,0:T(8,128)(2,1)}, f32[8,1,512]{2,1,0:T(1,128)}, f32[8,1,512]{2,1,0:T(1,128)}) custom-call(s32[8,8]{1,0:T(8,128)} %concatenate.119.meta_ref, bf16[1024,256]{1,0:T(8,128)(2,1)} %pad_maximum_fusion.5.q_ref, bf16[1024,512]{1,0:T(8,128)(2,1)} %copy-done, bf16[1024,512]{1,0:T(8,128)(2,1)} %collective-permute-done.refs_1_, ...), custom_call_target="tpu_custom_call" | custom-call | tf_op jit(solution)/shard_map/self_fwd/pallas_call | solution.py:334
  175.6 8.2 %collective-permute-done.13.refs_0_ = bf16[2048,512]{1,0:T(8,128)(2,1)S(1)} collective-permute-done((bf16[2048,512]{1,0:T(8,128)(2,1)}, bf16[2048,512]{1,0:T(8,128)(2,1)S(1)}, u32[]{:S(2)}, u32[]{:S(2)}) %collective-permute-start.13) | collective-permute-done | bytes 2097184 | tf_op jit(solution)/shard_map/ppermute | solution.py:683
  216.6 17.8 %collective-permute-done.17 = f32[4]{0:T(128)S(1)} collective-permute-done((f32[4]{0:T(128)S(1)}, f32[4]{0:T(128)S(1)}, u32[]{:S(2)}, u32[]{:S(2)}) %collective-permute-start.17) | collective-permute-done | bytes 48 | tf_op jit(solution)/shard_map/ppermute | solution.py:683
  240.9 48.1 %cross_fwd.1 = (bf16[1024,256]{1,0:T(8,128)(2,1)}, f32[8,1,512]{2,1,0:T(1,128)}) custom-call(s32[5,8]{1,0:T(8,128)} %stack.99.seg_ref, bf16[1024,256]{1,0:T(8,128)(2,1)} %pad_maximum_fusion.7.refs_1_.refs_2_.q_ref.refs_3_, bf16[2048,512]{1,0:T(8,128)(2,1)} %gate.27.refs_0_, bf16[2048,512]{1,0:T(8,128)(2,1)} %get-tuple-element.99.refs_1_, ...), custom_call_target="tpu_custom_call" | custom-call | tf_op jit(solution)/shard_map/cross_fwd/pallas_call | solution.py:169
  306.1 8.4 %multiply_convert_fusion = (bf16[256,4096]{1,0:T(8,128)(2,1)}, f32[256,4096]{1,0:T(8,128)}) fusion(f32[4096]{0:T(1024)S(1)} %add.655, bf16[256,1024]{1,0:T(8,128)(2,1)S(1)} %fusion.58.refs_0_, bf16[1024,4096]{1,0:T(8,128)(2,1)} %all-gather.12.cloned.1.call-done), kind=kOutput, calls=%fused_computation.14 | convolution fusion | flops 2153775104 | bytes 15220736 | tf_op jit(solution)/shard_map/dot_general | solution.py:31
  314.5 6.6 fusion.132
  331.8 7.3 fusion.133
  339.1 9.0 %multiply_reduce_fusion = (bf16[1024]{0:T(1024)(128)(2,1)}, f32[256]{0:T(256)S(1)}, f32[256]{0:T(256)S(1)}, bf16[1024]{0:T(1024)(128)(2,1)}, f32[256,1024]{1,0:T(8,128)S(1)}) fusion(f32[256,1024]{1,0:T(8,128)S(1)} %get-tuple-element.456, f32[256]{0:T(256)S(1)} %add_rsqrt_fusion.1, f32[256]{0:T(256)S(1)} %broadcast_multiply_fusion.7, ...), kind=kOutput, calls=%fused_computation.66 | convolution fusion | flops 2150102528 | bytes 13643776 | tf_op jit(solution)/shard_map/dot_general | solution.py:41
  353.4 7.0 grad_columns.2.refs_5_
  373.3 28.5 %cross_bwd.2 = (bf16[1024,256]{1,0:T(8,128)(2,1)}, bf16[2048,512]{1,0:T(8,128)(2,1)}, bf16[1024,512]{1,0:T(8,128)(2,1)}, bf16[1024,512]{1,0:T(8,128)(2,1)}) custom-call(s32[5,8]{1,0:T(8,128)} %stack.99.seg_ref, bf16[1024,256]{1,0:T(8,128)(2,1)} %pad_maximum_fusion.7.refs_1_.refs_2_.q_ref.refs_3_, bf16[1024,256]{1,0:T(8,128)(2,1)} %pad_maximum_fusion.14.refs_1_.g_ref, ...), custom_call_target="tpu_custom_call" | custom-call | tf_op jit(solution)/shard_map/cross_bwd/pallas_call | solution.py:255
  401.9 20.4 %collective-permute-start.36 = (bf16[1024,512]{1,0:T(8,128)(2,1)}, bf16[1024,512]{1,0:T(8,128)(2,1)}, u32[]{:S(2)}, u32[]{:S(2)}) collective-permute-start(bf16[1024,512]{1,0:T(8,128)(2,1)} %get-tuple-element.117), channel_id=1, source_target_pairs={{0,8},{4,12},{8,0},{12,4},{1,9},{5,13},{9,1},{13,5},{2,10},{6,14},... | collective-permute-start | bytes 3145736 | tf_op jit(solution)/shard_map/ppermute | solution.py:683
  426.7 46.0 %cross_bwd.3 = (bf16[1024,256]{1,0:T(8,128)(2,1)}, bf16[2048,512]{1,0:T(8,128)(2,1)}, bf16[2048,512]{1,0:T(8,128)(2,1)}) custom-call(s32[5,8]{1,0:T(8,128)} %stack.99.seg_ref, bf16[1024,256]{1,0:T(8,128)(2,1)} %pad_maximum_fusion.7.refs_1_.refs_2_.q_ref.refs_3_, bf16[1024,256]{1,0:T(8,128)(2,1)} %pad_maximum_fusion.14.refs_1_.g_ref, ...), custom_call_target="tpu_custom_call" | custom-call | tf_op jit(solution)/shard_map/cross_bwd/pallas_call | solution.py:255
  501.5 6.3 collective-permute-done.41
  512.5 12.1 %reduce-scatter.12.cloned.1.call-start = ((), (), s32[]{:S(2)}) async-start(), calls=%async_computation.13 | async-start | bytes 8257536 | tf_op jit(solution)/shard_map/reduce_scatter | solution.py:859
  545.4 38.0 %self_bwd.1 = (bf16[1024,256]{1,0:T(8,128)(2,1)}, bf16[1024,512]{1,0:T(8,128)(2,1)}, bf16[1024,512]{1,0:T(8,128)(2,1)}, bf16[1024,512]{1,0:T(8,128)(2,1)}, bf16[...) custom-call(s32[8,8]{1,0:T(8,128)} %concatenate.119.meta_ref, bf16[1024,256]{1,0:T(8,128)(2,1)} %pad_maximum_fusion.5.q_ref, ...), custom_call_target="tpu_custom_call" | custom-call | tf_op jit(solution)/shard_map/self_bwd/pallas_call | solution.py:411
  583.5 7.1 grad_columns.3
  594.0 7.1 sum_terms.2
  601.1 8.0 %plane_shares.2 = (bf16[2048,256]{1,0:T(8,128)(2,1)}, bf16[2048,256]{1,0:T(8,128)(2,1)}, bf16[2048,256]{1,0:T(8,128)(2,1)}, bf16[2048,256]{1,0:T(8,128)(2,1)}) custom-call(s32[1]{0:T(128)} %bitcast.63.plane_ref, bf16[2048,512]{1,0:T(8,128)(2,1)} %get-tuple-element.127.refs_0_, bf16[1024,512]{1,0:T(8,128)(2,1)} %gate.25.refs_1_.refs_2_.refs_3_.refs_4_, ...), custom_call_target="tpu_custom_call" | custom-call | flops 20000000000 | bytes 33554432 | tf_op jit(solution)/shard_map/plane_shares/pallas_call | solution.py:596
  613.5 6.8 weight_grad.2.refs_1_.refs_3_
  646.2 6.6 collective-permute-done.49.refs_4_.refs_1_
  667.1 6.9 weight_grad.3.refs_0_
  674.0 8.8 %collective-permute-done.52 = bf16[256,1024]{1,0:T(8,128)(2,1)S(1)} collective-permute-done((bf16[256,1024]{1,0:T(8,128)(2,1)}, bf16[256,1024]{1,0:T(8,128)(2,1)S(1)}, u32[]{:S(2)}, u32[]{:S(2)}) %collective-permute-start.52) | collective-permute-done | bytes 524320 | tf_op jit(solution)/shard_map/ppermute | solution.py:683
  682.8 9.4 %collective-permute-done.51 = bf16[256,1024]{1,0:T(8,128)(2,1)S(1)} collective-permute-done((bf16[256,1024]{1,0:T(8,128)(2,1)}, bf16[256,1024]{1,0:T(8,128)(2,1)S(1)}, u32[]{:S(2)}, u32[]{:S(2)}) %collective-permute-start.51) | collective-permute-done | bytes 524320 | tf_op jit(solution)/shard_map/ppermute | solution.py:683
  693.7 6.8 put_blocks.1.refs_1_.refs_4_
  700.5 6.0 plane_shares.3
  723.5 31.0 %collective-permute-done.56.refs_6_ = bf16[1024,256]{1,0:T(8,128)(2,1)S(1)} collective-permute-done((bf16[1024,256]{1,0:T(8,128)(2,1)}, bf16[1024,256]{1,0:T(8,128)(2,1)S(1)}, u32[]{:S(2)}, u32[]{:S(2)}) %collective-permute-start.56) | collective-permute-done | bytes 524320 | tf_op jit(solution)/shard_map/ppermute | solution.py:683
  767.7 9.4 %collective-permute-done.59 = bf16[128,896]{1,0:T(8,128)(2,1)S(1)} collective-permute-done((bf16[128,896]{1,0:T(8,128)(2,1)}, bf16[128,896]{1,0:T(8,128)(2,1)S(1)}, u32[]{:S(2)}, u32[]{:S(2)}) %collective-permute-start.59) | collective-permute-done | bytes 229408 | tf_op jit(solution)/shard_map/ppermute | solution.py:683
  (630 shorter events, 316.3 us)
Async XLA Ops:
  7.2 38.8 %all-gather.6.cloned.1.call-start = ((), (), s32[]{:S(2)}) async-start(), calls=%async_computation.5 | async-start | bytes 2064384 | tf_op jit(solution)/shard_map/all_gather | solution.py:757
  10.8 59.3 %all-gather.8.cloned.1.call-start = ((), (), s32[]{:S(2)}) async-start(), calls=%async_computation.6 | async-start | bytes 1179648 | tf_op jit(solution)/shard_map/all_gather | solution.py:770
  37.5 153.1 %all-gather.10.cloned.1.call-start = ((), (), s32[]{:S(2)}) async-start(), calls=%async_computation.7 | async-start | bytes 8257536 | tf_op jit(solution)/shard_map/all_gather | solution.py:832
  46.0 260.1 %all-gather.12.cloned.1.call-start = ((), (), s32[]{:S(2)}) async-start(), calls=%async_computation.8 | async-start | bytes 9437184 | tf_op jit(solution)/shard_map/all_gather | solution.py:836
  56.6 46.2 %collective-permute-start.23 = (bf16[128,2048]{1,0:T(8,128)(2,1)}, bf16[128,2048]{1,0:T(8,128)(2,1)S(1)}, u32[]{:S(2)}, u32[]{:S(2)}) collective-permute-start(bf16[128,2048]{1,0:T(8,128)(2,1)} %gate.31.refs_0_), channel_id=1, source_target_pairs={{0,1},{1,0},{2,3},{3,2},{4,5},{5,4},{6,7},{7,6},{8,9},{9,8},{10,11... | collective-permute-start | bytes 1572872 | tf_op jit(solution)/shard_map/ppermute | solution.py:683
  60.0 42.7 %collective-permute-start.24 = (bf16[128,2048]{1,0:T(8,128)(2,1)}, bf16[128,2048]{1,0:T(8,128)(2,1)}, u32[]{:S(2)}, u32[]{:S(2)}) collective-permute-start(bf16[128,2048]{1,0:T(8,128)(2,1)} %gate.31.refs_0_), channel_id=1, source_target_pairs={{0,2},{1,3},{2,0},{3,1},{4,6},{5,7},{6,4},{7,5},{8,10},{9,11},{10,... | collective-permute-start | bytes 1572872 | tf_op jit(solution)/shard_map/ppermute | solution.py:683
  61.1 41.7 %collective-permute-start.25 = (bf16[128,2048]{1,0:T(8,128)(2,1)}, bf16[128,2048]{1,0:T(8,128)(2,1)}, u32[]{:S(2)}, u32[]{:S(2)}) collective-permute-start(bf16[128,2048]{1,0:T(8,128)(2,1)} %gate.31.refs_0_), channel_id=1, source_target_pairs={{0,3},{1,2},{2,1},{3,0},{4,7},{5,6},{6,5},{7,4},{8,11},{9,10},{10,... | collective-permute-start | bytes 1572872 | tf_op jit(solution)/shard_map/ppermute | solution.py:683
  106.3 208.2 %all-gather.14.cloned.1.call-start = ((), (), s32[]{:S(2)}) async-start(), calls=%async_computation.9 | async-start | bytes 9437184 | tf_op jit(solution)/shard_map/all_gather | solution.py:838
  107.4 365.3 %reduce-scatter.6.cloned.1.call-start = ((), (), s32[]{:S(2)}) async-start(), calls=%async_computation.10 | async-start | bytes 9437184 | tf_op jit(solution)/shard_map/reduce_scatter | solution.py:859
  111.7 72.1 %collective-permute-start.13 = (bf16[2048,512]{1,0:T(8,128)(2,1)}, bf16[2048,512]{1,0:T(8,128)(2,1)S(1)}, u32[]{:S(2)}, u32[]{:S(2)}) collective-permute-start(bf16[2048,512]{1,0:T(8,128)(2,1)} %gate.27.refs_0_), channel_id=1, source_target_pairs={{0,4},{4,0},{8,12},{12,8},{1,5},{5,1},{9,13},{13,9},{2,6},{6,2},{1... | collective-permute-start | bytes 6291464 | tf_op jit(solution)/shard_map/ppermute | solution.py:683
  112.3 71.6 %collective-permute-start.14 = (bf16[2048,512]{1,0:T(8,128)(2,1)}, bf16[2048,512]{1,0:T(8,128)(2,1)}, u32[]{:S(2)}, u32[]{:S(2)}) collective-permute-start(bf16[2048,512]{1,0:T(8,128)(2,1)} %gate.27.refs_0_), channel_id=1, source_target_pairs={{0,8},{4,12},{8,0},{12,4},{1,9},{5,13},{9,1},{13,5},{2,10},{6,14},... | collective-permute-start | bytes 6291464 | tf_op jit(solution)/shard_map/ppermute | solution.py:683
  187.6 52.0 %collective-permute-start.15 = (bf16[1024,512]{1,0:T(8,128)(2,1)}, bf16[1024,512]{1,0:T(8,128)(2,1)S(1)}, u32[]{:S(2)}, u32[]{:S(2)}) collective-permute-start(bf16[1024,512]{1,0:T(8,128)(2,1)} %slice.524), channel_id=1, source_target_pairs={{0,4},{4,0},{8,12},{12,8},{1,5},{5,1},{9,13},{13,9},{2,6},{6,2},{1... | collective-permute-start | bytes 3145736 | tf_op jit(solution)/shard_map/ppermute | solution.py:683
  188.9 50.6 %collective-permute-start.16 = (bf16[1024,512]{1,0:T(8,128)(2,1)}, bf16[1024,512]{1,0:T(8,128)(2,1)S(1)}, u32[]{:S(2)}, u32[]{:S(2)}) collective-permute-start(bf16[1024,512]{1,0:T(8,128)(2,1)} %slice.525), channel_id=1, source_target_pairs={{0,8},{4,12},{8,0},{12,4},{1,9},{5,13},{9,1},{13,5},{2,10},{6,14},... | collective-permute-start | bytes 3145736 | tf_op jit(solution)/shard_map/ppermute | solution.py:683
  331.5 154.3 %reduce-scatter.8.cloned.1.call-start = ((), (), s32[]{:S(2)}) async-start(), calls=%async_computation.11 | async-start | bytes 9437184 | tf_op jit(solution)/shard_map/reduce_scatter | solution.py:859
  360.4 259.9 %reduce-scatter.10.cloned.1.call-start = ((), (), s32[]{:S(2)}) async-start(), calls=%async_computation.12 | async-start | bytes 2621440 | tf_op jit(solution)/shard_map/reduce_scatter | solution.py:962
  401.8 70.9 %collective-permute-start.35 = (bf16[1024,512]{1,0:T(8,128)(2,1)}, bf16[1024,512]{1,0:T(8,128)(2,1)}, u32[]{:S(2)}, u32[]{:S(2)}) collective-permute-start(bf16[1024,512]{1,0:T(8,128)(2,1)} %get-tuple-element.116), channel_id=1, source_target_pairs={{0,4},{4,0},{8,12},{12,8},{1,5},{5,1},{9,13},{13,9},{2,6},{6,2},{1... | collective-permute-start | bytes 3145736 | tf_op jit(solution)/shard_map/ppermute | solution.py:683
  401.9 70.9 %collective-permute-start.36 = (bf16[1024,512]{1,0:T(8,128)(2,1)}, bf16[1024,512]{1,0:T(8,128)(2,1)}, u32[]{:S(2)}, u32[]{:S(2)}) collective-permute-start(bf16[1024,512]{1,0:T(8,128)(2,1)} %get-tuple-element.117), channel_id=1, source_target_pairs={{0,8},{4,12},{8,0},{12,4},{1,9},{5,13},{9,1},{13,5},{2,10},{6,14},... | collective-permute-start | bytes 3145736 | tf_op jit(solution)/shard_map/ppermute | solution.py:683
  422.3 50.4 %collective-permute-start.32 = (bf16[256,1024]{1,0:T(8,128)(2,1)}, bf16[256,1024]{1,0:T(8,128)(2,1)S(1)}, u32[]{:S(2)}, u32[]{:S(2)}) collective-permute-start(bf16[256,1024]{1,0:T(8,128)(2,1)} %gate.35.refs_0_), channel_id=1, source_target_pairs={{0,1},{1,0},{2,3},{3,2},{4,5},{5,4},{6,7},{7,6},{8,9},{9,8},{10,11... | collective-permute-start | bytes 1572872 | tf_op jit(solution)/shard_map/ppermute | solution.py:683
  422.3 50.4 %collective-permute-start.33 = (bf16[256,1024]{1,0:T(8,128)(2,1)}, bf16[256,1024]{1,0:T(8,128)(2,1)S(1)}, u32[]{:S(2)}, u32[]{:S(2)}) collective-permute-start(bf16[256,1024]{1,0:T(8,128)(2,1)} %gate.35.refs_0_), channel_id=1, source_target_pairs={{0,2},{1,3},{2,0},{3,1},{4,6},{5,7},{6,4},{7,5},{8,10},{9,11},{10,... | collective-permute-start | bytes 1572872 | tf_op jit(solution)/shard_map/ppermute | solution.py:683
  424.8 47.9 %collective-permute-start.34 = (bf16[256,1024]{1,0:T(8,128)(2,1)}, bf16[256,1024]{1,0:T(8,128)(2,1)S(1)}, u32[]{:S(2)}, u32[]{:S(2)}) collective-permute-start(bf16[256,1024]{1,0:T(8,128)(2,1)} %gate.35.refs_0_), channel_id=1, source_target_pairs={{0,3},{1,2},{2,1},{3,0},{4,7},{5,6},{6,5},{7,4},{8,11},{9,10},{10,... | collective-permute-start | bytes 1572872 | tf_op jit(solution)/shard_map/ppermute | solution.py:683
  512.5 181.2 %reduce-scatter.12.cloned.1.call-start = ((), (), s32[]{:S(2)}) async-start(), calls=%async_computation.13 | async-start | bytes 8257536 | tf_op jit(solution)/shard_map/reduce_scatter | solution.py:859
  538.2 55.8 %collective-permute-start.44 = (bf16[2048,512]{1,0:T(8,128)(2,1)}, bf16[2048,512]{1,0:T(8,128)(2,1)}, u32[]{:S(2)}, u32[]{:S(2)}) collective-permute-start(bf16[2048,512]{1,0:T(8,128)(2,1)} %add_half.4.refs_5_), channel_id=1, source_target_pairs={{0,4},{4,0},{8,12},{12,8},{1,5},{5,1},{9,13},{13,9},{2,6},{6,2},{1... | collective-permute-start | bytes 6291464 | tf_op jit(solution)/shard_map/ppermute | solution.py:683
  543.3 50.7 %collective-permute-start.45 = (bf16[2048,512]{1,0:T(8,128)(2,1)}, bf16[2048,512]{1,0:T(8,128)(2,1)}, u32[]{:S(2)}, u32[]{:S(2)}) collective-permute-start(bf16[2048,512]{1,0:T(8,128)(2,1)} %add_half.5.refs_6_), channel_id=1, source_target_pairs={{0,8},{4,12},{8,0},{12,4},{1,9},{5,13},{9,1},{13,5},{2,10},{6,14},... | collective-permute-start | bytes 6291464 | tf_op jit(solution)/shard_map/ppermute | solution.py:683
  590.6 165.2 %reduce-scatter.14.cloned.1.call-start = ((), (), s32[]{:S(2)}) async-start(), calls=%async_computation.14 | async-start | bytes 3244032 | tf_op jit(solution)/shard_map/reduce_scatter | solution.py:859
  593.7 31.3 %collective-permute-start.46 = (bf16[512,512]{1,0:T(8,128)(2,1)S(1)}, bf16[512,512]{1,0:T(8,128)(2,1)S(1)}, u32[]{:S(2)}, u32[]{:S(2)}) collective-permute-start(bf16[512,512]{1,0:T(8,128)(2,1)S(1)} %copy-done.102), channel_id=1, source_target_pairs={{0,4},{4,0},{8,12},{12,8},{1,5},{5,1},{9,13},{13,9},{2,6},{6,2},{1... | collective-permute-start | bytes 1572872 | tf_op jit(solution)/shard_map/ppermute | solution.py:683
  609.1 43.6 %collective-permute-start.49 = (bf16[2048,256]{1,0:T(8,128)(2,1)}, bf16[2048,256]{1,0:T(8,128)(2,1)}, u32[]{:S(2)}, u32[]{:S(2)}) collective-permute-start(bf16[2048,256]{1,0:T(8,128)(2,1)} %get-tuple-element.129.refs_2_), channel_id=1, source_target_pairs={{0,1},{1,0},{2,3},{3,2},{4,5},{5,4},{6,7},{7,6},{8,9},{9,8},{10,11... | collective-permute-start | bytes 3145736 | tf_op jit(solution)/shard_map/ppermute | solution.py:683
  609.2 91.3 %collective-permute-start.53 = (bf16[2048,256]{1,0:T(8,128)(2,1)}, bf16[2048,256]{1,0:T(8,128)(2,1)}, u32[]{:S(2)}, u32[]{:S(2)}) collective-permute-start(bf16[2048,256]{1,0:T(8,128)(2,1)} %get-tuple-element.130.refs_3_), channel_id=1, source_target_pairs={{0,2},{1,3},{2,0},{3,1},{4,6},{5,7},{6,4},{7,5},{8,10},{9,11},{10,... | collective-permute-start | bytes 3145736 | tf_op jit(solution)/shard_map/ppermute | solution.py:683
  612.1 88.3 %collective-permute-start.54 = (bf16[2048,256]{1,0:T(8,128)(2,1)}, bf16[2048,256]{1,0:T(8,128)(2,1)}, u32[]{:S(2)}, u32[]{:S(2)}) collective-permute-start(bf16[2048,256]{1,0:T(8,128)(2,1)} %get-tuple-element.131.refs_4_), channel_id=1, source_target_pairs={{0,3},{1,2},{2,1},{3,0},{4,7},{5,6},{6,5},{7,4},{8,11},{9,10},{10,... | collective-permute-start | bytes 3145736 | tf_op jit(solution)/shard_map/ppermute | solution.py:683
  623.1 35.4 %collective-permute-start.47 = (bf16[1024,512]{1,0:T(8,128)(2,1)}, bf16[1024,512]{1,0:T(8,128)(2,1)}, u32[]{:S(2)}, u32[]{:S(2)}) collective-permute-start(bf16[1024,512]{1,0:T(8,128)(2,1)} %add_half.6.refs_4_.refs_1_), channel_id=1, source_target_pairs={{0,4},{4,0},{8,12},{12,8},{1,5},{5,1},{9,13},{13,9},{2,6},{6,2},{1... | collective-permute-start | bytes 3145736 | tf_op jit(solution)/shard_map/ppermute | solution.py:683
  627.8 30.7 %collective-permute-start.48 = (bf16[1024,512]{1,0:T(8,128)(2,1)}, bf16[1024,512]{1,0:T(8,128)(2,1)}, u32[]{:S(2)}, u32[]{:S(2)}) collective-permute-start(bf16[1024,512]{1,0:T(8,128)(2,1)} %add_half.7.refs_5_.refs_2_), channel_id=1, source_target_pairs={{0,8},{4,12},{8,0},{12,4},{1,9},{5,13},{9,1},{13,5},{2,10},{6,14},... | collective-permute-start | bytes 3145736 | tf_op jit(solution)/shard_map/ppermute | solution.py:683
  709.7 44.7 %collective-permute-start.56 = (bf16[1024,256]{1,0:T(8,128)(2,1)}, bf16[1024,256]{1,0:T(8,128)(2,1)S(1)}, u32[]{:S(2)}, u32[]{:S(2)}) collective-permute-start(bf16[1024,256]{1,0:T(8,128)(2,1)} %get-tuple-element.149), channel_id=1, source_target_pairs={{0,2},{1,3},{2,0},{3,1},{4,6},{5,7},{6,4},{7,5},{8,10},{9,11},{10,... | collective-permute-start | bytes 1572872 | tf_op jit(solution)/shard_map/ppermute | solution.py:683
  709.7 44.7 %collective-permute-start.55 = (bf16[1024,256]{1,0:T(8,128)(2,1)}, bf16[1024,256]{1,0:T(8,128)(2,1)S(1)}, u32[]{:S(2)}, u32[]{:S(2)}) collective-permute-start(bf16[1024,256]{1,0:T(8,128)(2,1)} %get-tuple-element.148), channel_id=1, source_target_pairs={{0,1},{1,0},{2,3},{3,2},{4,5},{5,4},{6,7},{7,6},{8,9},{9,8},{10,11... | collective-permute-start | bytes 1572872 | tf_op jit(solution)/shard_map/ppermute | solution.py:683
  (145 other events, 1353.4 us)
Sparse Core Ops, SparseCore 0:
  10.9 29.4 all-gather.5
  42.9 27.1 all-gather.7
  72.0 72.0 all-gather.9
  145.8 89.6 all-gather.11
  237.2 53.7 all-gather.13
  331.6 71.4 reduce-scatter.5
  407.0 78.7 reduce-scatter.7
  512.6 42.8 reduce-scatter.9
  590.7 96.2 reduce-scatter.11
  693.8 44.9 reduce-scatter.13

commit v3 on v2

--- a/solution.py
+++ b/solution.py
@@ -933,7 +933,7 @@
     enc_passed = relay_start(*halves)
     cross_q_grad, *enc_terms = cross_bwd(0, cross_queries, enc_kv, *saved, cross_q_grad, [])
     (cross_q_grad,) = after([cross_q_grad], [*out_rows[1:], *enc_passed, own_down])
-    (cross_q_all,) = after([heads_to_rows(cross_q_grad)], [own_up])
+    cross_q_all = heads_to_rows(cross_q_grad)
     grad_one, gain_one, shift_one = normalize_back(
         grad_two + contract_cols(cross_q_all, w_cross), unit_one, factor_one, vec_all[3]
     )
@@ -957,10 +957,10 @@
     small_part = [jnp.concatenate([vec_part, up_part[:, j]], axis=1) for j in range(depth)]
     small_part = jnp.concatenate([by_shard(part, shard_rows) for part in small_part], axis=1)
     self_grads = rows_to_heads(self_grads)
-    own_down, own_up = after([own_down, own_up], [self_grads])
+    enc_joined = relay_join([*enc_terms, far], enc_passed, [cross_q_all])
+    own_down, own_up = after([own_down, own_up], [self_grads, *enc_joined[1:]])
     by_plane = by_plane_order([own_up, own_down], plane, depth)
     ffn = lax.psum_scatter(by_plane, T, scatter_dimension=1, tiled=True)
-    enc_joined = relay_join([*enc_terms, far], enc_passed, [cross_q_all])
     enc_terms = relay_finish(enc_joined)
     q_grad, *kv_terms = self_bwd(
         queries, kv, meta, self_grads, self_context, self_lse, [*enc_joined[1:], by_plane]
@@ -984,7 +984,8 @@
     portion = row_count // groups
     returned = [pick_rows(out_rows, near[j], portion) for j in range(groups)]
     ffn = after([ffn], kv_joined[1:])[0].astype(wide)
-    ffn_new = updated(2, ffn[:, :hidden_width]) + updated(3, ffn[:, hidden_width:].T)
+    (down_grad,) = after([ffn[:, hidden_width:].T], kv_joined[1:])
+    ffn_new = updated(2, ffn[:, :hidden_width]) + updated(3, down_grad)
 
     kv_grad, kv_columns = sum_terms(relay_finish(kv_joined), [grad_w_enc, enc_sent[1], *ffn_new, *returned], SOME_COST)
     returned = spread(after(returned, [kv_grad]), C)
@@ -1028,7 +1029,7 @@
             + [in_cross]
             + column_blocks(own_first[:, 3 * head_width + 128 :], 2)
         ),
-        1: jnp.stack([out_self.T, out_cross.T]),
+        1: after([jnp.stack([out_self.T, out_cross.T])], token_sent[1:])[0],
         4: own_first[:, 3 * head_width : 3 * head_width + 128].reshape(-1)[:n_head].reshape(head_bias.shape),
         5: small_part[n_vec : n_vec + n_up].reshape(up_bias.shape),
         6: small_part[:n_vec].reshape(vectors.shape),

time: 800 us -> 784 us (0.980); the launches traced: 795 us -> 769 us
  Pallas kernels: 270 us -> 255 us
  waiting for transfers between devices: 190 us -> 179 us
  starting transfers between devices: 119 us -> 109 us
  local copies, waits for them, and re-layouts: 72.9 us -> 82 us
    reduce_scatter x4, starting transfers between devices: 12.9 us -> 1.06 us  [owned(): lax.psum_scatter(gradient.astype(low), SHARD, scatter_dimension=0, tiled=...]
    ppermute x58, waiting for transfers between devices: 184 us -> 174 us  [swap(): lax.ppermute(value, axis, [(i, i ^ j) for i in range(lax.axis_size(axis))])]
    unnamed x257 -> x258, local copies, waits for them, and re-layouts: 33.1 us -> 38.7 us
  transfers between devices with their start and end apart: 71 -> 71, of which waited for: 31 -> 30; matrix products, arithmetic and copies ran while one was open for 18% -> 20% of each run, Pallas kernels for 33% -> 33%
where the time goes in v3:
time: 784 us; the launch traced here: 769 us
  Pallas kernels  255 us (33%)
  waiting for transfers between devices  179 us (23%)
  starting transfers between devices  109 us (14%)
  local copies, waits for them, and re-layouts  82 us (10%)
  matrix products  62.7 us (8%)
  other arithmetic  56.5 us (7%)
  between operations  24.2 us (3%)
    ppermute x58, waiting for transfers between devices, swap(): lax.ppermute(value, axis, [(i, i ^ j) for i in range(lax.axis_size(axis))])  174 us
    ppermute x58, starting transfers between devices, swap(): lax.ppermute(value, axis, [(i, i ^ j) for i in range(lax.axis_size(axis))])  100 us
    pallas_call x2, Pallas kernels, cross_bwd(): pl.pallas_call(partial(cross_bwd_body, heads, bounds, kind, step), grid_s...  69.1 us
    pallas_call x1, Pallas kernels, cross_fwd(): pl.pallas_call(partial(cross_fwd_body, heads, bounds), grid_spec=pltpu.Pr...  43.5 us
    unnamed x258, local copies, waits for them, and re-layouts  38.7 us
    pallas_call x1, Pallas kernels, self_bwd(): pl.pallas_call(partial(self_bwd_body, heads, bounds, len(others)), grid_s...  35.9 us
    dot_general x7, matrix products, product(): return jnp.dot(left_side, right_side, preferred_element_type=jnp.float32)  33.7 us
    pallas_call x1, Pallas kernels, self_fwd(): pl.pallas_call(partial(self_fwd_body, heads, bounds), grid_spec=pltpu.Pre...  32.8 us
  transfers between devices with their start and end apart: 71, of which 30 were waited for; matrix products, arithmetic and copies ran while one was open for 20% of the time, Pallas kernels for 33%

profile of v3, /device:TPU:0, one launch (start us, length us, event | category | flops | bytes accessed | tf_op | source)
XLA Modules:
  0.0 768.6 jit_solution(12259210167240946956)
XLA Ops:
  17.6 6.5 collective-permute-done.4.refs_1_
  24.1 9.5 %collective-permute-done.5.refs_2_ = bf16[128,896]{1,0:T(8,128)(2,1)S(1)} collective-permute-done((bf16[128,896]{1,0:T(8,128)(2,1)S(1)}, bf16[128,896]{1,0:T(8,128)(2,1)S(1)}, u32[]{:S(2)}, u32[]{:S(2)}) %collective-permute-start.5) | collective-permute-done | bytes 229408 | tf_op jit(solution)/shard_map/ppermute | solution.py:683
  70.2 8.4 %collective-permute-done.1.refs_2_ = bf16[1024,512]{1,0:T(8,128)(2,1)S(1)} collective-permute-done((bf16[1024,512]{1,0:T(8,128)(2,1)S(1)}, bf16[1024,512]{1,0:T(8,128)(2,1)S(1)}, u32[]{:S(2)}, u32[]{:S(2)}) %collective-permute-start.1) | collective-permute-done | bytes 1048608 | tf_op jit(solution)/shard_map/ppermute | solution.py:683
  82.9 5.9 fusion.7.refs_3_.refs_0_
  88.8 12.0 %collective-permute-done.2.refs_0_ = bf16[512,512]{1,0:T(8,128)(2,1)S(1)} collective-permute-done((bf16[512,512]{1,0:T(8,128)(2,1)S(1)}, bf16[512,512]{1,0:T(8,128)(2,1)S(1)}, u32[]{:S(2)}, u32[]{:S(2)}) %collective-permute-start.2) | collective-permute-done | bytes 524320 | tf_op jit(solution)/shard_map/ppermute | solution.py:683
  126.0 32.8 %self_fwd.1 = (bf16[1024,256]{1,0:T(8,128)(2,1)}, f32[8,1,512]{2,1,0:T(1,128)}, f32[8,1,512]{2,1,0:T(1,128)}) custom-call(s32[8,8]{1,0:T(8,128)} %concatenate.119.meta_ref, bf16[1024,256]{1,0:T(8,128)(2,1)} %pad_maximum_fusion.5.q_ref, bf16[1024,512]{1,0:T(8,128)(2,1)} %copy-done, bf16[1024,512]{1,0:T(8,128)(2,1)} %collective-permute-done.refs_1_, ...), custom_call_target="tpu_custom_call" | custom-call | tf_op jit(solution)/shard_map/self_fwd/pallas_call | solution.py:334
  172.8 11.1 %collective-permute-done.13.refs_0_ = bf16[2048,512]{1,0:T(8,128)(2,1)S(1)} collective-permute-done((bf16[2048,512]{1,0:T(8,128)(2,1)}, bf16[2048,512]{1,0:T(8,128)(2,1)S(1)}, u32[]{:S(2)}, u32[]{:S(2)}) %collective-permute-start.13) | collective-permute-done | bytes 2097184 | tf_op jit(solution)/shard_map/ppermute | solution.py:683
  216.7 17.7 %collective-permute-done.17 = f32[4]{0:T(128)S(1)} collective-permute-done((f32[4]{0:T(128)S(1)}, f32[4]{0:T(128)S(1)}, u32[]{:S(2)}, u32[]{:S(2)}) %collective-permute-start.17) | collective-permute-done | bytes 48 | tf_op jit(solution)/shard_map/ppermute | solution.py:683
  241.0 43.5 %cross_fwd.1 = (bf16[1024,256]{1,0:T(8,128)(2,1)}, f32[8,1,512]{2,1,0:T(1,128)}) custom-call(s32[5,8]{1,0:T(8,128)} %stack.99.seg_ref, bf16[1024,256]{1,0:T(8,128)(2,1)} %pad_maximum_fusion.7.refs_1_.refs_2_.q_ref.refs_3_, bf16[2048,512]{1,0:T(8,128)(2,1)} %gate.28.refs_0_, bf16[2048,512]{1,0:T(8,128)(2,1)} %get-tuple-element.99.refs_1_, ...), custom_call_target="tpu_custom_call" | custom-call | tf_op jit(solution)/shard_map/cross_fwd/pallas_call | solution.py:169
  305.0 8.4 %multiply_convert_fusion = (bf16[256,4096]{1,0:T(8,128)(2,1)}, f32[256,4096]{1,0:T(8,128)}) fusion(f32[4096]{0:T(1024)S(1)} %add.655, bf16[256,1024]{1,0:T(8,128)(2,1)S(1)} %fusion.58.refs_0_, bf16[1024,4096]{1,0:T(8,128)(2,1)} %all-gather.12.cloned.1.call-done), kind=kOutput, calls=%fused_computation.14 | convolution fusion | flops 2153775104 | bytes 15220736 | tf_op jit(solution)/shard_map/dot_general | solution.py:31
  313.5 6.6 fusion.132
  325.6 5.8 convolution_convert_fusion.refs_1_.refs_4_
  332.0 7.0 fusion.133
  339.1 8.3 %multiply_reduce_fusion = (bf16[1024]{0:T(1024)(128)(2,1)S(1)}, f32[256]{0:T(256)S(1)}, f32[256]{0:T(256)S(1)}, bf16[1024]{0:T(1024)(128)(2,1)S(1)}, f32[256,1024]{1,0:T(8,128)S(1)}) fusion(f32[256,1024]{1,0:T(8,128)S(1)} %get-tuple-element.491, f32[256]{0:T(256)S(1)} %add_rsqrt_fusion.1, f32[256]{0:T(256)S(1)} %broadcast_multiply_fusion.10, ...), kind=kOutput, calls=%fused_computation.66 | convolution fusion | flops 2150102528 | bytes 13643776 | tf_op jit(solution)/shard_map/dot_general | solution.py:41
  351.8 6.8 grad_columns.2.refs_5_
  366.8 6.6 collective-permute-done.30
  374.2 46.2 %cross_bwd.2 = (bf16[1024,256]{1,0:T(8,128)(2,1)}, bf16[2048,512]{1,0:T(8,128)(2,1)}, bf16[1024,512]{1,0:T(8,128)(2,1)}, bf16[1024,512]{1,0:T(8,128)(2,1)}) custom-call(s32[5,8]{1,0:T(8,128)} %stack.99.seg_ref, bf16[1024,256]{1,0:T(8,128)(2,1)} %pad_maximum_fusion.7.refs_1_.refs_2_.q_ref.refs_3_, bf16[1024,256]{1,0:T(8,128)(2,1)} %pad_maximum_fusion.14.refs_1_.g_ref, ...), custom_call_target="tpu_custom_call" | custom-call | tf_op jit(solution)/shard_map/cross_bwd/pallas_call | solution.py:255
  426.7 22.8 %cross_bwd.3 = (bf16[1024,256]{1,0:T(8,128)(2,1)}, bf16[2048,512]{1,0:T(8,128)(2,1)}, bf16[2048,512]{1,0:T(8,128)(2,1)}) custom-call(s32[5,8]{1,0:T(8,128)} %stack.99.seg_ref, bf16[1024,256]{1,0:T(8,128)(2,1)} %pad_maximum_fusion.7.refs_1_.refs_2_.q_ref.refs_3_, bf16[1024,256]{1,0:T(8,128)(2,1)} %pad_maximum_fusion.14.refs_1_.g_ref, ...), custom_call_target="tpu_custom_call" | custom-call | tf_op jit(solution)/shard_map/cross_bwd/pallas_call | solution.py:255
  449.6 9.7 %collective-permute-done.33.refs_2_ = bf16[256,1024]{1,0:T(8,128)(2,1)S(1)} collective-permute-done((bf16[256,1024]{1,0:T(8,128)(2,1)}, bf16[256,1024]{1,0:T(8,128)(2,1)S(1)}, u32[]{:S(2)}, u32[]{:S(2)}) %collective-permute-start.33) | collective-permute-done | bytes 524320 | tf_op jit(solution)/shard_map/ppermute | solution.py:683
  463.0 6.0 collective-permute-start.38
  516.9 10.6 %collective-permute-start.45 = (bf16[2048,512]{1,0:T(8,128)(2,1)S(1)}, bf16[2048,512]{1,0:T(8,128)(2,1)}, u32[]{:S(2)}, u32[]{:S(2)}) collective-permute-start(bf16[2048,512]{1,0:T(8,128)(2,1)S(1)} %copy-done.3), channel_id=1, source_target_pairs={{0,8},{4,12},{8,0},{12,4},{1,9},{5,13},{9,1},{13,5},{2,10},{6,14},... | collective-permute-start | bytes 6291464 | tf_op jit(solution)/shard_map/ppermute | solution.py:683
  529.0 35.9 %self_bwd.1 = (bf16[1024,256]{1,0:T(8,128)(2,1)}, bf16[1024,512]{1,0:T(8,128)(2,1)}, bf16[1024,512]{1,0:T(8,128)(2,1)}, bf16[1024,512]{1,0:T(8,128)(2,1)}, bf16[...) custom-call(s32[8,8]{1,0:T(8,128)} %concatenate.119.meta_ref, bf16[1024,256]{1,0:T(8,128)(2,1)} %pad_maximum_fusion.5.q_ref, ...), custom_call_target="tpu_custom_call" | custom-call | tf_op jit(solution)/shard_map/self_bwd/pallas_call | solution.py:411
  564.9 7.1 grad_columns.3
  575.1 7.1 sum_terms.2
  582.3 7.9 %plane_shares.2 = (bf16[2048,256]{1,0:T(8,128)(2,1)}, bf16[2048,256]{1,0:T(8,128)(2,1)}, bf16[2048,256]{1,0:T(8,128)(2,1)}, bf16[2048,256]{1,0:T(8,128)(2,1)}) custom-call(s32[1]{0:T(128)} %bitcast.63.plane_ref, bf16[2048,512]{1,0:T(8,128)(2,1)} %get-tuple-element.127.refs_0_, bf16[1024,512]{1,0:T(8,128)(2,1)} %gate.26.refs_1_.refs_2_.refs_3_.refs_4_, ...), custom_call_target="tpu_custom_call" | custom-call | flops 20000000000 | bytes 33554432 | tf_op jit(solution)/shard_map/plane_shares/pallas_call | solution.py:596
  594.6 6.5 weight_grad.2.refs_1_.refs_3_
  623.5 12.8 %collective-permute-done.47.refs_1_ = bf16[1024,512]{1,0:T(8,128)(2,1)} collective-permute-done((bf16[1024,512]{1,0:T(8,128)(2,1)}, bf16[1024,512]{1,0:T(8,128)(2,1)}, u32[]{:S(2)}, u32[]{:S(2)}) %collective-permute-start.47) | collective-permute-done | bytes 1048608 | tf_op jit(solution)/shard_map/ppermute | solution.py:683
  651.2 6.9 weight_grad.3.refs_0_
  665.2 6.7 put_blocks.1.refs_1_.refs_4_
  671.9 5.9 plane_shares.3
  694.4 22.3 %collective-permute-done.56.refs_6_.refs_2_ = bf16[1024,256]{1,0:T(8,128)(2,1)S(1)} collective-permute-done((bf16[1024,256]{1,0:T(8,128)(2,1)}, bf16[1024,256]{1,0:T(8,128)(2,1)S(1)}, u32[]{:S(2)}, u32[]{:S(2)}) %collective-permute-start.56) | collective-permute-done | bytes 524320 | tf_op jit(solution)/shard_map/ppermute | solution.py:683
  731.1 10.6 %collective-permute-done.59 = bf16[128,896]{0,1:T(8,128)(2,1)} collective-permute-done((bf16[128,896]{0,1:T(8,128)(2,1)}, bf16[128,896]{0,1:T(8,128)(2,1)}, u32[]{:S(2)}, u32[]{:S(2)}) %collective-permute-start.59) | collective-permute-done | bytes 229408 | tf_op jit(solution)/shard_map/ppermute | solution.py:683
  (639 shorter events, 322.6 us)
Async XLA Ops:
  7.2 38.8 %all-gather.6.cloned.1.call-start = ((), (), s32[]{:S(2)}) async-start(), calls=%async_computation.5 | async-start | bytes 2064384 | tf_op jit(solution)/shard_map/all_gather | solution.py:757
  10.9 59.3 %all-gather.8.cloned.1.call-start = ((), (), s32[]{:S(2)}) async-start(), calls=%async_computation.6 | async-start | bytes 1179648 | tf_op jit(solution)/shard_map/all_gather | solution.py:770
  37.6 153.2 %all-gather.10.cloned.1.call-start = ((), (), s32[]{:S(2)}) async-start(), calls=%async_computation.7 | async-start | bytes 8257536 | tf_op jit(solution)/shard_map/all_gather | solution.py:832
  46.0 259.0 %all-gather.12.cloned.1.call-start = ((), (), s32[]{:S(2)}) async-start(), calls=%async_computation.8 | async-start | bytes 9437184 | tf_op jit(solution)/shard_map/all_gather | solution.py:836
  56.6 46.2 %collective-permute-start.23 = (bf16[128,2048]{1,0:T(8,128)(2,1)}, bf16[128,2048]{1,0:T(8,128)(2,1)}, u32[]{:S(2)}, u32[]{:S(2)}) collective-permute-start(bf16[128,2048]{1,0:T(8,128)(2,1)} %gate.32.refs_0_), channel_id=1, source_target_pairs={{0,1},{1,0},{2,3},{3,2},{4,5},{5,4},{6,7},{7,6},{8,9},{9,8},{10,11... | collective-permute-start | bytes 1572872 | tf_op jit(solution)/shard_map/ppermute | solution.py:683
  60.1 42.7 %collective-permute-start.24 = (bf16[128,2048]{1,0:T(8,128)(2,1)}, bf16[128,2048]{1,0:T(8,128)(2,1)}, u32[]{:S(2)}, u32[]{:S(2)}) collective-permute-start(bf16[128,2048]{1,0:T(8,128)(2,1)} %gate.32.refs_0_), channel_id=1, source_target_pairs={{0,2},{1,3},{2,0},{3,1},{4,6},{5,7},{6,4},{7,5},{8,10},{9,11},{10,... | collective-permute-start | bytes 1572872 | tf_op jit(solution)/shard_map/ppermute | solution.py:683
  61.1 41.7 %collective-permute-start.25 = (bf16[128,2048]{1,0:T(8,128)(2,1)}, bf16[128,2048]{1,0:T(8,128)(2,1)}, u32[]{:S(2)}, u32[]{:S(2)}) collective-permute-start(bf16[128,2048]{1,0:T(8,128)(2,1)} %gate.32.refs_0_), channel_id=1, source_target_pairs={{0,3},{1,2},{2,1},{3,0},{4,7},{5,6},{6,5},{7,4},{8,11},{9,10},{10,... | collective-permute-start | bytes 1572872 | tf_op jit(solution)/shard_map/ppermute | solution.py:683
  106.4 207.1 %all-gather.14.cloned.1.call-start = ((), (), s32[]{:S(2)}) async-start(), calls=%async_computation.9 | async-start | bytes 9437184 | tf_op jit(solution)/shard_map/all_gather | solution.py:838
  107.6 351.8 %reduce-scatter.6.cloned.1.call-start = ((), (), s32[]{:S(2)}) async-start(), calls=%async_computation.10 | async-start | bytes 9437184 | tf_op jit(solution)/shard_map/reduce_scatter | solution.py:859
  111.5 72.3 %collective-permute-start.13 = (bf16[2048,512]{1,0:T(8,128)(2,1)}, bf16[2048,512]{1,0:T(8,128)(2,1)S(1)}, u32[]{:S(2)}, u32[]{:S(2)}) collective-permute-start(bf16[2048,512]{1,0:T(8,128)(2,1)} %gate.28.refs_0_), channel_id=1, source_target_pairs={{0,4},{4,0},{8,12},{12,8},{1,5},{5,1},{9,13},{13,9},{2,6},{6,2},{1... | collective-permute-start | bytes 6291464 | tf_op jit(solution)/shard_map/ppermute | solution.py:683
  112.2 71.8 %collective-permute-start.14 = (bf16[2048,512]{1,0:T(8,128)(2,1)}, bf16[2048,512]{1,0:T(8,128)(2,1)}, u32[]{:S(2)}, u32[]{:S(2)}) collective-permute-start(bf16[2048,512]{1,0:T(8,128)(2,1)} %gate.28.refs_0_), channel_id=1, source_target_pairs={{0,8},{4,12},{8,0},{12,4},{1,9},{5,13},{9,1},{13,5},{2,10},{6,14},... | collective-permute-start | bytes 6291464 | tf_op jit(solution)/shard_map/ppermute | solution.py:683
  187.6 52.0 %collective-permute-start.15 = (bf16[1024,512]{1,0:T(8,128)(2,1)}, bf16[1024,512]{1,0:T(8,128)(2,1)S(1)}, u32[]{:S(2)}, u32[]{:S(2)}) collective-permute-start(bf16[1024,512]{1,0:T(8,128)(2,1)} %slice.524), channel_id=1, source_target_pairs={{0,4},{4,0},{8,12},{12,8},{1,5},{5,1},{9,13},{13,9},{2,6},{6,2},{1... | collective-permute-start | bytes 3145736 | tf_op jit(solution)/shard_map/ppermute | solution.py:683
  189.0 50.6 %collective-permute-start.16 = (bf16[1024,512]{1,0:T(8,128)(2,1)}, bf16[1024,512]{1,0:T(8,128)(2,1)S(1)}, u32[]{:S(2)}, u32[]{:S(2)}) collective-permute-start(bf16[1024,512]{1,0:T(8,128)(2,1)} %slice.525), channel_id=1, source_target_pairs={{0,8},{4,12},{8,0},{12,4},{1,9},{5,13},{9,1},{13,5},{2,10},{6,14},... | collective-permute-start | bytes 3145736 | tf_op jit(solution)/shard_map/ppermute | solution.py:683
  292.7 27.7 %collective-permute-start.28 = (bf16[256,1024]{1,0:T(8,128)(2,1)}, bf16[256,1024]{1,0:T(8,128)(2,1)S(1)}, u32[]{:S(2)}, u32[]{:S(2)}) collective-permute-start(bf16[256,1024]{1,0:T(8,128)(2,1)} %get-tuple-element.112), channel_id=1, source_target_pairs={{0,12},{5,9},{10,6},{15,3},{16,28},{21,25},{26,22},{31,19}} | collective-permute-start | bytes 1572872 | tf_op jit(solution)/shard_map/ppermute | solution.py:898
  331.4 163.1 %reduce-scatter.8.cloned.1.call-start = ((), (), s32[]{:S(2)}) async-start(), calls=%async_computation.11 | async-start | bytes 9437184 | tf_op jit(solution)/shard_map/reduce_scatter | solution.py:859
  358.7 242.4 %reduce-scatter.10.cloned.1.call-start = ((), (), s32[]{:S(2)}) async-start(), calls=%async_computation.12 | async-start | bytes 2621440 | tf_op jit(solution)/shard_map/reduce_scatter | solution.py:963
  420.4 38.9 %collective-permute-start.35 = (bf16[1024,512]{1,0:T(8,128)(2,1)}, bf16[1024,512]{1,0:T(8,128)(2,1)}, u32[]{:S(2)}, u32[]{:S(2)}) collective-permute-start(bf16[1024,512]{1,0:T(8,128)(2,1)} %get-tuple-element.116), channel_id=1, source_target_pairs={{0,4},{4,0},{8,12},{12,8},{1,5},{5,1},{9,13},{13,9},{2,6},{6,2},{1... | collective-permute-start | bytes 3145736 | tf_op jit(solution)/shard_map/ppermute | solution.py:683
  422.3 37.0 %collective-permute-start.36 = (bf16[1024,512]{1,0:T(8,128)(2,1)}, bf16[1024,512]{1,0:T(8,128)(2,1)}, u32[]{:S(2)}, u32[]{:S(2)}) collective-permute-start(bf16[1024,512]{1,0:T(8,128)(2,1)} %get-tuple-element.117), channel_id=1, source_target_pairs={{0,8},{4,12},{8,0},{12,4},{1,9},{5,13},{9,1},{13,5},{2,10},{6,14},... | collective-permute-start | bytes 3145736 | tf_op jit(solution)/shard_map/ppermute | solution.py:683
  422.3 37.0 %collective-permute-start.33 = (bf16[256,1024]{1,0:T(8,128)(2,1)}, bf16[256,1024]{1,0:T(8,128)(2,1)S(1)}, u32[]{:S(2)}, u32[]{:S(2)}) collective-permute-start(bf16[256,1024]{1,0:T(8,128)(2,1)} %gate.36.refs_0_), channel_id=1, source_target_pairs={{0,2},{1,3},{2,0},{3,1},{4,6},{5,7},{6,4},{7,5},{8,10},{9,11},{10,... | collective-permute-start | bytes 1572872 | tf_op jit(solution)/shard_map/ppermute | solution.py:683
  422.7 36.6 %collective-permute-start.34 = (bf16[256,1024]{1,0:T(8,128)(2,1)}, bf16[256,1024]{1,0:T(8,128)(2,1)S(1)}, u32[]{:S(2)}, u32[]{:S(2)}) collective-permute-start(bf16[256,1024]{1,0:T(8,128)(2,1)} %gate.36.refs_0_), channel_id=1, source_target_pairs={{0,3},{1,2},{2,1},{3,0},{4,7},{5,6},{6,5},{7,4},{8,11},{9,10},{10,... | collective-permute-start | bytes 1572872 | tf_op jit(solution)/shard_map/ppermute | solution.py:683
  498.3 166.8 %reduce-scatter.12.cloned.1.call-start = ((), (), s32[]{:S(2)}) async-start(), calls=%async_computation.13 | async-start | bytes 8257536 | tf_op jit(solution)/shard_map/reduce_scatter | solution.py:859
  511.3 63.8 %collective-permute-start.44 = (bf16[2048,512]{1,0:T(8,128)(2,1)}, bf16[2048,512]{1,0:T(8,128)(2,1)}, u32[]{:S(2)}, u32[]{:S(2)}) collective-permute-start(bf16[2048,512]{1,0:T(8,128)(2,1)} %add_half.4.refs_3_.refs_5_), channel_id=1, source_target_pairs={{0,4},{4,0},{8,12},{12,8},{1,5},{5,1},{9,13},{13,9},{2,6},{6,2},{1... | collective-permute-start | bytes 6291464 | tf_op jit(solution)/shard_map/ppermute | solution.py:683
  516.9 58.2 %collective-permute-start.45 = (bf16[2048,512]{1,0:T(8,128)(2,1)S(1)}, bf16[2048,512]{1,0:T(8,128)(2,1)}, u32[]{:S(2)}, u32[]{:S(2)}) collective-permute-start(bf16[2048,512]{1,0:T(8,128)(2,1)S(1)} %copy-done.3), channel_id=1, source_target_pairs={{0,8},{4,12},{8,0},{12,4},{1,9},{5,13},{9,1},{13,5},{2,10},{6,14},... | collective-permute-start | bytes 6291464 | tf_op jit(solution)/shard_map/ppermute | solution.py:683
  572.0 146.0 %reduce-scatter.14.cloned.1.call-start = ((), (), s32[]{:S(2)}) async-start(), calls=%async_computation.14 | async-start | bytes 3244032 | tf_op jit(solution)/shard_map/reduce_scatter | solution.py:859
  573.6 30.6 %collective-permute-start.46 = (bf16[512,512]{1,0:T(8,128)(2,1)}, bf16[512,512]{1,0:T(8,128)(2,1)}, u32[]{:S(2)}, u32[]{:S(2)}) collective-permute-start(bf16[512,512]{1,0:T(8,128)(2,1)} %get-tuple-element.133), channel_id=1, source_target_pairs={{0,4},{4,0},{8,12},{12,8},{1,5},{5,1},{9,13},{13,9},{2,6},{6,2},{1... | collective-permute-start | bytes 1572872 | tf_op jit(solution)/shard_map/ppermute | solution.py:683
  590.2 33.3 %collective-permute-start.49 = (bf16[2048,256]{1,0:T(8,128)(2,1)}, bf16[2048,256]{1,0:T(8,128)(2,1)S(1)}, u32[]{:S(2)}, u32[]{:S(2)}) collective-permute-start(bf16[2048,256]{1,0:T(8,128)(2,1)} %get-tuple-element.129.refs_2_), channel_id=1, source_target_pairs={{0,1},{1,0},{2,3},{3,2},{4,5},{5,4},{6,7},{7,6},{8,9},{9,8},{10,11... | collective-permute-start | bytes 3145736 | tf_op jit(solution)/shard_map/ppermute | solution.py:683
  590.2 81.7 %collective-permute-start.53 = (bf16[2048,256]{1,0:T(8,128)(2,1)}, bf16[2048,256]{1,0:T(8,128)(2,1)}, u32[]{:S(2)}, u32[]{:S(2)}) collective-permute-start(bf16[2048,256]{1,0:T(8,128)(2,1)} %get-tuple-element.130.refs_3_), channel_id=1, source_target_pairs={{0,2},{1,3},{2,0},{3,1},{4,6},{5,7},{6,4},{7,5},{8,10},{9,11},{10,... | collective-permute-start | bytes 3145736 | tf_op jit(solution)/shard_map/ppermute | solution.py:683
  591.8 80.1 %collective-permute-start.54 = (bf16[2048,256]{1,0:T(8,128)(2,1)}, bf16[2048,256]{1,0:T(8,128)(2,1)}, u32[]{:S(2)}, u32[]{:S(2)}) collective-permute-start(bf16[2048,256]{1,0:T(8,128)(2,1)} %get-tuple-element.131.refs_4_), channel_id=1, source_target_pairs={{0,3},{1,2},{2,1},{3,0},{4,7},{5,6},{6,5},{7,4},{8,11},{9,10},{10,... | collective-permute-start | bytes 3145736 | tf_op jit(solution)/shard_map/ppermute | solution.py:683
  603.0 33.3 %collective-permute-start.47 = (bf16[1024,512]{1,0:T(8,128)(2,1)}, bf16[1024,512]{1,0:T(8,128)(2,1)}, u32[]{:S(2)}, u32[]{:S(2)}) collective-permute-start(bf16[1024,512]{1,0:T(8,128)(2,1)} %add_half.6.refs_4_.refs_1_), channel_id=1, source_target_pairs={{0,4},{4,0},{8,12},{12,8},{1,5},{5,1},{9,13},{13,9},{2,6},{6,2},{1... | collective-permute-start | bytes 3145736 | tf_op jit(solution)/shard_map/ppermute | solution.py:683
  606.2 35.6 %collective-permute-start.48 = (bf16[1024,512]{1,0:T(8,128)(2,1)}, bf16[1024,512]{1,0:T(8,128)(2,1)}, u32[]{:S(2)}, u32[]{:S(2)}) collective-permute-start(bf16[1024,512]{1,0:T(8,128)(2,1)} %add_half.7.refs_5_.refs_2_), channel_id=1, source_target_pairs={{0,8},{4,12},{8,0},{12,4},{1,9},{5,13},{9,1},{13,5},{2,10},{6,14},... | collective-permute-start | bytes 3145736 | tf_op jit(solution)/shard_map/ppermute | solution.py:683
  680.3 36.3 %collective-permute-start.56 = (bf16[1024,256]{1,0:T(8,128)(2,1)}, bf16[1024,256]{1,0:T(8,128)(2,1)S(1)}, u32[]{:S(2)}, u32[]{:S(2)}) collective-permute-start(bf16[1024,256]{1,0:T(8,128)(2,1)} %get-tuple-element.149), channel_id=1, source_target_pairs={{0,2},{1,3},{2,0},{3,1},{4,6},{5,7},{6,4},{7,5},{8,10},{9,11},{10,... | collective-permute-start | bytes 1572872 | tf_op jit(solution)/shard_map/ppermute | solution.py:683
  680.3 36.3 %collective-permute-start.55 = (bf16[1024,256]{1,0:T(8,128)(2,1)}, bf16[1024,256]{1,0:T(8,128)(2,1)S(1)}, u32[]{:S(2)}, u32[]{:S(2)}) collective-permute-start(bf16[1024,256]{1,0:T(8,128)(2,1)} %get-tuple-element.148), channel_id=1, source_target_pairs={{0,1},{1,0},{2,3},{3,2},{4,5},{5,4},{6,7},{7,6},{8,9},{9,8},{10,11... | collective-permute-start | bytes 1572872 | tf_op jit(solution)/shard_map/ppermute | solution.py:683
  (144 other events, 1266.6 us)
Sparse Core Ops, SparseCore 0:
  11.0 29.4 all-gather.5
  43.0 27.1 all-gather.7
  72.1 72.2 all-gather.9
  146.1 89.3 all-gather.11
  237.3 53.7 all-gather.13
  331.6 70.7 reduce-scatter.5
  406.2 75.9 reduce-scatter.7
  498.5 55.7 reduce-scatter.9
  572.1 80.9 reduce-scatter.11
  665.3 43.9 reduce-scatter.13

commit v4 on v3

--- a/solution.py
+++ b/solution.py
@@ -1011,7 +1011,8 @@
     own_proj = [own_proj[:, a:b] for a, b in zip(cuts, cuts[1:])]
     proj_parts = [column_blocks(part, depth) for part in own_proj]
     proj_parts = [jnp.concatenate([p[j] for p in proj_parts], axis=1) for j in range(depth)]
-    own_first, *proj_parts = after([own_first, *proj_parts], token_sent[1:])
+    proj_parts = after(proj_parts, token_sent[1:2])
+    (own_first,) = after([own_first], token_sent[1:])
     own_first = own_first.astype(wide)
     proj = total(spread(proj_parts, T))
     result = put_blocks(jnp.concatenate(returned), places, wide)

time: 784 us -> 801 us (1.022); the launches traced: 769 us -> 795 us
  starting transfers between devices: 109 us -> 120 us
    unnamed x258 -> x256, local copies, waits for them, and re-layouts: 38.7 us -> 37.3 us
  transfers between devices with their start and end apart: 71 -> 71, of which waited for: 30 -> 27; matrix products, arithmetic and copies ran while one was open for 20% -> 21% of each run, Pallas kernels for 33% -> 32%
where the time goes in v4:
time: 801 us; the launch traced here: 795 us
  Pallas kernels  259 us (32%)
  waiting for transfers between devices  185 us (23%)
  starting transfers between devices  120 us (15%)
  local copies, waits for them, and re-layouts  81.6 us (10%)
  matrix products  64.7 us (8%)
  other arithmetic  60.5 us (8%)
  between operations  24.4 us (3%)
    ppermute x58, waiting for transfers between devices, swap(): lax.ppermute(value, axis, [(i, i ^ j) for i in range(lax.axis_size(axis))])  180 us
    ppermute x58, starting transfers between devices, swap(): lax.ppermute(value, axis, [(i, i ^ j) for i in range(lax.axis_size(axis))])  106 us
    pallas_call x2, Pallas kernels, cross_bwd(): pl.pallas_call(partial(cross_bwd_body, heads, bounds, kind, step), grid_s...  68.8 us
    pallas_call x1, Pallas kernels, cross_fwd(): pl.pallas_call(partial(cross_fwd_body, heads, bounds), grid_spec=pltpu.Pr...  43.5 us
    pallas_call x1, Pallas kernels, self_bwd(): pl.pallas_call(partial(self_bwd_body, heads, bounds, len(others)), grid_s...  38 us
    unnamed x256, local copies, waits for them, and re-layouts  37.3 us
    pallas_call x1, Pallas kernels, self_fwd(): pl.pallas_call(partial(self_fwd_body, heads, bounds), grid_spec=pltpu.Pre...  34.8 us
    dot_general x7, matrix products, product(): return jnp.dot(left_side, right_side, preferred_element_type=jnp.float32)  34.7 us
  transfers between devices with their start and end apart: 71, of which 27 were waited for; matrix products, arithmetic and copies ran while one was open for 21% of the time, Pallas kernels for 32%

profile of v4, /device:TPU:0, one launch (start us, length us, event | category | flops | bytes accessed | tf_op | source)
XLA Modules:
  0.0 795.1 jit_solution(1223200155558382452)
XLA Ops:
  17.6 6.5 collective-permute-done.4.refs_1_
  24.1 9.5 %collective-permute-done.5.refs_2_ = bf16[128,896]{1,0:T(8,128)(2,1)S(1)} collective-permute-done((bf16[128,896]{1,0:T(8,128)(2,1)S(1)}, bf16[128,896]{1,0:T(8,128)(2,1)S(1)}, u32[]{:S(2)}, u32[]{:S(2)}) %collective-permute-start.5) | collective-permute-done | bytes 229408 | tf_op jit(solution)/shard_map/ppermute | solution.py:683
  70.2 8.4 %collective-permute-done.1.refs_2_ = bf16[1024,512]{1,0:T(8,128)(2,1)S(1)} collective-permute-done((bf16[1024,512]{1,0:T(8,128)(2,1)S(1)}, bf16[1024,512]{1,0:T(8,128)(2,1)S(1)}, u32[]{:S(2)}, u32[]{:S(2)}) %collective-permute-start.1) | collective-permute-done | bytes 1048608 | tf_op jit(solution)/shard_map/ppermute | solution.py:683
  88.7 12.0 %collective-permute-done.2.refs_0_ = bf16[512,512]{1,0:T(8,128)(2,1)S(1)} collective-permute-done((bf16[512,512]{1,0:T(8,128)(2,1)S(1)}, bf16[512,512]{1,0:T(8,128)(2,1)S(1)}, u32[]{:S(2)}, u32[]{:S(2)}) %collective-permute-start.2) | collective-permute-done | bytes 524320 | tf_op jit(solution)/shard_map/ppermute | solution.py:683
  125.9 34.8 %self_fwd.1 = (bf16[1024,256]{1,0:T(8,128)(2,1)}, f32[8,1,512]{2,1,0:T(1,128)}, f32[8,1,512]{2,1,0:T(1,128)}) custom-call(s32[8,8]{1,0:T(8,128)} %concatenate.119.meta_ref, bf16[1024,256]{1,0:T(8,128)(2,1)} %pad_maximum_fusion.5.q_ref, bf16[1024,512]{1,0:T(8,128)(2,1)} %copy-done, bf16[1024,512]{1,0:T(8,128)(2,1)} %collective-permute-done.refs_1_, ...), custom_call_target="tpu_custom_call" | custom-call | tf_op jit(solution)/shard_map/self_fwd/pallas_call | solution.py:334
  175.5 8.4 %collective-permute-done.13.refs_0_ = bf16[2048,512]{1,0:T(8,128)(2,1)S(1)} collective-permute-done((bf16[2048,512]{1,0:T(8,128)(2,1)}, bf16[2048,512]{1,0:T(8,128)(2,1)S(1)}, u32[]{:S(2)}, u32[]{:S(2)}) %collective-permute-start.13) | collective-permute-done | bytes 2097184 | tf_op jit(solution)/shard_map/ppermute | solution.py:683
  216.7 17.7 %collective-permute-done.17 = f32[4]{0:T(128)S(1)} collective-permute-done((f32[4]{0:T(128)S(1)}, f32[4]{0:T(128)S(1)}, u32[]{:S(2)}, u32[]{:S(2)}) %collective-permute-start.17) | collective-permute-done | bytes 48 | tf_op jit(solution)/shard_map/ppermute | solution.py:683
  240.9 43.5 %cross_fwd.1 = (bf16[1024,256]{1,0:T(8,128)(2,1)}, f32[8,1,512]{2,1,0:T(1,128)}) custom-call(s32[5,8]{1,0:T(8,128)} %stack.99.seg_ref, bf16[1024,256]{1,0:T(8,128)(2,1)} %pad_maximum_fusion.7.refs_1_.refs_2_.q_ref.refs_3_, bf16[2048,512]{1,0:T(8,128)(2,1)} %gate.29.refs_0_, bf16[2048,512]{1,0:T(8,128)(2,1)} %get-tuple-element.98.refs_1_, ...), custom_call_target="tpu_custom_call" | custom-call | tf_op jit(solution)/shard_map/cross_fwd/pallas_call | solution.py:169
  296.1 6.3 collective-permute-start.27
  308.0 8.4 %multiply_convert_fusion = (bf16[256,4096]{1,0:T(8,128)(2,1)}, f32[256,4096]{1,0:T(8,128)}) fusion(f32[4096]{0:T(1024)S(1)} %add.655, bf16[256,1024]{1,0:T(8,128)(2,1)S(1)} %fusion.58.refs_0_, bf16[1024,4096]{1,0:T(8,128)(2,1)} %all-gather.12.cloned.1.call-done), kind=kOutput, calls=%fused_computation.14 | convolution fusion | flops 2153775104 | bytes 15220736 | tf_op jit(solution)/shard_map/dot_general | solution.py:31
  316.4 6.6 fusion.132
  336.1 8.1 %fusion.133 = (bf16[4096]{0:T(1024)(128)(2,1)}, bf16[256,4096]{1,0:T(8,128)(2,1)S(1)}) fusion(f32[256,4096]{1,0:T(8,128)} %get-tuple-element.491, bf16[256,1024]{1,0:T(8,128)(2,1)} %gate.36, bf16[1024,4096]{1,0:T(8,128)(2,1)} %all-gather.14.cloned.1.call-done), kind=kOutput, calls=%fused_computation.371 | convolution fusion | flops 2161111040 | bytes 15212544 | tf_op jit(solution)/shard_map/dot_general | solution.py:31
  344.2 8.8 %multiply_reduce_fusion = (bf16[1024]{0:T(1024)(128)(2,1)}, f32[256]{0:T(256)S(1)}, f32[256]{0:T(256)S(1)}, bf16[1024]{0:T(1024)(128)(2,1)}, f32[256,1024]{1,0:T(8,128)S(1)}) fusion(f32[256,1024]{1,0:T(8,128)S(1)} %get-tuple-element.489, f32[256]{0:T(256)S(1)} %add_rsqrt_fusion.1, f32[256]{0:T(256)S(1)} %broadcast_multiply_fusion.10, ...), kind=kOutput, calls=%fused_computation.66 | convolution fusion | flops 2150102528 | bytes 13643776 | tf_op jit(solution)/shard_map/dot_general | solution.py:41
  358.0 7.1 grad_columns.2.refs_5_
  375.9 22.8 %cross_bwd.2 = (bf16[1024,256]{1,0:T(8,128)(2,1)}, bf16[2048,512]{1,0:T(8,128)(2,1)}, bf16[1024,512]{1,0:T(8,128)(2,1)}, bf16[1024,512]{1,0:T(8,128)(2,1)}) custom-call(s32[5,8]{1,0:T(8,128)} %stack.99.seg_ref, bf16[1024,256]{1,0:T(8,128)(2,1)} %pad_maximum_fusion.7.refs_1_.refs_2_.q_ref.refs_3_, bf16[1024,256]{1,0:T(8,128)(2,1)} %pad_maximum_fusion.14.refs_1_.g_ref, ...), custom_call_target="tpu_custom_call" | custom-call | tf_op jit(solution)/shard_map/cross_bwd/pallas_call | solution.py:255
  398.7 8.1 %collective-permute-start.35 = (bf16[1024,512]{1,0:T(8,128)(2,1)}, bf16[1024,512]{1,0:T(8,128)(2,1)}, u32[]{:S(2)}, u32[]{:S(2)}) collective-permute-start(bf16[1024,512]{1,0:T(8,128)(2,1)} %get-tuple-element.115), channel_id=1, source_target_pairs={{0,4},{4,0},{8,12},{12,8},{1,5},{5,1},{9,13},{13,9},{2,6},{6,2},{1... | collective-permute-start | bytes 3145736 | tf_op jit(solution)/shard_map/ppermute | solution.py:683
  406.8 17.5 %collective-permute-start.36 = (bf16[1024,512]{1,0:T(8,128)(2,1)}, bf16[1024,512]{1,0:T(8,128)(2,1)}, u32[]{:S(2)}, u32[]{:S(2)}) collective-permute-start(bf16[1024,512]{1,0:T(8,128)(2,1)} %get-tuple-element.116), channel_id=1, source_target_pairs={{0,8},{4,12},{8,0},{12,4},{1,9},{5,13},{9,1},{13,5},{2,10},{6,14},... | collective-permute-start | bytes 3145736 | tf_op jit(solution)/shard_map/ppermute | solution.py:683
  428.6 46.0 %cross_bwd.3 = (bf16[1024,256]{1,0:T(8,128)(2,1)}, bf16[2048,512]{1,0:T(8,128)(2,1)}, bf16[2048,512]{1,0:T(8,128)(2,1)}) custom-call(s32[5,8]{1,0:T(8,128)} %stack.99.seg_ref, bf16[1024,256]{1,0:T(8,128)(2,1)} %pad_maximum_fusion.7.refs_1_.refs_2_.q_ref.refs_3_, bf16[1024,256]{1,0:T(8,128)(2,1)} %pad_maximum_fusion.14.refs_1_.g_ref, ...), custom_call_target="tpu_custom_call" | custom-call | tf_op jit(solution)/shard_map/cross_bwd/pallas_call | solution.py:255
  535.1 38.0 %self_bwd.1 = (bf16[1024,256]{1,0:T(8,128)(2,1)}, bf16[1024,512]{1,0:T(8,128)(2,1)}, bf16[1024,512]{1,0:T(8,128)(2,1)}, bf16[1024,512]{1,0:T(8,128)(2,1)}, bf16[...) custom-call(s32[8,8]{1,0:T(8,128)} %concatenate.119.meta_ref, bf16[1024,256]{1,0:T(8,128)(2,1)} %pad_maximum_fusion.5.q_ref, ...), custom_call_target="tpu_custom_call" | custom-call | tf_op jit(solution)/shard_map/self_bwd/pallas_call | solution.py:411
  575.9 7.1 grad_columns.3
  583.1 6.8 sum_terms.2
  589.9 8.1 %plane_shares.2 = (bf16[2048,256]{1,0:T(8,128)(2,1)}, bf16[2048,256]{1,0:T(8,128)(2,1)}, bf16[2048,256]{1,0:T(8,128)(2,1)}, bf16[2048,256]{1,0:T(8,128)(2,1)}) custom-call(s32[1]{0:T(128)} %bitcast.63.plane_ref, bf16[2048,512]{1,0:T(8,128)(2,1)} %get-tuple-element.126.refs_0_, bf16[1024,512]{1,0:T(8,128)(2,1)} %gate.27.refs_1_.refs_2_.refs_3_.refs_4_, ...), custom_call_target="tpu_custom_call" | custom-call | flops 20000000000 | bytes 33554432 | tf_op jit(solution)/shard_map/plane_shares/pallas_call | solution.py:596
  602.4 6.3 weight_grad.2.refs_1_.refs_3_
  629.0 11.9 %collective-permute-done.49.refs_4_.refs_1_ = bf16[2048,256]{1,0:T(8,128)(2,1)S(1)} collective-permute-done((bf16[2048,256]{1,0:T(8,128)(2,1)}, bf16[2048,256]{1,0:T(8,128)(2,1)S(1)}, u32[]{:S(2)}, u32[]{:S(2)}) %collective-permute-start.49) | collective-permute-done | bytes 1048608 | tf_op jit(solution)/shard_map/ppermute | solution.py:683
  640.9 10.4 %collective-permute-done.47.refs_1_ = bf16[1024,512]{1,0:T(8,128)(2,1)} collective-permute-done((bf16[1024,512]{1,0:T(8,128)(2,1)}, bf16[1024,512]{1,0:T(8,128)(2,1)}, u32[]{:S(2)}, u32[]{:S(2)}) %collective-permute-start.47) | collective-permute-done | bytes 1048608 | tf_op jit(solution)/shard_map/ppermute | solution.py:683
  659.8 7.0 weight_grad.3.refs_0_
  666.8 12.5 %collective-permute-done.52 = bf16[256,1024]{1,0:T(8,128)(2,1)S(1)} collective-permute-done((bf16[256,1024]{1,0:T(8,128)(2,1)}, bf16[256,1024]{1,0:T(8,128)(2,1)S(1)}, u32[]{:S(2)}, u32[]{:S(2)}) %collective-permute-start.52) | collective-permute-done | bytes 524320 | tf_op jit(solution)/shard_map/ppermute | solution.py:683
  679.4 9.5 %collective-permute-done.51 = bf16[256,1024]{1,0:T(8,128)(2,1)S(1)} collective-permute-done((bf16[256,1024]{1,0:T(8,128)(2,1)}, bf16[256,1024]{1,0:T(8,128)(2,1)S(1)}, u32[]{:S(2)}, u32[]{:S(2)}) %collective-permute-start.51) | collective-permute-done | bytes 524320 | tf_op jit(solution)/shard_map/ppermute | solution.py:683
  690.3 6.6 put_blocks.1.refs_1_.refs_4_
  714.7 25.1 %collective-permute-done.55.refs_1_.refs_4_ = bf16[1024,256]{1,0:T(8,128)(2,1)S(1)} collective-permute-done((bf16[1024,256]{1,0:T(8,128)(2,1)}, bf16[1024,256]{1,0:T(8,128)(2,1)S(1)}, u32[]{:S(2)}, u32[]{:S(2)}) %collective-permute-start.55) | collective-permute-done | bytes 524320 | tf_op jit(solution)/shard_map/ppermute | solution.py:683
  749.8 12.1 %collective-permute-done.56.refs_2_ = bf16[1024,256]{1,0:T(8,128)(2,1)S(1)} collective-permute-done((bf16[1024,256]{1,0:T(8,128)(2,1)}, bf16[1024,256]{1,0:T(8,128)(2,1)S(1)}, u32[]{:S(2)}, u32[]{:S(2)}) %collective-permute-start.56) | collective-permute-done | bytes 524320 | tf_op jit(solution)/shard_map/ppermute | solution.py:683
  763.1 7.6 collective-permute-done.59
  (638 shorter events, 321.0 us)
Async XLA Ops:
  7.2 38.8 %all-gather.6.cloned.1.call-start = ((), (), s32[]{:S(2)}) async-start(), calls=%async_computation.5 | async-start | bytes 2064384 | tf_op jit(solution)/shard_map/all_gather | solution.py:757
  10.9 59.3 %all-gather.8.cloned.1.call-start = ((), (), s32[]{:S(2)}) async-start(), calls=%async_computation.6 | async-start | bytes 1179648 | tf_op jit(solution)/shard_map/all_gather | solution.py:770
  37.6 153.2 %all-gather.10.cloned.1.call-start = ((), (), s32[]{:S(2)}) async-start(), calls=%async_computation.7 | async-start | bytes 8257536 | tf_op jit(solution)/shard_map/all_gather | solution.py:832
  46.0 262.0 %all-gather.12.cloned.1.call-start = ((), (), s32[]{:S(2)}) async-start(), calls=%async_computation.8 | async-start | bytes 9437184 | tf_op jit(solution)/shard_map/all_gather | solution.py:836
  56.6 46.2 %collective-permute-start.23 = (bf16[128,2048]{1,0:T(8,128)(2,1)}, bf16[128,2048]{1,0:T(8,128)(2,1)}, u32[]{:S(2)}, u32[]{:S(2)}) collective-permute-start(bf16[128,2048]{1,0:T(8,128)(2,1)} %gate.33.refs_0_), channel_id=1, source_target_pairs={{0,1},{1,0},{2,3},{3,2},{4,5},{5,4},{6,7},{7,6},{8,9},{9,8},{10,11... | collective-permute-start | bytes 1572872 | tf_op jit(solution)/shard_map/ppermute | solution.py:683
  60.1 42.7 %collective-permute-start.24 = (bf16[128,2048]{1,0:T(8,128)(2,1)}, bf16[128,2048]{1,0:T(8,128)(2,1)}, u32[]{:S(2)}, u32[]{:S(2)}) collective-permute-start(bf16[128,2048]{1,0:T(8,128)(2,1)} %gate.33.refs_0_), channel_id=1, source_target_pairs={{0,2},{1,3},{2,0},{3,1},{4,6},{5,7},{6,4},{7,5},{8,10},{9,11},{10,... | collective-permute-start | bytes 1572872 | tf_op jit(solution)/shard_map/ppermute | solution.py:683
  61.1 41.7 %collective-permute-start.25 = (bf16[128,2048]{1,0:T(8,128)(2,1)}, bf16[128,2048]{1,0:T(8,128)(2,1)}, u32[]{:S(2)}, u32[]{:S(2)}) collective-permute-start(bf16[128,2048]{1,0:T(8,128)(2,1)} %gate.33.refs_0_), channel_id=1, source_target_pairs={{0,3},{1,2},{2,1},{3,0},{4,7},{5,6},{6,5},{7,4},{8,11},{9,10},{10,... | collective-permute-start | bytes 1572872 | tf_op jit(solution)/shard_map/ppermute | solution.py:683
  106.3 210.1 %all-gather.14.cloned.1.call-start = ((), (), s32[]{:S(2)}) async-start(), calls=%async_computation.9 | async-start | bytes 9437184 | tf_op jit(solution)/shard_map/all_gather | solution.py:838
  107.5 367.3 %reduce-scatter.6.cloned.1.call-start = ((), (), s32[]{:S(2)}) async-start(), calls=%async_computation.10 | async-start | bytes 9437184 | tf_op jit(solution)/shard_map/reduce_scatter | solution.py:859
  111.5 72.4 %collective-permute-start.13 = (bf16[2048,512]{1,0:T(8,128)(2,1)}, bf16[2048,512]{1,0:T(8,128)(2,1)S(1)}, u32[]{:S(2)}, u32[]{:S(2)}) collective-permute-start(bf16[2048,512]{1,0:T(8,128)(2,1)} %gate.29.refs_0_), channel_id=1, source_target_pairs={{0,4},{4,0},{8,12},{12,8},{1,5},{5,1},{9,13},{13,9},{2,6},{6,2},{1... | collective-permute-start | bytes 6291464 | tf_op jit(solution)/shard_map/ppermute | solution.py:683
  112.1 71.9 %collective-permute-start.14 = (bf16[2048,512]{1,0:T(8,128)(2,1)}, bf16[2048,512]{1,0:T(8,128)(2,1)}, u32[]{:S(2)}, u32[]{:S(2)}) collective-permute-start(bf16[2048,512]{1,0:T(8,128)(2,1)} %gate.29.refs_0_), channel_id=1, source_target_pairs={{0,8},{4,12},{8,0},{12,4},{1,9},{5,13},{9,1},{13,5},{2,10},{6,14},... | collective-permute-start | bytes 6291464 | tf_op jit(solution)/shard_map/ppermute | solution.py:683
  187.6 52.0 %collective-permute-start.15 = (bf16[1024,512]{1,0:T(8,128)(2,1)}, bf16[1024,512]{1,0:T(8,128)(2,1)S(1)}, u32[]{:S(2)}, u32[]{:S(2)}) collective-permute-start(bf16[1024,512]{1,0:T(8,128)(2,1)} %slice.524), channel_id=1, source_target_pairs={{0,4},{4,0},{8,12},{12,8},{1,5},{5,1},{9,13},{13,9},{2,6},{6,2},{1... | collective-permute-start | bytes 3145736 | tf_op jit(solution)/shard_map/ppermute | solution.py:683
  189.0 50.6 %collective-permute-start.16 = (bf16[1024,512]{1,0:T(8,128)(2,1)}, bf16[1024,512]{1,0:T(8,128)(2,1)S(1)}, u32[]{:S(2)}, u32[]{:S(2)}) collective-permute-start(bf16[1024,512]{1,0:T(8,128)(2,1)} %slice.525), channel_id=1, source_target_pairs={{0,8},{4,12},{8,0},{12,4},{1,9},{5,13},{9,1},{13,5},{2,10},{6,14},... | collective-permute-start | bytes 3145736 | tf_op jit(solution)/shard_map/ppermute | solution.py:683
  335.5 171.9 %reduce-scatter.8.cloned.1.call-start = ((), (), s32[]{:S(2)}) async-start(), calls=%async_computation.11 | async-start | bytes 9437184 | tf_op jit(solution)/shard_map/reduce_scatter | solution.py:859
  365.2 243.6 %reduce-scatter.10.cloned.1.call-start = ((), (), s32[]{:S(2)}) async-start(), calls=%async_computation.12 | async-start | bytes 2621440 | tf_op jit(solution)/shard_map/reduce_scatter | solution.py:963
  398.7 76.1 %collective-permute-start.35 = (bf16[1024,512]{1,0:T(8,128)(2,1)}, bf16[1024,512]{1,0:T(8,128)(2,1)}, u32[]{:S(2)}, u32[]{:S(2)}) collective-permute-start(bf16[1024,512]{1,0:T(8,128)(2,1)} %get-tuple-element.115), channel_id=1, source_target_pairs={{0,4},{4,0},{8,12},{12,8},{1,5},{5,1},{9,13},{13,9},{2,6},{6,2},{1... | collective-permute-start | bytes 3145736 | tf_op jit(solution)/shard_map/ppermute | solution.py:683
  406.8 68.0 %collective-permute-start.36 = (bf16[1024,512]{1,0:T(8,128)(2,1)}, bf16[1024,512]{1,0:T(8,128)(2,1)}, u32[]{:S(2)}, u32[]{:S(2)}) collective-permute-start(bf16[1024,512]{1,0:T(8,128)(2,1)} %get-tuple-element.116), channel_id=1, source_target_pairs={{0,8},{4,12},{8,0},{12,4},{1,9},{5,13},{9,1},{13,5},{2,10},{6,14},... | collective-permute-start | bytes 3145736 | tf_op jit(solution)/shard_map/ppermute | solution.py:683
  424.2 50.4 %collective-permute-start.32 = (bf16[256,1024]{1,0:T(8,128)(2,1)}, bf16[256,1024]{1,0:T(8,128)(2,1)S(1)}, u32[]{:S(2)}, u32[]{:S(2)}) collective-permute-start(bf16[256,1024]{1,0:T(8,128)(2,1)} %gate.37.refs_0_), channel_id=1, source_target_pairs={{0,1},{1,0},{2,3},{3,2},{4,5},{5,4},{6,7},{7,6},{8,9},{9,8},{10,11... | collective-permute-start | bytes 1572872 | tf_op jit(solution)/shard_map/ppermute | solution.py:683
  424.2 50.4 %collective-permute-start.33 = (bf16[256,1024]{1,0:T(8,128)(2,1)}, bf16[256,1024]{1,0:T(8,128)(2,1)S(1)}, u32[]{:S(2)}, u32[]{:S(2)}) collective-permute-start(bf16[256,1024]{1,0:T(8,128)(2,1)} %gate.37.refs_0_), channel_id=1, source_target_pairs={{0,2},{1,3},{2,0},{3,1},{4,6},{5,7},{6,4},{7,5},{8,10},{9,11},{10,... | collective-permute-start | bytes 1572872 | tf_op jit(solution)/shard_map/ppermute | solution.py:683
  425.5 49.2 %collective-permute-start.34 = (bf16[256,1024]{1,0:T(8,128)(2,1)}, bf16[256,1024]{1,0:T(8,128)(2,1)S(1)}, u32[]{:S(2)}, u32[]{:S(2)}) collective-permute-start(bf16[256,1024]{1,0:T(8,128)(2,1)} %gate.37.refs_0_), channel_id=1, source_target_pairs={{0,3},{1,2},{2,1},{3,0},{4,7},{5,6},{6,5},{7,4},{8,11},{9,10},{10,... | collective-permute-start | bytes 1572872 | tf_op jit(solution)/shard_map/ppermute | solution.py:683
  511.3 185.7 %reduce-scatter.12.cloned.1.call-start = ((), (), s32[]{:S(2)}) async-start(), calls=%async_computation.13 | async-start | bytes 8257536 | tf_op jit(solution)/shard_map/reduce_scatter | solution.py:859
  530.6 52.4 %collective-permute-start.44 = (bf16[2048,512]{1,0:T(8,128)(2,1)}, bf16[2048,512]{1,0:T(8,128)(2,1)}, u32[]{:S(2)}, u32[]{:S(2)}) collective-permute-start(bf16[2048,512]{1,0:T(8,128)(2,1)} %add_half.4.refs_3_.refs_5_), channel_id=1, source_target_pairs={{0,4},{4,0},{8,12},{12,8},{1,5},{5,1},{9,13},{13,9},{2,6},{6,2},{1... | collective-permute-start | bytes 6291464 | tf_op jit(solution)/shard_map/ppermute | solution.py:683
  530.7 52.4 %collective-permute-start.45 = (bf16[2048,512]{1,0:T(8,128)(2,1)S(1)}, bf16[2048,512]{1,0:T(8,128)(2,1)}, u32[]{:S(2)}, u32[]{:S(2)}) collective-permute-start(bf16[2048,512]{1,0:T(8,128)(2,1)S(1)} %copy-done.3), channel_id=1, source_target_pairs={{0,8},{4,12},{8,0},{12,4},{1,9},{5,13},{9,1},{13,5},{2,10},{6,14},... | collective-permute-start | bytes 6291464 | tf_op jit(solution)/shard_map/ppermute | solution.py:683
  574.4 37.2 %collective-permute-start.46 = (bf16[512,512]{1,0:T(8,128)(2,1)}, bf16[512,512]{1,0:T(8,128)(2,1)}, u32[]{:S(2)}, u32[]{:S(2)}) collective-permute-start(bf16[512,512]{1,0:T(8,128)(2,1)} %get-tuple-element.132), channel_id=1, source_target_pairs={{0,4},{4,0},{8,12},{12,8},{1,5},{5,1},{9,13},{13,9},{2,6},{6,2},{1... | collective-permute-start | bytes 1572872 | tf_op jit(solution)/shard_map/ppermute | solution.py:683
  583.0 195.1 %reduce-scatter.14.cloned.1.call-start = ((), (), s32[]{:S(2)}) async-start(), calls=%async_computation.14 | async-start | bytes 3244032 | tf_op jit(solution)/shard_map/reduce_scatter | solution.py:859
  598.0 42.9 %collective-permute-start.49 = (bf16[2048,256]{1,0:T(8,128)(2,1)}, bf16[2048,256]{1,0:T(8,128)(2,1)S(1)}, u32[]{:S(2)}, u32[]{:S(2)}) collective-permute-start(bf16[2048,256]{1,0:T(8,128)(2,1)} %get-tuple-element.128.refs_2_), channel_id=1, source_target_pairs={{0,1},{1,0},{2,3},{3,2},{4,5},{5,4},{6,7},{7,6},{8,9},{9,8},{10,11... | collective-permute-start | bytes 3145736 | tf_op jit(solution)/shard_map/ppermute | solution.py:683
  598.0 99.0 %collective-permute-start.53 = (bf16[2048,256]{1,0:T(8,128)(2,1)}, bf16[2048,256]{1,0:T(8,128)(2,1)}, u32[]{:S(2)}, u32[]{:S(2)}) collective-permute-start(bf16[2048,256]{1,0:T(8,128)(2,1)} %get-tuple-element.129.refs_3_), channel_id=1, source_target_pairs={{0,2},{1,3},{2,0},{3,1},{4,6},{5,7},{6,4},{7,5},{8,10},{9,11},{10,... | collective-permute-start | bytes 3145736 | tf_op jit(solution)/shard_map/ppermute | solution.py:683
  600.7 96.3 %collective-permute-start.54 = (bf16[2048,256]{1,0:T(8,128)(2,1)}, bf16[2048,256]{1,0:T(8,128)(2,1)}, u32[]{:S(2)}, u32[]{:S(2)}) collective-permute-start(bf16[2048,256]{1,0:T(8,128)(2,1)} %get-tuple-element.130.refs_4_), channel_id=1, source_target_pairs={{0,3},{1,2},{2,1},{3,0},{4,7},{5,6},{6,5},{7,4},{8,11},{9,10},{10,... | collective-permute-start | bytes 3145736 | tf_op jit(solution)/shard_map/ppermute | solution.py:683
  610.7 40.6 %collective-permute-start.47 = (bf16[1024,512]{1,0:T(8,128)(2,1)}, bf16[1024,512]{1,0:T(8,128)(2,1)}, u32[]{:S(2)}, u32[]{:S(2)}) collective-permute-start(bf16[1024,512]{1,0:T(8,128)(2,1)} %add_half.6.refs_4_.refs_1_), channel_id=1, source_target_pairs={{0,4},{4,0},{8,12},{12,8},{1,5},{5,1},{9,13},{13,9},{2,6},{6,2},{1... | collective-permute-start | bytes 3145736 | tf_op jit(solution)/shard_map/ppermute | solution.py:683
  613.5 37.8 %collective-permute-start.48 = (bf16[1024,512]{1,0:T(8,128)(2,1)}, bf16[1024,512]{1,0:T(8,128)(2,1)}, u32[]{:S(2)}, u32[]{:S(2)}) collective-permute-start(bf16[1024,512]{1,0:T(8,128)(2,1)} %add_half.7.refs_5_.refs_2_), channel_id=1, source_target_pairs={{0,8},{4,12},{8,0},{12,4},{1,9},{5,13},{9,1},{13,5},{2,10},{6,14},... | collective-permute-start | bytes 3145736 | tf_op jit(solution)/shard_map/ppermute | solution.py:683
  702.7 47.1 %collective-permute-start.57 = (bf16[1024,256]{1,0:T(8,128)(2,1)}, bf16[1024,256]{1,0:T(8,128)(2,1)S(1)}, u32[]{:S(2)}, u32[]{:S(2)}) collective-permute-start(bf16[1024,256]{1,0:T(8,128)(2,1)} %get-tuple-element.149), channel_id=1, source_target_pairs={{0,3},{1,2},{2,1},{3,0},{4,7},{5,6},{6,5},{7,4},{8,11},{9,10},{10,... | collective-permute-start | bytes 1572872 | tf_op jit(solution)/shard_map/ppermute | solution.py:683
  706.1 55.8 %collective-permute-start.56 = (bf16[1024,256]{1,0:T(8,128)(2,1)}, bf16[1024,256]{1,0:T(8,128)(2,1)S(1)}, u32[]{:S(2)}, u32[]{:S(2)}) collective-permute-start(bf16[1024,256]{1,0:T(8,128)(2,1)} %get-tuple-element.148), channel_id=1, source_target_pairs={{0,2},{1,3},{2,0},{3,1},{4,6},{5,7},{6,4},{7,5},{8,10},{9,11},{10,... | collective-permute-start | bytes 1572872 | tf_op jit(solution)/shard_map/ppermute | solution.py:683
  (143 other events, 1461.9 us)
Sparse Core Ops, SparseCore 0:
  11.0 29.4 all-gather.5
  43.0 27.1 all-gather.7
  72.1 72.4 all-gather.9
  146.3 89.1 all-gather.11
  237.2 53.8 all-gather.13
  335.7 69.1 reduce-scatter.5
  408.7 80.2 reduce-scatter.7
  511.4 43.7 reduce-scatter.9
  583.1 104.3 reduce-scatter.11
  697.1 44.8 reduce-scatter.13
